TPU v7x, 32 devices: a whole 2x2x4 slice. The times are simulated.
32 devices in a mesh: owner: 16 (over z, y, x), pair: 2 (over core).
Axes of the slice: x: 2, y: 2, z: 4, core: 2. Of those that a mesh axis runs over, the one named last changes fastest.
Arguments:
- incident: float32 [32, 2, 32, 512], P('owner', None, None, 'pair'), may hold values from -6 to 6
- tmat: float32 [32, 2, 512, 512], P('owner', None, 'pair'), may hold values from -0.1875 to 0.1875
- blocks: float32 [336, 2, 512, 512], P('owner', None, None, 'pair'), may hold values from -0.09375 to 0.09375
- block_rows: int32 [336], P('owner'), may hold values from 0 to 1
- partners: int32 [336], replicated, may hold values from 0 to 31, as said below
- live: int32 [16], P('owner'), may hold values from 1 to 21, as said below
- owner_of: int32 [32], replicated, may hold values from 0 to 31, as said below
Outputs:
- scattered: float32 [32, 2, 32, 512], P('owner', None, None, 'pair')
- exciting: float32 [32, 2, 32, 512], P('owner', None, None, 'pair')
Inputs may be any that keep to these rules, and one draw needn't show every extreme that they name: A permutation: particle p's coefficients and T-matrix stand in row owner_of[p]. `partners`: the 21 slots of one owner name distinct particles whose rows lie with owners either less than 7 positions away on either side around the cycle of owners or exactly 8 positions away, never the owner itself, at most 2 with any one other owner; for every owner some other owner holds exactly 2 of them. Slots n with n mod 21 below live[n // 21] are live; some owner has all 21 slots live.
All inputs are finite; a program needn't handle non-finite values.
Results may differ from a plain program's by a relative error of at most 0.0003.
Values sent between devices are 32-bit elements; how exact they have to be, the bound alone decides.
No kernel may reach another device: no remote copies, remote signals or barrier semaphores. Data moves between devices by JAX's collectives and lax.ppermute only.
A program may use at most 128 MiB of HBM per device.

v0:
```python
import functools

import jax
import jax.numpy as jnp
from jax import lax
from jax.experimental import pallas as pl
from jax.experimental.pallas import tpu as pltpu
from jax.sharding import PartitionSpec as P

ITERS = 2
COLUMNS = 4
BUFFERS = 4
F32 = jnp.float32
BF16 = jnp.bfloat16
MIB = 1 << 20
STREAM_LIMIT = 48 * MIB
VMEM = pl.BlockSpec(memory_space=pltpu.VMEM)
SMEM = pl.BlockSpec(memory_space=pltpu.SMEM)
ANY = pl.BlockSpec(memory_space=pl.ANY)
HBM = pl.BlockSpec(memory_space=pltpu.MemorySpace.HBM)


def split_value(value):
    high = value.astype(BF16)
    low = (value - high.astype(F32)).astype(BF16)
    return high, low


def stacked_parts(real, imag):
    real_high, real_low = split_value(real)
    imag_high, imag_low = split_value(imag)
    with_real = jnp.concatenate((real_high, imag_high, real_low, imag_low), axis=0)
    with_imag = jnp.concatenate((-imag_high, real_high, -imag_low, real_low), axis=0)
    return with_real, with_imag


def dot_nt(left, right):
    return lax.dot_general(left, right, (((1,), (1,)), ((), ())), preferred_element_type=F32)


def dot_nn(left, right):
    return jnp.dot(left, right, preferred_element_type=F32)


def params(*byte_counts):
    return pltpu.CompilerParams(vmem_limit_bytes=sum(byte_counts) + 6 * MIB)


def size_of(*arrays):
    return sum(value.size * value.dtype.itemsize for value in arrays)


def place_of(column, particle, layer, particles, layers):
    return (column * particles + particle) * layers + layer


def tmat_kernel(mine_ref, theirs_ref, tmat_ref, side_ref, exciting_ref, scattered_ref):
    particles, _, directions, width = mine_ref.shape
    half = width // 2
    start = pl.multiple_of(side_ref[0] * half, half)
    for row in range(particles):
        real = mine_ref[row, 0] + theirs_ref[row, 0]
        imag = mine_ref[row, 1] + theirs_ref[row, 1]
        with_real, with_imag = stacked_parts(real, imag)
        real_high, real_low = split_value(tmat_ref[row, 0])
        imag_high, imag_low = split_value(tmat_ref[row, 1])
        left = jnp.concatenate((real_high, imag_high, real_low, imag_low), axis=1)
        right = jnp.concatenate((with_real, with_imag, with_real, with_imag), axis=1)
        total = dot_nt(left, right)
        out = (total[:, : 2 * directions] + total[:, 2 * directions :]).T
        scattered_ref[row, 0] = out[:directions]
        scattered_ref[row, 1] = out[directions:]
        for part in range(2):
            window = (row, part, slice(None), pl.ds(start, half))
            exciting_ref[row, part] = mine_ref[window] + theirs_ref[window]


def apply_tmat(mine, theirs, tmat, side):
    particles, _, directions, width = mine.shape
    half_shape = jax.ShapeDtypeStruct((particles, 2, directions, width // 2), F32)
    return pl.pallas_call(
        tmat_kernel,
        out_shape=(half_shape, half_shape),
        in_specs=[VMEM, VMEM, VMEM, SMEM],
        out_specs=(VMEM, VMEM),
        compiler_params=params(2 * size_of(mine, theirs, tmat)),
        name="tmat_apply",
    )(mine, theirs, tmat, side)


def chosen_slots(group_ref, alive, groups, list_ref):
    def step(slot, found):
        list_ref[found] = slot
        group = group_ref[slot]
        wanted = jnp.logical_and(group >= groups[0], group <= groups[1])
        return found + jnp.where(wanted, 1, 0)

    return lax.fori_loop(0, alive, step, 0)


def backward_kernel(first, groups, base, rows_ref, live_ref, place_ref, group_ref, side_ref, *refs):
    own_ref, other_ref, blocks_ref = refs[:3]
    refs = refs[3:]
    if first:
        out_ref, parts_ref, list_ref, left_ref, buf_ref, sems, made_ref, made_sems = refs[-8:]
    else:
        out_ref, list_ref, left_ref, buf_ref, sems = refs
    directions, half = own_ref.shape[2], own_ref.shape[3]
    width = 2 * half
    wanted = chosen_slots(group_ref, live_ref[0], groups, list_ref)

    def fetch(turn, place):
        return pltpu.make_async_copy(
            blocks_ref.at[list_ref[turn]], buf_ref.at[place], sems.at[place]
        )

    def keep(turn, place):
        return pltpu.make_async_copy(
            made_ref.at[place], parts_ref.at[list_ref[turn]], made_sems.at[place]
        )

    for early in range(BUFFERS):

        @pl.when(early < wanted)
        def _():
            fetch(early, early).start()

    for field_ref, side in ((own_ref, side_ref[0]), (other_ref, 1 - side_ref[0])):
        for row in range(field_ref.shape[0]):
            with_real, with_imag = stacked_parts(field_ref[row, 0], field_ref[row, 1])
            for part, value in enumerate((with_real, with_imag)):
                start = pl.multiple_of(part * width + side * half, half)
                left_ref[row, :, pl.ds(start, half)] = value
    out_ref[...] = jnp.zeros_like(out_ref)

    def body(turn, carry):
        here = lax.rem(turn, BUFFERS)
        fetch(turn, here).wait()
        slot = list_ref[turn]
        holder = rows_ref[slot]
        if first:
            spot = lax.rem(turn, 2)

            @pl.when(turn >= 2)
            def _():
                keep(turn - 2, spot).wait()

            high, low = split_value(buf_ref[here].reshape(2 * width, half))
            made_ref[spot, 0] = high.reshape(2, width, half)
            made_ref[spot, 1] = low.reshape(2, width, half)
            keep(turn, spot).start()
        else:
            high = buf_ref[here, 0].reshape(2 * width, half)
            low = buf_ref[here, 1].reshape(2 * width, half)
        total = dot_nn(left_ref[holder], high)
        rest = dot_nn(left_ref[holder, : 2 * directions], low)
        out = total[: 2 * directions] + total[2 * directions :] + rest
        place = place_ref[slot] - base
        out_ref[place, 0] = out[:directions]
        out_ref[place, 1] = out[directions:]

        @pl.when(turn + BUFFERS < wanted)
        def _():
            fetch(turn + BUFFERS, here).start()

        return carry

    lax.fori_loop(0, wanted, body, 0)
    if first:

        @pl.when(wanted >= 2)
        def _():
            keep(wanted - 2, lax.rem(wanted, 2)).wait()

        @pl.when(wanted >= 1)
        def _():
            keep(wanted - 1, lax.rem(wanted - 1, 2)).wait()


def backward(first, groups, base, count, index, side, own_half, other_half, blocks, parts):
    particles, _, directions, half = own_half.shape
    width = 2 * half
    slots = blocks.shape[0]
    out_shape = [jax.ShapeDtypeStruct((count, 2, directions, half), F32)]
    out_specs = [VMEM]
    source = blocks if first else parts
    scratch = [
        pltpu.SMEM((slots + 1,), jnp.int32),
        pltpu.VMEM((particles, 4 * directions, 2 * width), BF16),
        pltpu.VMEM((BUFFERS,) + source.shape[1:], source.dtype),
        pltpu.SemaphoreType.DMA((BUFFERS,)),
    ]
    operands = [*index, side, own_half, other_half, source]
    in_specs = [SMEM] * 5 + [VMEM, VMEM, HBM]
    aliases = {}
    if first:
        out_shape.append(jax.ShapeDtypeStruct((slots, 2, 2, width, half), BF16))
        out_specs.append(HBM)
        scratch.append(pltpu.VMEM((2, 2, 2, width, half), BF16))
        scratch.append(pltpu.SemaphoreType.DMA((2,)))
        if parts is not None:
            aliases = {len(operands): 1}
            operands.append(parts)
            in_specs.append(HBM)
    return pl.pallas_call(
        functools.partial(backward_kernel, first, groups, base),
        out_shape=out_shape,
        in_specs=in_specs,
        out_specs=out_specs,
        scratch_shapes=scratch,
        input_output_aliases=aliases,
        compiler_params=pltpu.CompilerParams(vmem_limit_bytes=STREAM_LIMIT),
        cost_estimate=pl.CostEstimate(
            flops=slots * 24 * directions * width * half,
            bytes_accessed=size_of(blocks) // 2,
            transcendentals=0,
        ),
        name="backward_group" + str(groups[0]),
    )(*operands)


def forward_kernel(groups, copies, count, rows_ref, live_ref, place_ref, group_ref, *refs):
    field_refs = refs[:count]
    parts_ref = refs[count]
    out_ref, list_ref, every_ref, acc_ref, buf_ref, sems = refs[-6:]
    directions = out_ref.shape[2]
    wanted = chosen_slots(group_ref, live_ref[0], groups, list_ref)

    def fetch(turn, place):
        return pltpu.make_async_copy(
            parts_ref.at[list_ref[turn]], buf_ref.at[place], sems.at[place]
        )

    for early in range(BUFFERS):

        @pl.when(early < wanted)
        def _():
            fetch(early, early).start()

    acc_ref[...] = jnp.zeros_like(acc_ref)
    for number, row, place in copies:
        every_ref[place] = field_refs[number][row]

    def body(turn, carry):
        here = lax.rem(turn, BUFFERS)
        slot = list_ref[turn]
        holder = rows_ref[slot]
        place = place_ref[slot]
        with_real, with_imag = stacked_parts(every_ref[place, 0], every_ref[place, 1])
        fetch(turn, here).wait()
        total = dot_nt(with_real, buf_ref[here, 0, 0]) + dot_nt(with_imag, buf_ref[here, 0, 1])
        rest = dot_nt(with_real[: 2 * directions], buf_ref[here, 1, 0])
        rest += dot_nt(with_imag[: 2 * directions], buf_ref[here, 1, 1])
        acc_ref[holder] += total[: 2 * directions] + total[2 * directions :] + rest

        @pl.when(turn + BUFFERS < wanted)
        def _():
            fetch(turn + BUFFERS, here).start()

        return carry

    lax.fori_loop(0, wanted, body, 0)
    for row in range(acc_ref.shape[0]):
        out_ref[row, 0] = acc_ref[row, :directions]
        out_ref[row, 1] = acc_ref[row, directions:]


def forward(groups, index, fields, copies, parts, particles, total_rows, after):
    slots, _, _, width, half = parts.shape
    directions = fields[0].shape[2]
    out_shape = jax.ShapeDtypeStruct((particles, 2, directions, width), F32)
    return pl.pallas_call(
        functools.partial(forward_kernel, groups, copies, len(fields)),
        out_shape=out_shape,
        in_specs=[SMEM] * 4 + [VMEM] * len(fields) + [HBM] + [ANY] * len(after),
        out_specs=VMEM,
        scratch_shapes=[
            pltpu.SMEM((slots + 1,), jnp.int32),
            pltpu.VMEM((total_rows, 2, directions, half), F32),
            pltpu.VMEM((particles, 2 * directions, width), F32),
            pltpu.VMEM((BUFFERS,) + parts.shape[1:], BF16),
            pltpu.SemaphoreType.DMA((BUFFERS,)),
        ],
        compiler_params=pltpu.CompilerParams(vmem_limit_bytes=STREAM_LIMIT),
        cost_estimate=pl.CostEstimate(
            flops=slots * 16 * directions * width * half,
            bytes_accessed=size_of(parts) // 3,
            transcendentals=0,
        ),
        name="forward_group" + str(groups[0]),
    )(*index, *fields, parts, *after)


def pack_kernel(plans, count, *refs):
    in_refs, out_refs = refs[:count], refs[-len(plans) :]
    for out_ref, plan in zip(out_refs, plans):
        for row, terms in enumerate(plan):
            value = in_refs[terms[0][0]][terms[0][1]]
            for number, source in terms[1:]:
                value = value + in_refs[number][source]
            out_ref[row] = value


def pack(name, inputs, plans, after=()):
    shapes = [jax.ShapeDtypeStruct((len(plan),) + inputs[0].shape[1:], F32) for plan in plans]
    return pl.pallas_call(
        functools.partial(pack_kernel, plans, len(inputs)),
        out_shape=shapes,
        in_specs=[VMEM] * len(inputs) + [ANY] * len(after),
        out_specs=[VMEM] * len(plans),
        compiler_params=params(size_of(*inputs), size_of(*shapes)),
        name=name,
    )(*inputs, *after)


def total_kernel(counts, side_ref, incident_ref, *refs):
    nears, halves, out_ref = refs[: counts[0]], refs[counts[0] : -1], refs[-1]
    particles, half = incident_ref.shape[0], incident_ref.shape[3]
    start = pl.multiple_of(side_ref[0] * half, half)
    near = nears[0][...]
    for ref in nears[1:]:
        near = near + ref[...]
    out_ref[...] = near
    for particle in range(particles):
        value = incident_ref[particle]
        for ref, step in zip(halves, counts[1]):
            value = value + ref[particle * step]
        window = (particle, slice(None), slice(None), pl.ds(start, half))
        out_ref[window] = out_ref[window] + value


def whole_total(side, incident, nears, halves):
    arrays = [value for value, _ in halves]
    steps = tuple(step for _, step in halves)
    return pl.pallas_call(
        functools.partial(total_kernel, (len(nears), steps)),
        out_shape=jax.ShapeDtypeStruct(nears[0].shape, F32),
        in_specs=[SMEM] + [VMEM] * (1 + len(nears) + len(arrays)),
        out_specs=VMEM,
        compiler_params=params(size_of(*nears, nears[0], incident, *arrays)),
        name="total",
    )(side, incident, *nears, *arrays)


def from_other(value):
    return lax.ppermute(value, "pair", [(0, 1), (1, 0)])


def across(value, bit):
    count = lax.axis_size("owner")
    return lax.ppermute(value, "owner", [(source, source ^ bit) for source in range(count)])


def along(value, shift):
    count = lax.axis_size("owner")
    step = shift * COLUMNS
    return lax.ppermute(
        value, "owner", [(source, (source + step) % count) for source in range(count)]
    )


def scatter_step(incident, scattered, blocks, parts, index, side, layers):
    particles = incident.shape[0]
    every = range(particles)
    by_x = range((particles + 1) // 2)
    by_y = range((particles + 1) // 2, particles)
    rest = range(1, layers)
    at = functools.partial(place_of, particles=particles, layers=layers)
    total_rows = COLUMNS * particles * layers
    first_d = at(3, 0, 0)
    first = parts is None

    def diagonal(particle, layer):
        return at(0, particle, layer)

    other = from_other(scattered)
    x1 = across(scattered, 1)
    y1 = across(scattered, 2)
    fetched = (side, scattered, other, blocks)
    products_d, *made = backward(
        first, (2, 2), first_d, total_rows - first_d, index, *fetched, parts
    )
    if first:
        parts = made[0]

    inputs = [products_d, x1, y1, scattered]
    x_plan = [[(0, diagonal(particle, layer))] for particle in by_x for layer in range(layers)]
    y_plan = [[(0, diagonal(particle, layer))] for particle in by_y for layer in range(layers)]
    x_head, y_head = len(x_plan), len(y_plan)
    x_plan += [[(2, particle)] for particle in by_y]
    y_plan += [[(1, particle)] for particle in by_x]
    x2, y2, copied = pack(
        "pack_second", inputs, [x_plan, y_plan, [[(3, particle)] for particle in every]]
    )
    x2, y2 = across(x2, 1), across(y2, 2)
    z2 = [along(copied, -shift) for shift in rest]
    products, *made = backward(first, (0, 1), 0, first_d, index, *fetched, parts)
    if first:
        parts = made[0]

    inputs = [products, x2, y2]
    x_plan, y_plan = [], []
    for particle in every:
        for layer in range(layers):
            x_terms = [(0, at(1, particle, layer))]
            y_terms = [(0, at(2, particle, layer))]
            if particle in by_x:
                y_terms.append((1, diagonal(particle, layer)))
            else:
                x_terms.append((2, diagonal(particle - len(by_x), layer)))
            x_plan.append(x_terms)
            y_plan.append(y_terms)
    x3, y3, mark = pack("pack_third", inputs, [x_plan, y_plan, [[(1, 0)]]])
    x3, y3 = across(x3, 1), across(y3, 2)

    fields = [x1, y1] + z2
    copies = []
    for particle in every:
        copies.append((0, particle, at(1, particle, 0)))
        copies.append((1, particle, at(2, particle, 0)))
        for shift in rest:
            copies.append((1 + shift, particle, at(0, particle, shift)))
    near_first = forward(
        (0, 0), index, fields, tuple(copies), parts, particles, total_rows, [mark]
    )

    inputs = [products, x3, y3] + z2
    tails = [[(2 + shift, particle)] for particle in every for shift in rest]
    z_plans = [
        [
            [(0, at(0, particle, shift)), (1, diagonal(particle, shift)), (2, diagonal(particle, shift))]
            for particle in every
        ]
        for shift in rest
    ]
    x4, y4, *z4 = pack("pack_fourth", inputs, [tails, tails] + z_plans, [near_first])
    x4, y4 = across(x4, 1), across(y4, 2)
    z4 = [along(value, shift) for shift, value in zip(rest, z4)]

    def tail(particle, shift):
        return particle * len(rest) + shift - 1

    x5, y5, mark = pack(
        "pack_fifth",
        [x4, y4],
        [
            [[(1, tail(particle, shift))] for particle in by_y for shift in rest],
            [[(0, tail(particle, shift))] for particle in by_x for shift in rest],
            [[(0, 0)]],
        ],
    )
    x5, y5 = across(x5, 1), across(y5, 2)
    copies = []
    for particle in every:
        for shift in rest:
            copies.append((0, tail(particle, shift), at(1, particle, shift)))
            copies.append((1, tail(particle, shift), at(2, particle, shift)))
    near_second = forward(
        (1, 1), index, [x4, y4], tuple(copies), parts, particles, total_rows, [mark]
    )
    copies = []
    for heads, ends, head, group in ((0, 2, x_head, by_y), (1, 3, y_head, by_x)):
        for order, particle in enumerate(group):
            copies.append((heads, head + order, at(3, particle, 0)))
            for shift in rest:
                copies.append((ends, tail(order, shift), at(3, particle, shift)))
    near_last = forward(
        (2, 2), index, [x2, y2, x5, y5], tuple(copies), parts, particles, total_rows, [near_second]
    )
    halves = [(products, layers), (x3, layers), (y3, layers)] + [(value, 1) for value in z4]
    return whole_total(side, incident, [near_first, near_second, near_last], halves), parts


def local(incident, tmat, blocks, block_rows, partners, live, owner_of):
    particles = incident.shape[0]
    slots = blocks.shape[0]
    layers = lax.axis_size("owner") // COLUMNS
    my_owner = lax.axis_index("owner").astype(jnp.int32)
    side = lax.axis_index("pair").astype(jnp.int32)
    my_partners = lax.dynamic_slice_in_dim(partners, my_owner * slots, slots)
    ids = jnp.arange(owner_of.shape[0], dtype=jnp.int32)
    partner_row = jnp.sum(
        jnp.where(my_partners[:, None] == ids[None, :], owner_of[None, :], 0), axis=1
    )
    partner_owner = partner_row // particles
    column = (partner_owner % COLUMNS) ^ (my_owner % COLUMNS)
    layer = (partner_owner // COLUMNS - my_owner // COLUMNS) % layers
    place = place_of(column, partner_row % particles, layer, particles, layers)
    group = jnp.where(column == 3, 2, jnp.where((column == 0) | (layer == 0), 0, 1))
    index = (block_rows, live, place, group)
    side_ref = side[None]

    zero = jnp.zeros_like(incident)
    mine = jnp.concatenate(
        (jnp.where(side == 0, incident, zero), jnp.where(side == 1, incident, zero)), axis=3
    )
    theirs = from_other(mine)
    exciting, scattered = apply_tmat(mine, theirs, tmat, side_ref)
    parts = None
    for _ in range(ITERS):
        mine, parts = scatter_step(
            incident, scattered, blocks, parts, index, side_ref, layers
        )
        theirs = from_other(mine)
        exciting, scattered = apply_tmat(mine, theirs, tmat, side_ref)
    return (scattered, exciting)


def solution(mesh):
    in_specs = (
        P("owner", None, None, "pair"),
        P("owner", None, "pair", None),
        P("owner", None, None, "pair"),
        P("owner"),
        P(),
        P("owner"),
        P(),
    )
    out_specs = (P("owner", None, None, "pair"), P("owner", None, None, "pair"))
    return jax.shard_map(local, mesh=mesh, in_specs=in_specs, out_specs=out_specs, check_vma=False)
```

profile of v0, /device:TPU:0, one launch (start us, length us, event | category | flops | bytes accessed | tf_op | source)
XLA Modules:
  0.0 147.6 jit_solution(14979144700826084148)
XLA Ops:
  4.4 1.6 %copy-done = f32[2,2,256,512]{3,2,1,0:T(8,128)S(1)} copy-done((f32[2,2,256,512]{3,2,1,0:T(8,128)S(1)}, f32[2,2,256,512]{3,2,1,0:T(8,128)}, u32[]{:S(2)}) %copy-start) | copy-done | bytes 2097176
  7.5 3.0 %collective-permute-start.1 = (f32[2,2,32,256]{3,2,1,0:T(8,128)S(1)}, f32[2,2,32,256]{3,2,1,0:T(8,128)S(1)}, u32[]{:S(2)}, u32[]{:S(2)}) collective-permute-start(f32[2,2,32,256]{3,2,1,0:T(8,128)S(1)} %get-tuple-element.38.refs_0_.refs_3_), channel_id=1, source_target_pairs={{0,2},{2,0},{4,6},{6,4},{8,10},{10,8},{12,14},{14,12},{16,18},{18,... | collective-permute-start | bytes 393224 | tf_op jit(solution)/shard_map/ppermute | solution.py:351
  12.7 3.4 %backward_group2.2 = (f32[8,2,32,256]{3,2,1,0:T(8,128)S(1)}, bf16[21,2,2,512,256]{4,3,2,1,0:T(8,128)(2,1)}) custom-call(s32[21]{0:T(128)S(1)} %copy-done.3, s32[1]{0:T(128)S(6)} %copy.11.live_ref, s32[21]{0:T(128)S(1)} %multiply_add_fusion.place_ref, s32[21]{0:T(128)S(1)} %get-tuple-element.74.group_ref, s32[1]{0:T(128)} %bitcast.side_ref, ...), custom_call_target="tpu_custom_call" | custom-call | flops 2113929216 | bytes 11010048 | tf_op jit(solution)/shard_map/backward_group2/pallas_call | solution.py:205
  18.2 5.4 %backward_group0.2 = (f32[24,2,32,256]{3,2,1,0:T(8,128)S(1)}, bf16[21,2,2,512,256]{4,3,2,1,0:T(8,128)(2,1)}) custom-call(s32[21]{0:T(128)S(1)} %copy-done.3, s32[1]{0:T(128)S(6)} %copy.11.live_ref, s32[21]{0:T(128)S(1)} %multiply_add_fusion.place_ref, s32[21]{0:T(128)S(1)} %get-tuple-element.74.group_ref, ...), custom_call_target="tpu_custom_call", output_to_operand_aliasing={{1}: (8, {})} | custom-call | flops 2113929216 | bytes 11010048 | tf_op jit(solution)/shard_map/backward_group0/pallas_call | solution.py:205
  23.6 1.8 %collective-permute-done.7.refs_1_.refs_0_ = f32[5,2,32,256]{3,2,1,0:T(8,128)S(1)} collective-permute-done((f32[5,2,32,256]{3,2,1,0:T(8,128)S(1)}, f32[5,2,32,256]{3,2,1,0:T(8,128)S(1)}, u32[]{:S(2)}, u32[]{:S(2)}) %collective-permute-start.7) | collective-permute-done | bytes 327712 | tf_op jit(solution)/shard_map/ppermute | solution.py:351
  25.8 5.7 %collective-permute-start.10 = (f32[8,2,32,256]{3,2,1,0:T(8,128)S(1)}, f32[8,2,32,256]{3,2,1,0:T(8,128)S(1)}, u32[]{:S(2)}, u32[]{:S(2)}) collective-permute-start(f32[8,2,32,256]{3,2,1,0:T(8,128)S(1)} %get-tuple-element.48), channel_id=1, source_target_pairs={{0,4},{2,6},{4,0},{6,2},{8,12},{10,14},{12,8},{14,10},{16,20},{18,... | collective-permute-start | bytes 1572872 | tf_op jit(solution)/shard_map/ppermute | solution.py:351
  31.5 7.5 %collective-permute-start.4 = (f32[2,2,32,256]{3,2,1,0:T(8,128)S(1)}, f32[2,2,32,256]{3,2,1,0:T(8,128)S(1)}, u32[]{:S(2)}, u32[]{:S(2)}) collective-permute-start(f32[2,2,32,256]{3,2,1,0:T(8,128)S(1)} %get-tuple-element.40), channel_id=1, source_target_pairs={{0,24},{2,26},{4,28},{6,30},{8,0},{10,2},{12,4},{14,6},{16,8},{18,... | collective-permute-start | bytes 393224 | tf_op jit(solution)/shard_map/ppermute | solution.py:357
  39.6 3.4 %collective-permute-done.4.refs_2_.refs_3_ = f32[2,2,32,256]{3,2,1,0:T(8,128)S(1)} collective-permute-done((f32[2,2,32,256]{3,2,1,0:T(8,128)S(1)}, f32[2,2,32,256]{3,2,1,0:T(8,128)S(1)}, u32[]{:S(2)}, u32[]{:S(2)}) %collective-permute-start.4) | collective-permute-done | bytes 131104 | tf_op jit(solution)/shard_map/ppermute | solution.py:357
  43.0 5.4 %collective-permute-done.5.refs_3_.refs_4_ = f32[2,2,32,256]{3,2,1,0:T(8,128)S(1)} collective-permute-done((f32[2,2,32,256]{3,2,1,0:T(8,128)S(1)}, f32[2,2,32,256]{3,2,1,0:T(8,128)S(1)}, u32[]{:S(2)}, u32[]{:S(2)}) %collective-permute-start.5) | collective-permute-done | bytes 131104 | tf_op jit(solution)/shard_map/ppermute | solution.py:357
  48.4 2.8 %forward_group0.2.refs_6_.refs_0_ = f32[2,2,32,512]{3,2,1,0:T(8,128)S(1)} custom-call(s32[21]{0:T(128)S(1)} %copy-done.3, s32[1]{0:T(128)S(6)} %copy.11.live_ref, s32[21]{0:T(128)S(1)} %multiply_add_fusion.place_ref, s32[21]{0:T(128)S(1)} %get-tuple-element.74.group_ref, f32[2,2,32,256]{3,2,1,0:T(8,128)S(1)} %collective-permute-done.1.refs_1_.refs_0_, ...), custom_call_target="tpu_custom_call" | custom-call | flops 1409286144 | bytes 7340032 | tf_op jit(solution)/shard_map/forward_group0/pallas_call | solution.py:272
  51.4 2.8 %collective-permute-start.11 = (f32[6,2,32,256]{3,2,1,0:T(8,128)S(1)}, f32[6,2,32,256]{3,2,1,0:T(8,128)S(1)}, u32[]{:S(2)}, u32[]{:S(2)}) collective-permute-start(f32[6,2,32,256]{3,2,1,0:T(8,128)S(1)} %get-tuple-element.49), channel_id=1, source_target_pairs={{0,2},{2,0},{4,6},{6,4},{8,10},{10,8},{12,14},{14,12},{16,18},{18,... | collective-permute-start | bytes 1179656 | tf_op jit(solution)/shard_map/ppermute | solution.py:351
  54.4 7.9 %collective-permute-done.11.refs_0_ = f32[6,2,32,256]{3,2,1,0:T(8,128)S(1)} collective-permute-done((f32[6,2,32,256]{3,2,1,0:T(8,128)S(1)}, f32[6,2,32,256]{3,2,1,0:T(8,128)S(1)}, u32[]{:S(2)}, u32[]{:S(2)}) %collective-permute-start.11) | collective-permute-done | bytes 393248 | tf_op jit(solution)/shard_map/ppermute | solution.py:351
  64.3 1.7 %collective-permute-start.14 = (f32[3,2,32,256]{3,2,1,0:T(8,128)S(1)}, f32[3,2,32,256]{3,2,1,0:T(8,128)S(1)}, u32[]{:S(2)}, u32[]{:S(2)}) collective-permute-start(f32[3,2,32,256]{3,2,1,0:T(8,128)S(1)} %get-tuple-element.53), channel_id=1, source_target_pairs={{0,4},{2,6},{4,0},{6,2},{8,12},{10,14},{12,8},{14,10},{16,20},{18,... | collective-permute-start | bytes 589832 | tf_op jit(solution)/shard_map/ppermute | solution.py:351
  66.1 3.4 %collective-permute-start.16 = (f32[2,2,32,256]{3,2,1,0:T(8,128)S(1)}, f32[2,2,32,256]{3,2,1,0:T(8,128)S(1)}, u32[]{:S(2)}, u32[]{:S(2)}) collective-permute-start(f32[2,2,32,256]{3,2,1,0:T(8,128)S(1)} %get-tuple-element.55), channel_id=1, source_target_pairs={{0,16},{2,18},{4,20},{6,22},{8,24},{10,26},{12,28},{14,30},{16,0},... | collective-permute-start | bytes 393224 | tf_op jit(solution)/shard_map/ppermute | solution.py:357
  69.5 2.9 %collective-permute-start.17 = (f32[2,2,32,256]{3,2,1,0:T(8,128)S(1)}, f32[2,2,32,256]{3,2,1,0:T(8,128)S(1)}, u32[]{:S(2)}, u32[]{:S(2)}) collective-permute-start(f32[2,2,32,256]{3,2,1,0:T(8,128)S(1)} %get-tuple-element.56), channel_id=1, source_target_pairs={{0,24},{2,26},{4,28},{6,30},{8,0},{10,2},{12,4},{14,6},{16,8},{18,... | collective-permute-start | bytes 393224 | tf_op jit(solution)/shard_map/ppermute | solution.py:357
  72.4 3.3 %forward_group1.2.refs_5_.refs_1_ = f32[2,2,32,512]{3,2,1,0:T(8,128)S(1)} custom-call(s32[21]{0:T(128)S(1)} %copy-done.4, s32[1]{0:T(128)S(6)} %copy.11.live_ref, s32[21]{0:T(128)S(1)} %multiply_add_fusion.place_ref, s32[21]{0:T(128)S(1)} %get-tuple-element.74.group_ref, f32[6,2,32,256]{3,2,1,0:T(8,128)S(1)} %collective-permute-done.11.refs_0_, ...), custom_call_target="tpu_custom_call" | custom-call | flops 1409286144 | bytes 7340032 | tf_op jit(solution)/shard_map/forward_group1/pallas_call | solution.py:272
  75.8 2.8 %forward_group2.2.refs_2_ = f32[2,2,32,512]{3,2,1,0:T(8,128)S(1)} custom-call(s32[21]{0:T(128)S(1)} %copy-done.4, s32[1]{0:T(128)S(6)} %copy.11.live_ref, s32[21]{0:T(128)S(1)} %multiply_add_fusion.place_ref, s32[21]{0:T(128)S(1)} %get-tuple-element.74.group_ref, f32[5,2,32,256]{3,2,1,0:T(8,128)S(1)} %collective-permute-done.7.refs_1_.refs_0_, ...), custom_call_target="tpu_custom_call" | custom-call | flops 1409286144 | bytes 7340032 | tf_op jit(solution)/shard_map/forward_group2/pallas_call | solution.py:272
  83.3 3.7 %collective-permute-start.20 = (f32[2,2,32,256]{3,2,1,0:T(8,128)S(1)}, f32[2,2,32,256]{3,2,1,0:T(8,128)S(1)}, u32[]{:S(2)}, u32[]{:S(2)}) collective-permute-start(f32[2,2,32,256]{3,2,1,0:T(8,128)S(1)} %get-tuple-element.57.refs_0_.refs_3_), channel_id=1, source_target_pairs={{0,4},{2,6},{4,0},{6,2},{8,12},{10,14},{12,8},{14,10},{16,20},{18,... | collective-permute-start | bytes 393224 | tf_op jit(solution)/shard_map/ppermute | solution.py:351
  87.0 2.5 %backward_group2.3.refs_0_ = f32[8,2,32,256]{3,2,1,0:T(8,128)S(1)} custom-call(s32[21]{0:T(128)S(1)} %copy-done.4, s32[1]{0:T(128)S(6)} %copy.11.live_ref, s32[21]{0:T(128)S(1)} %multiply_add_fusion.place_ref, s32[21]{0:T(128)S(1)} %get-tuple-element.74.group_ref, s32[1]{0:T(128)} %bitcast.side_ref, f32[2,2,32,256]{3,2,1,0:T(8,128)S(1)} %get-tuple-element.57.refs_0_.refs_3_, ...), custom_call_target="tpu_custom_call" | custom-call | flops 2113929216 | bytes 11010048 | tf_op jit(solution)/shard_map/backward_group2/pallas_call | solution.py:205
  91.1 1.8 %collective-permute-start.25 = (f32[5,2,32,256]{3,2,1,0:T(8,128)S(1)}, f32[5,2,32,256]{3,2,1,0:T(8,128)S(1)}, u32[]{:S(2)}, u32[]{:S(2)}) collective-permute-start(f32[5,2,32,256]{3,2,1,0:T(8,128)S(1)} %get-tuple-element.59), channel_id=1, source_target_pairs={{0,2},{2,0},{4,6},{6,4},{8,10},{10,8},{12,14},{14,12},{16,18},{18,... | collective-permute-start | bytes 983048 | tf_op jit(solution)/shard_map/ppermute | solution.py:351
  92.9 1.7 %collective-permute-start.26 = (f32[5,2,32,256]{3,2,1,0:T(8,128)S(1)}, f32[5,2,32,256]{3,2,1,0:T(8,128)S(1)}, u32[]{:S(2)}, u32[]{:S(2)}) collective-permute-start(f32[5,2,32,256]{3,2,1,0:T(8,128)S(1)} %get-tuple-element.60), channel_id=1, source_target_pairs={{0,4},{2,6},{4,0},{6,2},{8,12},{10,14},{12,8},{14,10},{16,20},{18,... | collective-permute-start | bytes 983048 | tf_op jit(solution)/shard_map/ppermute | solution.py:351
  94.6 3.7 %backward_group0.3.refs_0_.refs_3_ = f32[24,2,32,256]{3,2,1,0:T(8,128)S(1)} custom-call(s32[21]{0:T(128)S(1)} %copy-done.4, s32[1]{0:T(128)S(6)} %copy.11.live_ref, s32[21]{0:T(128)S(1)} %multiply_add_fusion.place_ref, s32[21]{0:T(128)S(1)} %get-tuple-element.74.group_ref, s32[1]{0:T(128)} %bitcast.side_ref, ...), custom_call_target="tpu_custom_call" | custom-call | flops 2113929216 | bytes 11010048 | tf_op jit(solution)/shard_map/backward_group0/pallas_call | solution.py:205
  98.4 2.2 %collective-permute-done.25.refs_1_.refs_0_ = f32[5,2,32,256]{3,2,1,0:T(8,128)S(1)} collective-permute-done((f32[5,2,32,256]{3,2,1,0:T(8,128)S(1)}, f32[5,2,32,256]{3,2,1,0:T(8,128)S(1)}, u32[]{:S(2)}, u32[]{:S(2)}) %collective-permute-start.25) | collective-permute-done | bytes 327712 | tf_op jit(solution)/shard_map/ppermute | solution.py:351
  106.0 4.6 %collective-permute-done.22.refs_2_.refs_3_ = f32[2,2,32,256]{3,2,1,0:T(8,128)S(1)} collective-permute-done((f32[2,2,32,256]{3,2,1,0:T(8,128)S(1)}, f32[2,2,32,256]{3,2,1,0:T(8,128)S(1)}, u32[]{:S(2)}, u32[]{:S(2)}) %collective-permute-start.22) | collective-permute-done | bytes 131104 | tf_op jit(solution)/shard_map/ppermute | solution.py:357
  110.6 5.4 %collective-permute-done.23.refs_3_.refs_4_ = f32[2,2,32,256]{3,2,1,0:T(8,128)S(1)} collective-permute-done((f32[2,2,32,256]{3,2,1,0:T(8,128)S(1)}, f32[2,2,32,256]{3,2,1,0:T(8,128)S(1)}, u32[]{:S(2)}, u32[]{:S(2)}) %collective-permute-start.23) | collective-permute-done | bytes 131104 | tf_op jit(solution)/shard_map/ppermute | solution.py:357
  116.0 2.8 %forward_group0.3.refs_6_.refs_0_ = f32[2,2,32,512]{3,2,1,0:T(8,128)S(1)} custom-call(s32[21]{0:T(128)S(1)} %copy-done.4, s32[1]{0:T(128)S(6)} %copy.11.live_ref, s32[21]{0:T(128)S(1)} %multiply_add_fusion.place_ref, s32[21]{0:T(128)S(1)} %get-tuple-element.74.group_ref, f32[2,2,32,256]{3,2,1,0:T(8,128)S(1)} %collective-permute-done.19.refs_1_.refs_0_, ...), custom_call_target="tpu_custom_call" | custom-call | flops 1409286144 | bytes 7340032 | tf_op jit(solution)/shard_map/forward_group0/pallas_call | solution.py:272
  118.9 2.9 %collective-permute-start.29 = (f32[6,2,32,256]{3,2,1,0:T(8,128)S(1)}, f32[6,2,32,256]{3,2,1,0:T(8,128)S(1)}, u32[]{:S(2)}, u32[]{:S(2)}) collective-permute-start(f32[6,2,32,256]{3,2,1,0:T(8,128)S(1)} %get-tuple-element.64), channel_id=1, source_target_pairs={{0,2},{2,0},{4,6},{6,4},{8,10},{10,8},{12,14},{14,12},{16,18},{18,... | collective-permute-start | bytes 1179656 | tf_op jit(solution)/shard_map/ppermute | solution.py:351
  121.8 7.6 %collective-permute-done.29.refs_0_ = f32[6,2,32,256]{3,2,1,0:T(8,128)S(1)} collective-permute-done((f32[6,2,32,256]{3,2,1,0:T(8,128)S(1)}, f32[6,2,32,256]{3,2,1,0:T(8,128)S(1)}, u32[]{:S(2)}, u32[]{:S(2)}) %collective-permute-start.29) | collective-permute-done | bytes 393248 | tf_op jit(solution)/shard_map/ppermute | solution.py:351
  132.2 3.1 %collective-permute-start.34 = (f32[2,2,32,256]{3,2,1,0:T(8,128)S(1)}, f32[2,2,32,256]{3,2,1,0:T(8,128)S(1)}, u32[]{:S(2)}, u32[]{:S(2)}) collective-permute-start(f32[2,2,32,256]{3,2,1,0:T(8,128)S(1)} %get-tuple-element.70), channel_id=1, source_target_pairs={{0,16},{2,18},{4,20},{6,22},{8,24},{10,26},{12,28},{14,30},{16,0},... | collective-permute-start | bytes 393224 | tf_op jit(solution)/shard_map/ppermute | solution.py:357
  135.3 2.9 %collective-permute-start.35 = (f32[2,2,32,256]{3,2,1,0:T(8,128)S(1)}, f32[2,2,32,256]{3,2,1,0:T(8,128)S(1)}, u32[]{:S(2)}, u32[]{:S(2)}) collective-permute-start(f32[2,2,32,256]{3,2,1,0:T(8,128)S(1)} %get-tuple-element.71), channel_id=1, source_target_pairs={{0,24},{2,26},{4,28},{6,30},{8,0},{10,2},{12,4},{14,6},{16,8},{18,... | collective-permute-start | bytes 393224 | tf_op jit(solution)/shard_map/ppermute | solution.py:357
  138.3 3.2 %forward_group1.3.refs_5_.refs_1_ = f32[2,2,32,512]{3,2,1,0:T(8,128)S(1)} custom-call(s32[21]{0:T(128)S(1)} %copy-done.4, s32[1]{0:T(128)S(6)} %copy.11.live_ref, s32[21]{0:T(128)S(1)} %multiply_add_fusion.place_ref, s32[21]{0:T(128)S(1)} %get-tuple-element.74.group_ref, f32[6,2,32,256]{3,2,1,0:T(8,128)S(1)} %collective-permute-done.29.refs_0_, ...), custom_call_target="tpu_custom_call" | custom-call | flops 1409286144 | bytes 7340032 | tf_op jit(solution)/shard_map/forward_group1/pallas_call | solution.py:272
  141.5 2.8 %forward_group2.3.refs_2_ = f32[2,2,32,512]{3,2,1,0:T(8,128)S(1)} custom-call(s32[21]{0:T(128)S(1)} %copy-done.4, s32[1]{0:T(128)S(6)} %copy.11.live_ref, s32[21]{0:T(128)S(1)} %multiply_add_fusion.place_ref, s32[21]{0:T(128)S(1)} %get-tuple-element.74.group_ref, f32[5,2,32,256]{3,2,1,0:T(8,128)S(1)} %collective-permute-done.25.refs_1_.refs_0_, ...), custom_call_target="tpu_custom_call" | custom-call | flops 1409286144 | bytes 7340032 | tf_op jit(solution)/shard_map/forward_group2/pallas_call | solution.py:272
  (81 shorter events, 29.9 us)
Async XLA Ops:
  7.5 8.6 %collective-permute-start.1 = (f32[2,2,32,256]{3,2,1,0:T(8,128)S(1)}, f32[2,2,32,256]{3,2,1,0:T(8,128)S(1)}, u32[]{:S(2)}, u32[]{:S(2)}) collective-permute-start(f32[2,2,32,256]{3,2,1,0:T(8,128)S(1)} %get-tuple-element.38.refs_0_.refs_3_), channel_id=1, source_target_pairs={{0,2},{2,0},{4,6},{6,4},{8,10},{10,8},{12,14},{14,12},{16,18},{18,... | collective-permute-start | bytes 393224 | tf_op jit(solution)/shard_map/ppermute | solution.py:351
  10.5 5.6 %collective-permute-start.2 = (f32[2,2,32,256]{3,2,1,0:T(8,128)S(1)}, f32[2,2,32,256]{3,2,1,0:T(8,128)S(1)}, u32[]{:S(2)}, u32[]{:S(2)}) collective-permute-start(f32[2,2,32,256]{3,2,1,0:T(8,128)S(1)} %get-tuple-element.38.refs_0_.refs_3_), channel_id=1, source_target_pairs={{0,4},{2,6},{4,0},{6,2},{8,12},{10,14},{12,8},{14,10},{16,20},{18,... | collective-permute-start | bytes 393224 | tf_op jit(solution)/shard_map/ppermute | solution.py:351
  16.3 9.1 %collective-permute-start.7 = (f32[5,2,32,256]{3,2,1,0:T(8,128)S(1)}, f32[5,2,32,256]{3,2,1,0:T(8,128)S(1)}, u32[]{:S(2)}, u32[]{:S(2)}) collective-permute-start(f32[5,2,32,256]{3,2,1,0:T(8,128)S(1)} %get-tuple-element.44), channel_id=1, source_target_pairs={{0,2},{2,0},{4,6},{6,4},{8,10},{10,8},{12,14},{14,12},{16,18},{18,... | collective-permute-start | bytes 983048 | tf_op jit(solution)/shard_map/ppermute | solution.py:351
  16.9 8.8 %collective-permute-start.8 = (f32[5,2,32,256]{3,2,1,0:T(8,128)S(1)}, f32[5,2,32,256]{3,2,1,0:T(8,128)S(1)}, u32[]{:S(2)}, u32[]{:S(2)}) collective-permute-start(f32[5,2,32,256]{3,2,1,0:T(8,128)S(1)} %get-tuple-element.45), channel_id=1, source_target_pairs={{0,4},{2,6},{4,0},{6,2},{8,12},{10,14},{12,8},{14,10},{16,20},{18,... | collective-permute-start | bytes 983048 | tf_op jit(solution)/shard_map/ppermute | solution.py:351
  25.8 25.4 %collective-permute-start.10 = (f32[8,2,32,256]{3,2,1,0:T(8,128)S(1)}, f32[8,2,32,256]{3,2,1,0:T(8,128)S(1)}, u32[]{:S(2)}, u32[]{:S(2)}) collective-permute-start(f32[8,2,32,256]{3,2,1,0:T(8,128)S(1)} %get-tuple-element.48), channel_id=1, source_target_pairs={{0,4},{2,6},{4,0},{6,2},{8,12},{10,14},{12,8},{14,10},{16,20},{18,... | collective-permute-start | bytes 1572872 | tf_op jit(solution)/shard_map/ppermute | solution.py:351
  31.5 19.7 %collective-permute-start.9 = (f32[8,2,32,256]{3,2,1,0:T(8,128)S(1)}, f32[8,2,32,256]{3,2,1,0:T(8,128)S(1)}, u32[]{:S(2)}, u32[]{:S(2)}) collective-permute-start(f32[8,2,32,256]{3,2,1,0:T(8,128)S(1)} %get-tuple-element.47), channel_id=1, source_target_pairs={{0,2},{2,0},{4,6},{6,4},{8,10},{10,8},{12,14},{14,12},{16,18},{18,... | collective-permute-start | bytes 1572872 | tf_op jit(solution)/shard_map/ppermute | solution.py:351
  31.5 11.5 %collective-permute-start.4 = (f32[2,2,32,256]{3,2,1,0:T(8,128)S(1)}, f32[2,2,32,256]{3,2,1,0:T(8,128)S(1)}, u32[]{:S(2)}, u32[]{:S(2)}) collective-permute-start(f32[2,2,32,256]{3,2,1,0:T(8,128)S(1)} %get-tuple-element.40), channel_id=1, source_target_pairs={{0,24},{2,26},{4,28},{6,30},{8,0},{10,2},{12,4},{14,6},{16,8},{18,... | collective-permute-start | bytes 393224 | tf_op jit(solution)/shard_map/ppermute | solution.py:357
  39.0 9.4 %collective-permute-start.5 = (f32[2,2,32,256]{3,2,1,0:T(8,128)S(1)}, f32[2,2,32,256]{3,2,1,0:T(8,128)S(1)}, u32[]{:S(2)}, u32[]{:S(2)}) collective-permute-start(f32[2,2,32,256]{3,2,1,0:T(8,128)S(1)} %get-tuple-element.40), channel_id=1, source_target_pairs={{0,16},{2,18},{4,20},{6,22},{8,24},{10,26},{12,28},{14,30},{16,0},... | collective-permute-start | bytes 393224 | tf_op jit(solution)/shard_map/ppermute | solution.py:357
  39.0 9.4 %collective-permute-start.6 = (f32[2,2,32,256]{3,2,1,0:T(8,128)S(1)}, f32[2,2,32,256]{3,2,1,0:T(8,128)S(1)}, u32[]{:S(2)}, u32[]{:S(2)}) collective-permute-start(f32[2,2,32,256]{3,2,1,0:T(8,128)S(1)} %get-tuple-element.40), channel_id=1, source_target_pairs={{0,8},{2,10},{4,12},{6,14},{8,16},{10,18},{12,20},{14,22},{16,24},... | collective-permute-start | bytes 393224 | tf_op jit(solution)/shard_map/ppermute | solution.py:357
  51.4 10.9 %collective-permute-start.11 = (f32[6,2,32,256]{3,2,1,0:T(8,128)S(1)}, f32[6,2,32,256]{3,2,1,0:T(8,128)S(1)}, u32[]{:S(2)}, u32[]{:S(2)}) collective-permute-start(f32[6,2,32,256]{3,2,1,0:T(8,128)S(1)} %get-tuple-element.49), channel_id=1, source_target_pairs={{0,2},{2,0},{4,6},{6,4},{8,10},{10,8},{12,14},{14,12},{16,18},{18,... | collective-permute-start | bytes 1179656 | tf_op jit(solution)/shard_map/ppermute | solution.py:351
  54.2 9.6 %collective-permute-start.12 = (f32[6,2,32,256]{3,2,1,0:T(8,128)S(1)}, f32[6,2,32,256]{3,2,1,0:T(8,128)S(1)}, u32[]{:S(2)}, u32[]{:S(2)}) collective-permute-start(f32[6,2,32,256]{3,2,1,0:T(8,128)S(1)} %get-tuple-element.50), channel_id=1, source_target_pairs={{0,4},{2,6},{4,0},{6,2},{8,12},{10,14},{12,8},{14,10},{16,20},{18,... | collective-permute-start | bytes 1179656 | tf_op jit(solution)/shard_map/ppermute | solution.py:351
  63.8 12.0 %collective-permute-start.13 = (f32[3,2,32,256]{3,2,1,0:T(8,128)S(1)}, f32[3,2,32,256]{3,2,1,0:T(8,128)S(1)}, u32[]{:S(2)}, u32[]{:S(2)}) collective-permute-start(f32[3,2,32,256]{3,2,1,0:T(8,128)S(1)} %get-tuple-element.52), channel_id=1, source_target_pairs={{0,2},{2,0},{4,6},{6,4},{8,10},{10,8},{12,14},{14,12},{16,18},{18,... | collective-permute-start | bytes 589832 | tf_op jit(solution)/shard_map/ppermute | solution.py:351
  64.3 11.5 %collective-permute-start.14 = (f32[3,2,32,256]{3,2,1,0:T(8,128)S(1)}, f32[3,2,32,256]{3,2,1,0:T(8,128)S(1)}, u32[]{:S(2)}, u32[]{:S(2)}) collective-permute-start(f32[3,2,32,256]{3,2,1,0:T(8,128)S(1)} %get-tuple-element.53), channel_id=1, source_target_pairs={{0,4},{2,6},{4,0},{6,2},{8,12},{10,14},{12,8},{14,10},{16,20},{18,... | collective-permute-start | bytes 589832 | tf_op jit(solution)/shard_map/ppermute | solution.py:351
  66.0 12.5 %collective-permute-start.15 = (f32[2,2,32,256]{3,2,1,0:T(8,128)S(1)}, f32[2,2,32,256]{3,2,1,0:T(8,128)S(1)}, u32[]{:S(2)}, u32[]{:S(2)}) collective-permute-start(f32[2,2,32,256]{3,2,1,0:T(8,128)S(1)} %get-tuple-element.54), channel_id=1, source_target_pairs={{0,8},{2,10},{4,12},{6,14},{8,16},{10,18},{12,20},{14,22},{16,24},... | collective-permute-start | bytes 393224 | tf_op jit(solution)/shard_map/ppermute | solution.py:357
  66.1 12.5 %collective-permute-start.16 = (f32[2,2,32,256]{3,2,1,0:T(8,128)S(1)}, f32[2,2,32,256]{3,2,1,0:T(8,128)S(1)}, u32[]{:S(2)}, u32[]{:S(2)}) collective-permute-start(f32[2,2,32,256]{3,2,1,0:T(8,128)S(1)} %get-tuple-element.55), channel_id=1, source_target_pairs={{0,16},{2,18},{4,20},{6,22},{8,24},{10,26},{12,28},{14,30},{16,0},... | collective-permute-start | bytes 393224 | tf_op jit(solution)/shard_map/ppermute | solution.py:357
  69.5 9.1 %collective-permute-start.17 = (f32[2,2,32,256]{3,2,1,0:T(8,128)S(1)}, f32[2,2,32,256]{3,2,1,0:T(8,128)S(1)}, u32[]{:S(2)}, u32[]{:S(2)}) collective-permute-start(f32[2,2,32,256]{3,2,1,0:T(8,128)S(1)} %get-tuple-element.56), channel_id=1, source_target_pairs={{0,24},{2,26},{4,28},{6,30},{8,0},{10,2},{12,4},{14,6},{16,8},{18,... | collective-permute-start | bytes 393224 | tf_op jit(solution)/shard_map/ppermute | solution.py:357
  82.0 7.5 %collective-permute-start.19 = (f32[2,2,32,256]{3,2,1,0:T(8,128)S(1)}, f32[2,2,32,256]{3,2,1,0:T(8,128)S(1)}, u32[]{:S(2)}, u32[]{:S(2)}) collective-permute-start(f32[2,2,32,256]{3,2,1,0:T(8,128)S(1)} %get-tuple-element.57.refs_0_.refs_3_), channel_id=1, source_target_pairs={{0,2},{2,0},{4,6},{6,4},{8,10},{10,8},{12,14},{14,12},{16,18},{18,... | collective-permute-start | bytes 393224 | tf_op jit(solution)/shard_map/ppermute | solution.py:351
  83.3 7.7 %collective-permute-start.20 = (f32[2,2,32,256]{3,2,1,0:T(8,128)S(1)}, f32[2,2,32,256]{3,2,1,0:T(8,128)S(1)}, u32[]{:S(2)}, u32[]{:S(2)}) collective-permute-start(f32[2,2,32,256]{3,2,1,0:T(8,128)S(1)} %get-tuple-element.57.refs_0_.refs_3_), channel_id=1, source_target_pairs={{0,4},{2,6},{4,0},{6,2},{8,12},{10,14},{12,8},{14,10},{16,20},{18,... | collective-permute-start | bytes 393224 | tf_op jit(solution)/shard_map/ppermute | solution.py:351
  91.1 9.5 %collective-permute-start.25 = (f32[5,2,32,256]{3,2,1,0:T(8,128)S(1)}, f32[5,2,32,256]{3,2,1,0:T(8,128)S(1)}, u32[]{:S(2)}, u32[]{:S(2)}) collective-permute-start(f32[5,2,32,256]{3,2,1,0:T(8,128)S(1)} %get-tuple-element.59), channel_id=1, source_target_pairs={{0,2},{2,0},{4,6},{6,4},{8,10},{10,8},{12,14},{14,12},{16,18},{18,... | collective-permute-start | bytes 983048 | tf_op jit(solution)/shard_map/ppermute | solution.py:351
  92.9 8.9 %collective-permute-start.26 = (f32[5,2,32,256]{3,2,1,0:T(8,128)S(1)}, f32[5,2,32,256]{3,2,1,0:T(8,128)S(1)}, u32[]{:S(2)}, u32[]{:S(2)}) collective-permute-start(f32[5,2,32,256]{3,2,1,0:T(8,128)S(1)} %get-tuple-element.60), channel_id=1, source_target_pairs={{0,4},{2,6},{4,0},{6,2},{8,12},{10,14},{12,8},{14,10},{16,20},{18,... | collective-permute-start | bytes 983048 | tf_op jit(solution)/shard_map/ppermute | solution.py:351
  101.9 16.9 %collective-permute-start.27 = (f32[8,2,32,256]{3,2,1,0:T(8,128)S(1)}, f32[8,2,32,256]{3,2,1,0:T(8,128)S(1)}, u32[]{:S(2)}, u32[]{:S(2)}) collective-permute-start(f32[8,2,32,256]{3,2,1,0:T(8,128)S(1)} %get-tuple-element.62), channel_id=1, source_target_pairs={{0,2},{2,0},{4,6},{6,4},{8,10},{10,8},{12,14},{14,12},{16,18},{18,... | collective-permute-start | bytes 1572872 | tf_op jit(solution)/shard_map/ppermute | solution.py:351
  102.5 16.3 %collective-permute-start.28 = (f32[8,2,32,256]{3,2,1,0:T(8,128)S(1)}, f32[8,2,32,256]{3,2,1,0:T(8,128)S(1)}, u32[]{:S(2)}, u32[]{:S(2)}) collective-permute-start(f32[8,2,32,256]{3,2,1,0:T(8,128)S(1)} %get-tuple-element.63), channel_id=1, source_target_pairs={{0,4},{2,6},{4,0},{6,2},{8,12},{10,14},{12,8},{14,10},{16,20},{18,... | collective-permute-start | bytes 1572872 | tf_op jit(solution)/shard_map/ppermute | solution.py:351
  104.0 6.6 %collective-permute-start.22 = (f32[2,2,32,256]{3,2,1,0:T(8,128)S(1)}, f32[2,2,32,256]{3,2,1,0:T(8,128)S(1)}, u32[]{:S(2)}, u32[]{:S(2)}) collective-permute-start(f32[2,2,32,256]{3,2,1,0:T(8,128)S(1)} %get-tuple-element.58), channel_id=1, source_target_pairs={{0,24},{2,26},{4,28},{6,30},{8,0},{10,2},{12,4},{14,6},{16,8},{18,... | collective-permute-start | bytes 393224 | tf_op jit(solution)/shard_map/ppermute | solution.py:357
  104.5 11.5 %collective-permute-start.23 = (f32[2,2,32,256]{3,2,1,0:T(8,128)S(1)}, f32[2,2,32,256]{3,2,1,0:T(8,128)S(1)}, u32[]{:S(2)}, u32[]{:S(2)}) collective-permute-start(f32[2,2,32,256]{3,2,1,0:T(8,128)S(1)} %get-tuple-element.58), channel_id=1, source_target_pairs={{0,16},{2,18},{4,20},{6,22},{8,24},{10,26},{12,28},{14,30},{16,0},... | collective-permute-start | bytes 393224 | tf_op jit(solution)/shard_map/ppermute | solution.py:357
  104.6 11.4 %collective-permute-start.24 = (f32[2,2,32,256]{3,2,1,0:T(8,128)S(1)}, f32[2,2,32,256]{3,2,1,0:T(8,128)S(1)}, u32[]{:S(2)}, u32[]{:S(2)}) collective-permute-start(f32[2,2,32,256]{3,2,1,0:T(8,128)S(1)} %get-tuple-element.58), channel_id=1, source_target_pairs={{0,8},{2,10},{4,12},{6,14},{8,16},{10,18},{12,20},{14,22},{16,24},... | collective-permute-start | bytes 393224 | tf_op jit(solution)/shard_map/ppermute | solution.py:357
  118.9 10.5 %collective-permute-start.29 = (f32[6,2,32,256]{3,2,1,0:T(8,128)S(1)}, f32[6,2,32,256]{3,2,1,0:T(8,128)S(1)}, u32[]{:S(2)}, u32[]{:S(2)}) collective-permute-start(f32[6,2,32,256]{3,2,1,0:T(8,128)S(1)} %get-tuple-element.64), channel_id=1, source_target_pairs={{0,2},{2,0},{4,6},{6,4},{8,10},{10,8},{12,14},{14,12},{16,18},{18,... | collective-permute-start | bytes 1179656 | tf_op jit(solution)/shard_map/ppermute | solution.py:351
  121.8 9.1 %collective-permute-start.30 = (f32[6,2,32,256]{3,2,1,0:T(8,128)S(1)}, f32[6,2,32,256]{3,2,1,0:T(8,128)S(1)}, u32[]{:S(2)}, u32[]{:S(2)}) collective-permute-start(f32[6,2,32,256]{3,2,1,0:T(8,128)S(1)} %get-tuple-element.65), channel_id=1, source_target_pairs={{0,4},{2,6},{4,0},{6,2},{8,12},{10,14},{12,8},{14,10},{16,20},{18,... | collective-permute-start | bytes 1179656 | tf_op jit(solution)/shard_map/ppermute | solution.py:351
  130.9 10.6 %collective-permute-start.31 = (f32[3,2,32,256]{3,2,1,0:T(8,128)S(1)}, f32[3,2,32,256]{3,2,1,0:T(8,128)S(1)}, u32[]{:S(2)}, u32[]{:S(2)}) collective-permute-start(f32[3,2,32,256]{3,2,1,0:T(8,128)S(1)} %get-tuple-element.67), channel_id=1, source_target_pairs={{0,2},{2,0},{4,6},{6,4},{8,10},{10,8},{12,14},{14,12},{16,18},{18,... | collective-permute-start | bytes 589832 | tf_op jit(solution)/shard_map/ppermute | solution.py:351
  131.4 10.2 %collective-permute-start.32 = (f32[3,2,32,256]{3,2,1,0:T(8,128)S(1)}, f32[3,2,32,256]{3,2,1,0:T(8,128)S(1)}, u32[]{:S(2)}, u32[]{:S(2)}) collective-permute-start(f32[3,2,32,256]{3,2,1,0:T(8,128)S(1)} %get-tuple-element.68), channel_id=1, source_target_pairs={{0,4},{2,6},{4,0},{6,2},{8,12},{10,14},{12,8},{14,10},{16,20},{18,... | collective-permute-start | bytes 589832 | tf_op jit(solution)/shard_map/ppermute | solution.py:351
  131.9 12.4 %collective-permute-start.33 = (f32[2,2,32,256]{3,2,1,0:T(8,128)S(1)}, f32[2,2,32,256]{3,2,1,0:T(8,128)S(1)}, u32[]{:S(2)}, u32[]{:S(2)}) collective-permute-start(f32[2,2,32,256]{3,2,1,0:T(8,128)S(1)} %get-tuple-element.69), channel_id=1, source_target_pairs={{0,8},{2,10},{4,12},{6,14},{8,16},{10,18},{12,20},{14,22},{16,24},... | collective-permute-start | bytes 393224 | tf_op jit(solution)/shard_map/ppermute | solution.py:357
  132.2 12.2 %collective-permute-start.34 = (f32[2,2,32,256]{3,2,1,0:T(8,128)S(1)}, f32[2,2,32,256]{3,2,1,0:T(8,128)S(1)}, u32[]{:S(2)}, u32[]{:S(2)}) collective-permute-start(f32[2,2,32,256]{3,2,1,0:T(8,128)S(1)} %get-tuple-element.70), channel_id=1, source_target_pairs={{0,16},{2,18},{4,20},{6,22},{8,24},{10,26},{12,28},{14,30},{16,0},... | collective-permute-start | bytes 393224 | tf_op jit(solution)/shard_map/ppermute | solution.py:357
  135.3 9.0 %collective-permute-start.35 = (f32[2,2,32,256]{3,2,1,0:T(8,128)S(1)}, f32[2,2,32,256]{3,2,1,0:T(8,128)S(1)}, u32[]{:S(2)}, u32[]{:S(2)}) collective-permute-start(f32[2,2,32,256]{3,2,1,0:T(8,128)S(1)} %get-tuple-element.71), channel_id=1, source_target_pairs={{0,24},{2,26},{4,28},{6,30},{8,0},{10,2},{12,4},{14,6},{16,8},{18,... | collective-permute-start | bytes 393224 | tf_op jit(solution)/shard_map/ppermute | solution.py:357
  (10 other events, 81.0 us)
where the time goes:
time: 148 us
  starting transfers between devices  55.6 us (38%)
  waiting for transfers between devices  47.5 us (32%)
  Pallas kernels  38.1 us (26%)
  local copies, waits for them, and re-layouts  3.01 us (2%)
  other arithmetic  1.82 us (1%)
  between operations  1.66 us (1%)
    ppermute x20, starting transfers between devices, across(): lax.ppermute(value, 'owner', [(source, source ^ bit) for source in range(...  31.9 us
    ppermute x20, waiting for transfers between devices, across(): lax.ppermute(value, 'owner', [(source, source ^ bit) for source in range(...  25.6 us
    ppermute x12, starting transfers between devices, along(): lax.ppermute(value, 'owner', [(source, (source + step) % count) for sourc...  22.8 us
    ppermute x12, waiting for transfers between devices, along(): lax.ppermute(value, 'owner', [(source, (source + step) % count) for sourc...  18.8 us
    pallas_call x6, Pallas kernels, forward(): pl.pallas_call(functools.partial(forward_kernel, groups, copies, len(fiel...  17.7 us
    pallas_call x4, Pallas kernels, backward(): pl.pallas_call(functools.partial(backward_kernel, first, groups, base), o...  15 us
    pallas_call x3, Pallas kernels, apply_tmat(): pl.pallas_call(tmat_kernel, out_shape=(half_shape, half_shape), in_specs=...  4.57 us
    ppermute x5, waiting for transfers between devices, from_other(): return lax.ppermute(value, 'pair', [(0, 1), (1, 0)])  3.05 us
  transfers between devices with their start and end apart: 37, of which 15 were waited for; matrix products, arithmetic and copies ran while one was open for 1% of the time, Pallas kernels for 22%

commit v1 on v0

--- a/solution.py
+++ b/solution.py
@@ -54,46 +54,101 @@
     return (column * particles + particle) * layers + layer
 
 
-def tmat_kernel(mine_ref, theirs_ref, tmat_ref, side_ref, exciting_ref, scattered_ref):
-    particles, _, directions, width = mine_ref.shape
+def prepare_kernel(layers, owner_ref, partners_ref, rows_of_ref, tmat_ref, *refs):
+    parts_ref, place_ref, group_ref, buf_ref, sems = refs
+    particles, _, half, width = tmat_ref.shape
+    slots = place_ref.shape[0]
+
+    def fetch(row):
+        return pltpu.make_async_copy(tmat_ref.at[row], buf_ref.at[row], sems.at[row])
+
+    for row in range(particles):
+        fetch(row).start()
+    me = owner_ref[0]
+    my_column, my_layer = lax.rem(me, COLUMNS), lax.div(me, COLUMNS)
+
+    def step(slot, carry):
+        row = rows_of_ref[partners_ref[me * slots + slot]]
+        owner, particle = lax.div(row, particles), lax.rem(row, particles)
+        column = lax.bitwise_xor(lax.rem(owner, COLUMNS), my_column)
+        layer = lax.rem(lax.div(owner, COLUMNS) - my_layer + layers, layers)
+        place_ref[slot] = place_of(column, particle, layer, particles, layers)
+        near = jnp.where(column == COLUMNS - 1, 2, 1)
+        far = jnp.where(column == COLUMNS - 1, 4, 3)
+        group_ref[slot] = jnp.where(column == 0, 0, jnp.where(layer == 0, near, far))
+        return carry
+
+    lax.fori_loop(0, slots, step, 0)
+    for row in range(particles):
+        fetch(row).wait()
+        for part in range(2):
+            high, low = split_value(buf_ref[row, part])
+            parts_ref[row, :, part * width : (part + 1) * width] = high
+            parts_ref[row, :, (2 + part) * width : (3 + part) * width] = low
+
+
+def prepare(my_owner, partners, owner_of, tmat, slots, layers):
+    particles, _, half, width = tmat.shape
+    index_shape = jax.ShapeDtypeStruct((slots,), jnp.int32)
+    return pl.pallas_call(
+        functools.partial(prepare_kernel, layers),
+        out_shape=(
+            jax.ShapeDtypeStruct((particles, half, 4 * width), BF16),
+            index_shape,
+            index_shape,
+        ),
+        in_specs=[SMEM, SMEM, SMEM, HBM],
+        out_specs=(VMEM, SMEM, SMEM),
+        scratch_shapes=[pltpu.VMEM(tmat.shape, F32), pltpu.SemaphoreType.DMA((particles,))],
+        compiler_params=params(3 * size_of(tmat)),
+        name="prepare",
+    )(my_owner, partners, owner_of, tmat)
+
+
+def tmat_kernel(halves, side_ref, mine_ref, theirs_ref, parts_ref, *refs):
+    exciting_ref = refs[0] if len(refs) == 3 else None
+    scattered_ref, full_ref = refs[-2:]
+    particles, _, directions, width = full_ref.shape
     half = width // 2
     start = pl.multiple_of(side_ref[0] * half, half)
+    if halves:
+        full_ref[:, :, :, pl.ds(start, half)] = mine_ref[...]
+        full_ref[:, :, :, pl.ds(pl.multiple_of(half - start, half), half)] = theirs_ref[...]
+    else:
+        full_ref[...] = mine_ref[...] + theirs_ref[...]
     for row in range(particles):
-        real = mine_ref[row, 0] + theirs_ref[row, 0]
-        imag = mine_ref[row, 1] + theirs_ref[row, 1]
-        with_real, with_imag = stacked_parts(real, imag)
-        real_high, real_low = split_value(tmat_ref[row, 0])
-        imag_high, imag_low = split_value(tmat_ref[row, 1])
-        left = jnp.concatenate((real_high, imag_high, real_low, imag_low), axis=1)
+        with_real, with_imag = stacked_parts(full_ref[row, 0], full_ref[row, 1])
         right = jnp.concatenate((with_real, with_imag, with_real, with_imag), axis=1)
-        total = dot_nt(left, right)
+        total = dot_nt(parts_ref[row], right)
         out = (total[:, : 2 * directions] + total[:, 2 * directions :]).T
         scattered_ref[row, 0] = out[:directions]
         scattered_ref[row, 1] = out[directions:]
-        for part in range(2):
-            window = (row, part, slice(None), pl.ds(start, half))
-            exciting_ref[row, part] = mine_ref[window] + theirs_ref[window]
-
-
-def apply_tmat(mine, theirs, tmat, side):
-    particles, _, directions, width = mine.shape
-    half_shape = jax.ShapeDtypeStruct((particles, 2, directions, width // 2), F32)
+    if exciting_ref is not None:
+        exciting_ref[...] = full_ref[:, :, :, pl.ds(start, half)]
+
+
+def apply_tmat(halves, last, side, mine, theirs, parts):
+    particles, _, directions, _ = mine.shape
+    half = parts.shape[1]
+    half_shape = jax.ShapeDtypeStruct((particles, 2, directions, half), F32)
+    count = 2 if last else 1
     return pl.pallas_call(
-        tmat_kernel,
-        out_shape=(half_shape, half_shape),
-        in_specs=[VMEM, VMEM, VMEM, SMEM],
-        out_specs=(VMEM, VMEM),
-        compiler_params=params(2 * size_of(mine, theirs, tmat)),
+        functools.partial(tmat_kernel, halves),
+        out_shape=[half_shape] * count,
+        in_specs=[SMEM, VMEM, VMEM, VMEM],
+        out_specs=[VMEM] * count,
+        scratch_shapes=[pltpu.VMEM((particles, 2, directions, 2 * half), F32)],
+        compiler_params=params(3 * size_of(mine, theirs), size_of(parts)),
         name="tmat_apply",
-    )(mine, theirs, tmat, side)
+    )(side, mine, theirs, parts)
 
 
 def chosen_slots(group_ref, alive, groups, list_ref):
+    mask = sum(1 << group for group in groups)
+
     def step(slot, found):
         list_ref[found] = slot
-        group = group_ref[slot]
-        wanted = jnp.logical_and(group >= groups[0], group <= groups[1])
-        return found + jnp.where(wanted, 1, 0)
+        return found + (lax.shift_right_logical(mask, group_ref[slot]) & 1)
 
     return lax.fori_loop(0, alive, step, 0)
 
@@ -211,8 +266,8 @@
         input_output_aliases=aliases,
         compiler_params=pltpu.CompilerParams(vmem_limit_bytes=STREAM_LIMIT),
         cost_estimate=pl.CostEstimate(
-            flops=slots * 24 * directions * width * half,
-            bytes_accessed=size_of(blocks) // 2,
+            flops=directions * width * half,
+            bytes_accessed=size_of(own_half),
             transcendentals=0,
         ),
         name="backward_group" + str(groups[0]),
@@ -283,8 +338,8 @@
         ],
         compiler_params=pltpu.CompilerParams(vmem_limit_bytes=STREAM_LIMIT),
         cost_estimate=pl.CostEstimate(
-            flops=slots * 16 * directions * width * half,
-            bytes_accessed=size_of(parts) // 3,
+            flops=directions * width * half,
+            bytes_accessed=size_of(out_shape),
             transcendentals=0,
         ),
         name="forward_group" + str(groups[0]),
@@ -367,75 +422,82 @@
     rest = range(1, layers)
     at = functools.partial(place_of, particles=particles, layers=layers)
     total_rows = COLUMNS * particles * layers
-    first_d = at(3, 0, 0)
+    first_n, first_d = at(1, 0, 0), at(3, 0, 0)
     first = parts is None
 
-    def diagonal(particle, layer):
-        return at(0, particle, layer)
+    def row_of(particle, layer):
+        return particle * layers + layer
 
     other = from_other(scattered)
     x1 = across(scattered, 1)
     y1 = across(scattered, 2)
     fetched = (side, scattered, other, blocks)
     products_d, *made = backward(
-        first, (2, 2), first_d, total_rows - first_d, index, *fetched, parts
+        first, (2, 4), first_d, total_rows - first_d, index, *fetched, parts
     )
     if first:
         parts = made[0]
 
-    inputs = [products_d, x1, y1, scattered]
-    x_plan = [[(0, diagonal(particle, layer))] for particle in by_x for layer in range(layers)]
-    y_plan = [[(0, diagonal(particle, layer))] for particle in by_y for layer in range(layers)]
+    inputs = [products_d, x1, y1]
+    x_plan = [[(0, row_of(particle, layer))] for particle in by_x for layer in range(layers)]
+    y_plan = [[(0, row_of(particle, layer))] for particle in by_y for layer in range(layers)]
     x_head, y_head = len(x_plan), len(y_plan)
     x_plan += [[(2, particle)] for particle in by_y]
     y_plan += [[(1, particle)] for particle in by_x]
-    x2, y2, copied = pack(
-        "pack_second", inputs, [x_plan, y_plan, [[(3, particle)] for particle in every]]
-    )
+    x2, y2 = pack("pack_second", inputs, [x_plan, y_plan])
     x2, y2 = across(x2, 1), across(y2, 2)
-    z2 = [along(copied, -shift) for shift in rest]
-    products, *made = backward(first, (0, 1), 0, first_d, index, *fetched, parts)
+    products_n, *made = backward(first, (1, 3), first_n, first_d - first_n, index, *fetched, parts)
     if first:
         parts = made[0]
 
-    inputs = [products, x2, y2]
+    inputs = [products_n, x2, y2, scattered]
     x_plan, y_plan = [], []
     for particle in every:
         for layer in range(layers):
-            x_terms = [(0, at(1, particle, layer))]
-            y_terms = [(0, at(2, particle, layer))]
+            x_terms = [(0, at(1, particle, layer) - first_n)]
+            y_terms = [(0, at(2, particle, layer) - first_n)]
             if particle in by_x:
-                y_terms.append((1, diagonal(particle, layer)))
+                y_terms.append((1, row_of(particle, layer)))
             else:
-                x_terms.append((2, diagonal(particle - len(by_x), layer)))
+                x_terms.append((2, row_of(particle - len(by_x), layer)))
             x_plan.append(x_terms)
             y_plan.append(y_terms)
-    x3, y3, mark = pack("pack_third", inputs, [x_plan, y_plan, [[(1, 0)]]])
+    x3, y3, copied = pack(
+        "pack_third", inputs, [x_plan, y_plan, [[(3, particle)] for particle in every]]
+    )
     x3, y3 = across(x3, 1), across(y3, 2)
-
-    fields = [x1, y1] + z2
+    z3 = [along(copied, -shift) for shift in rest]
+    products_o, *made = backward(
+        first, (0,), 0, first_n, index, side, copied, other, blocks, parts
+    )
+    if first:
+        parts = made[0]
+
+    inputs = [products_o, x3, y3] + z3
+    tails = [[(2 + shift, particle)] for particle in every for shift in rest]
+    z_plans = [
+        [
+            [(number, row_of(particle, shift)) for number in range(3)]
+            for particle in every
+        ]
+        for shift in rest
+    ]
+    x4, y4, mark, *z4 = pack("pack_fourth", inputs, [tails, tails, [[(1, 0)]]] + z_plans)
+    x4, y4 = across(x4, 1), across(y4, 2)
+    z4 = [along(value, shift) for shift, value in zip(rest, z4)]
     copies = []
     for particle in every:
         copies.append((0, particle, at(1, particle, 0)))
         copies.append((1, particle, at(2, particle, 0)))
+        if particle in by_x:
+            copies.append((3, y_head + particle, at(3, particle, 0)))
+        else:
+            copies.append((2, x_head + particle - len(by_x), at(3, particle, 0)))
         for shift in rest:
-            copies.append((1 + shift, particle, at(0, particle, shift)))
+            copies.append((3 + shift, particle, at(0, particle, shift)))
     near_first = forward(
-        (0, 0), index, fields, tuple(copies), parts, particles, total_rows, [mark]
-    )
-
-    inputs = [products, x3, y3] + z2
-    tails = [[(2 + shift, particle)] for particle in every for shift in rest]
-    z_plans = [
-        [
-            [(0, at(0, particle, shift)), (1, diagonal(particle, shift)), (2, diagonal(particle, shift))]
-            for particle in every
-        ]
-        for shift in rest
-    ]
-    x4, y4, *z4 = pack("pack_fourth", inputs, [tails, tails] + z_plans, [near_first])
-    x4, y4 = across(x4, 1), across(y4, 2)
-    z4 = [along(value, shift) for shift, value in zip(rest, z4)]
+        (0, 1, 2), index, [x1, y1, x2, y2] + z3, tuple(copies), parts, particles, total_rows, [mark]
+    )
 
     def tail(particle, shift):
         return particle * len(rest) + shift - 1
@@ -448,6 +510,7 @@
             [[(0, tail(particle, shift))] for particle in by_x for shift in rest],
             [[(0, 0)]],
         ],
+        [near_first],
     )
     x5, y5 = across(x5, 1), across(y5, 2)
     copies = []
@@ -456,54 +519,36 @@
             copies.append((0, tail(particle, shift), at(1, particle, shift)))
             copies.append((1, tail(particle, shift), at(2, particle, shift)))
     near_second = forward(
-        (1, 1), index, [x4, y4], tuple(copies), parts, particles, total_rows, [mark]
+        (3,), index, [x4, y4], tuple(copies), parts, particles, total_rows, [mark]
     )
     copies = []
-    for heads, ends, head, group in ((0, 2, x_head, by_y), (1, 3, y_head, by_x)):
+    for number, group in ((0, by_y), (1, by_x)):
         for order, particle in enumerate(group):
-            copies.append((heads, head + order, at(3, particle, 0)))
             for shift in rest:
-                copies.append((ends, tail(order, shift), at(3, particle, shift)))
+                copies.append((number, tail(order, shift), at(3, particle, shift)))
     near_last = forward(
-        (2, 2), index, [x2, y2, x5, y5], tuple(copies), parts, particles, total_rows, [near_second]
-    )
-    halves = [(products, layers), (x3, layers), (y3, layers)] + [(value, 1) for value in z4]
+        (4,), index, [x5, y5], tuple(copies), parts, particles, total_rows, [near_second]
+    )
+    halves = [(products_o, layers), (x3, layers), (y3, layers)] + [(value, 1) for value in z4]
     return whole_total(side, incident, [near_first, near_second, near_last], halves), parts
 
 
 def local(incident, tmat, blocks, block_rows, partners, live, owner_of):
-    particles = incident.shape[0]
     slots = blocks.shape[0]
     layers = lax.axis_size("owner") // COLUMNS
-    my_owner = lax.axis_index("owner").astype(jnp.int32)
-    side = lax.axis_index("pair").astype(jnp.int32)
-    my_partners = lax.dynamic_slice_in_dim(partners, my_owner * slots, slots)
-    ids = jnp.arange(owner_of.shape[0], dtype=jnp.int32)
-    partner_row = jnp.sum(
-        jnp.where(my_partners[:, None] == ids[None, :], owner_of[None, :], 0), axis=1
-    )
-    partner_owner = partner_row // particles
-    column = (partner_owner % COLUMNS) ^ (my_owner % COLUMNS)
-    layer = (partner_owner // COLUMNS - my_owner // COLUMNS) % layers
-    place = place_of(column, partner_row % particles, layer, particles, layers)
-    group = jnp.where(column == 3, 2, jnp.where((column == 0) | (layer == 0), 0, 1))
+    my_owner = lax.axis_index("owner").astype(jnp.int32)[None]
+    side = lax.axis_index("pair").astype(jnp.int32)[None]
+    theirs = from_other(incident)
+    tmat_parts, place, group = prepare(my_owner, partners, owner_of, tmat, slots, layers)
     index = (block_rows, live, place, group)
-    side_ref = side[None]
-
-    zero = jnp.zeros_like(incident)
-    mine = jnp.concatenate(
-        (jnp.where(side == 0, incident, zero), jnp.where(side == 1, incident, zero)), axis=3
-    )
-    theirs = from_other(mine)
-    exciting, scattered = apply_tmat(mine, theirs, tmat, side_ref)
+    (scattered,) = apply_tmat(True, False, side, incident, theirs, tmat_parts)
     parts = None
-    for _ in range(ITERS):
-        mine, parts = scatter_step(
-            incident, scattered, blocks, parts, index, side_ref, layers
-        )
+    for turn in range(ITERS):
+        mine, parts = scatter_step(incident, scattered, blocks, parts, index, side, layers)
         theirs = from_other(mine)
-        exciting, scattered = apply_tmat(mine, theirs, tmat, side_ref)
-    return (scattered, exciting)
+        last = turn == ITERS - 1
+        *exciting, scattered = apply_tmat(False, last, side, mine, theirs, tmat_parts)
+    return (scattered, exciting[0])
 
 
 def solution(mesh):

time: 148 us -> 132 us (0.89)
  waiting for transfers between devices: 47.5 us -> 25.5 us
  Pallas kernels: 38.1 us -> 58.4 us
  starting transfers between devices: 55.6 us -> 40.2 us
  other arithmetic: 1.82 us -> 0 us
    ppermute x20, waiting for transfers between devices: 25.6 us -> 12.8 us  [across(): lax.ppermute(value, 'owner', [(source, source ^ bit) for source in range(...]
    pallas_call x4 -> x6, Pallas kernels: 15 us -> 27.2 us  [backward(): pl.pallas_call(functools.partial(backward_kernel, first, groups, base), o...]
    ppermute x20, starting transfers between devices: 31.9 us -> 22.2 us  [across(): lax.ppermute(value, 'owner', [(source, source ^ bit) for source in range(...]
    ppermute x12, waiting for transfers between devices: 18.8 us -> 9.63 us  [along(): lax.ppermute(value, 'owner', [(source, (source + step) % count) for sourc...]
    pallas_call x6, Pallas kernels: 17.7 us -> 25.2 us  [forward(): pl.pallas_call(functools.partial(forward_kernel, groups, copies, len(fiel...]
    ppermute x12, starting transfers between devices: 22.8 us -> 17 us  [along(): lax.ppermute(value, 'owner', [(source, (source + step) % count) for sourc...]
    unnamed x10 -> x14, local copies, waits for them, and re-layouts: 2.26 us -> 4.48 us
    pallas_call x3 -> x4, Pallas kernels: 4.57 us -> 5.27 us  [the longest x3 3.29 us: apply_tmat(): pl.pallas_call(functools.partial(tmat_kernel, halves), out_shape=[half_sh...]
  transfers between devices with their start and end apart: 37 -> 37, of which waited for: 15 -> 15; matrix products, arithmetic and copies ran while one was open for 1% -> 0% of each run, Pallas kernels for 22% -> 42%
where the time goes in v1:
time: 132 us; the launch traced here: 130 us
  Pallas kernels  58.4 us (44%)
  starting transfers between devices  40.2 us (30%)
  waiting for transfers between devices  25.5 us (19%)
  local copies, waits for them, and re-layouts  4.48 us (3%)
  between operations  1.65 us (1%)
    pallas_call x6, Pallas kernels, backward(): pl.pallas_call(functools.partial(backward_kernel, first, groups, base), o...  27.2 us
    pallas_call x6, Pallas kernels, forward(): pl.pallas_call(functools.partial(forward_kernel, groups, copies, len(fiel...  25.2 us
    ppermute x20, starting transfers between devices, across(): lax.ppermute(value, 'owner', [(source, source ^ bit) for source in range(...  22.2 us
    ppermute x12, starting transfers between devices, along(): lax.ppermute(value, 'owner', [(source, (source + step) % count) for sourc...  17 us
    ppermute x20, waiting for transfers between devices, across(): lax.ppermute(value, 'owner', [(source, source ^ bit) for source in range(...  12.8 us
    ppermute x12, waiting for transfers between devices, along(): lax.ppermute(value, 'owner', [(source, (source + step) % count) for sourc...  9.63 us
    unnamed x14, local copies, waits for them, and re-layouts  4.48 us
    pallas_call x3, Pallas kernels, apply_tmat(): pl.pallas_call(functools.partial(tmat_kernel, halves), out_shape=[half_sh...  3.29 us
  transfers between devices with their start and end apart: 37, of which 15 were waited for; matrix products, arithmetic and copies ran while one was open for 0% of the time, Pallas kernels for 42%

profile of v1, /device:TPU:0, one launch (start us, length us, event | category | flops | bytes accessed | tf_op | source)
XLA Modules:
  0.0 130.2 jit_solution(5001338252426613595)
XLA Ops:
  1.2 1.6 %copy-done = f32[2,2,256,512]{3,2,1,0:T(8,128)S(1)} copy-done((f32[2,2,256,512]{3,2,1,0:T(8,128)S(1)}, f32[2,2,256,512]{3,2,1,0:T(8,128)}, u32[]{:S(2)}) %copy-start) | copy-done | bytes 2097176
  4.1 2.0 %prepare.1 = (bf16[2,256,2048]{2,1,0:T(8,128)(2,1)S(1)}, s32[21]{0:T(128)S(1)}, s32[21]{0:T(128)S(1)}) custom-call(s32[1]{0:T(128)} %bitcast.1.owner_ref, s32[336]{0:T(512)S(1)} %copy-done.5, s32[32]{0:T(128)S(1)} %copy-done.6, f32[2,2,256,512]{3,2,1,0:T(8,128)S(1)} %copy-done), custom_call_target="tpu_custom_call" | custom-call | tf_op jit(solution)/shard_map/prepare/pallas_call | solution.py:93
  8.0 2.9 %collective-permute-start.1 = (f32[2,2,32,256]{3,2,1,0:T(8,128)S(1)}, f32[2,2,32,256]{3,2,1,0:T(8,128)S(1)}, u32[]{:S(2)}, u32[]{:S(2)}) collective-permute-start(f32[2,2,32,256]{3,2,1,0:T(8,128)S(1)} %tmat_apply.3.refs_0_.refs_3_), channel_id=1, source_target_pairs={{0,2},{2,0},{4,6},{6,4},{8,10},{10,8},{12,14},{14,12},{16,18},{18,... | collective-permute-start | bytes 393224 | tf_op jit(solution)/shard_map/ppermute | solution.py:406
  13.8 4.7 %backward_group2.2 = (f32[8,2,32,256]{3,2,1,0:T(8,128)S(1)}, bf16[21,2,2,512,256]{4,3,2,1,0:T(8,128)(2,1)}) custom-call(s32[21]{0:T(128)S(1)} %copy-done.3, s32[1]{0:T(128)S(6)} %copy.13.live_ref, s32[21]{0:T(128)S(1)} %get-tuple-element.41.place_ref, s32[21]{0:T(128)S(1)} %get-tuple-element.42.group_ref, s32[1]{0:T(128)} %bitcast.side_ref, ...), custom_call_target="tpu_custom_call" | custom-call | flops 4194304 | bytes 131072 | tf_op jit(solution)/shard_map/backward_group2/pallas_call | solution.py:260
  18.7 6.1 %backward_group1.2 = (f32[16,2,32,256]{3,2,1,0:T(8,128)S(1)}, bf16[21,2,2,512,256]{4,3,2,1,0:T(8,128)(2,1)}) custom-call(s32[21]{0:T(128)S(1)} %copy-done.3, s32[1]{0:T(128)S(6)} %copy.13.live_ref, s32[21]{0:T(128)S(1)} %get-tuple-element.41.place_ref, s32[21]{0:T(128)S(1)} %get-tuple-element.42.group_ref, ...), custom_call_target="tpu_custom_call", output_to_operand_aliasing={{1}: (8, {})} | custom-call | flops 4194304 | bytes 131072 | tf_op jit(solution)/shard_map/backward_group1/pallas_call | solution.py:260
  24.8 2.9 %collective-permute-done.4.refs_1_.refs_2_ = f32[5,2,32,256]{3,2,1,0:T(8,128)S(1)} collective-permute-done((f32[5,2,32,256]{3,2,1,0:T(8,128)S(1)}, f32[5,2,32,256]{3,2,1,0:T(8,128)S(1)}, u32[]{:S(2)}, u32[]{:S(2)}) %collective-permute-start.4) | collective-permute-done | bytes 327712 | tf_op jit(solution)/shard_map/ppermute | solution.py:406
  28.3 1.6 %collective-permute-start.9 = (f32[8,2,32,256]{3,2,1,0:T(8,128)S(1)}, f32[8,2,32,256]{3,2,1,0:T(8,128)S(1)}, u32[]{:S(2)}, u32[]{:S(2)}) collective-permute-start(f32[8,2,32,256]{3,2,1,0:T(8,128)S(1)} %get-tuple-element.53), channel_id=1, source_target_pairs={{0,2},{2,0},{4,6},{6,4},{8,10},{10,8},{12,14},{14,12},{16,18},{18,... | collective-permute-start | bytes 1572872 | tf_op jit(solution)/shard_map/ppermute | solution.py:406
  29.9 3.3 %collective-permute-start.6 = (f32[2,2,32,256]{3,2,1,0:T(8,128)S(1)}, f32[2,2,32,256]{3,2,1,0:T(8,128)S(1)}, u32[]{:S(2)}, u32[]{:S(2)}) collective-permute-start(f32[2,2,32,256]{3,2,1,0:T(8,128)S(1)} %get-tuple-element.49.refs_0_), channel_id=1, source_target_pairs={{0,24},{2,26},{4,28},{6,30},{8,0},{10,2},{12,4},{14,6},{16,8},{18,... | collective-permute-start | bytes 393224 | tf_op jit(solution)/shard_map/ppermute | solution.py:412
  34.7 5.4 %backward_group0.2 = (f32[8,2,32,256]{3,2,1,0:T(8,128)S(1)}, bf16[21,2,2,512,256]{4,3,2,1,0:T(8,128)(2,1)}) custom-call(s32[21]{0:T(128)S(1)} %copy-done.3, s32[1]{0:T(128)S(6)} %copy.13.live_ref, s32[21]{0:T(128)S(1)} %get-tuple-element.41.place_ref, s32[21]{0:T(128)S(1)} %get-tuple-element.42.group_ref, ...), custom_call_target="tpu_custom_call", output_to_operand_aliasing={{1}: (8, {})} | custom-call | flops 4194304 | bytes 131072 | tf_op jit(solution)/shard_map/backward_group0/pallas_call | solution.py:260
  40.2 3.5 %collective-permute-done.7.refs_4_.refs_5_ = f32[2,2,32,256]{3,2,1,0:T(8,128)S(1)} collective-permute-done((f32[2,2,32,256]{3,2,1,0:T(8,128)S(1)}, f32[2,2,32,256]{3,2,1,0:T(8,128)S(1)}, u32[]{:S(2)}, u32[]{:S(2)}) %collective-permute-start.7) | collective-permute-done | bytes 131104 | tf_op jit(solution)/shard_map/ppermute | solution.py:412
  46.3 5.6 %forward_group0.2.refs_2_.refs_0_ = f32[2,2,32,512]{3,2,1,0:T(8,128)S(1)} custom-call(s32[21]{0:T(128)S(1)} %copy-done.4, s32[1]{0:T(128)S(6)} %copy.13.live_ref, s32[21]{0:T(128)S(1)} %get-tuple-element.41.place_ref, s32[21]{0:T(128)S(1)} %get-tuple-element.42.group_ref, f32[2,2,32,256]{3,2,1,0:T(8,128)S(1)} %collective-permute-done.1.refs_1_.refs_0_, ...), custom_call_target="tpu_custom_call" | custom-call | flops 4194304 | bytes 262144 | tf_op jit(solution)/shard_map/forward_group0/pallas_call | solution.py:327
  55.2 1.7 %collective-permute-start.14 = (f32[3,2,32,256]{3,2,1,0:T(8,128)S(1)}, f32[3,2,32,256]{3,2,1,0:T(8,128)S(1)}, u32[]{:S(2)}, u32[]{:S(2)}) collective-permute-start(f32[3,2,32,256]{3,2,1,0:T(8,128)S(1)} %get-tuple-element.60), channel_id=1, source_target_pairs={{0,4},{2,6},{4,0},{6,2},{8,12},{10,14},{12,8},{14,10},{16,20},{18,... | collective-permute-start | bytes 589832 | tf_op jit(solution)/shard_map/ppermute | solution.py:406
  57.0 1.9 %collective-permute-start.16 = (f32[2,2,32,256]{3,2,1,0:T(8,128)S(1)}, f32[2,2,32,256]{3,2,1,0:T(8,128)S(1)}, u32[]{:S(2)}, u32[]{:S(2)}) collective-permute-start(f32[2,2,32,256]{3,2,1,0:T(8,128)S(1)} %get-tuple-element.62), channel_id=1, source_target_pairs={{0,16},{2,18},{4,20},{6,22},{8,24},{10,26},{12,28},{14,30},{16,0},... | collective-permute-start | bytes 393224 | tf_op jit(solution)/shard_map/ppermute | solution.py:412
  58.9 2.9 %collective-permute-start.17 = (f32[2,2,32,256]{3,2,1,0:T(8,128)S(1)}, f32[2,2,32,256]{3,2,1,0:T(8,128)S(1)}, u32[]{:S(2)}, u32[]{:S(2)}) collective-permute-start(f32[2,2,32,256]{3,2,1,0:T(8,128)S(1)} %get-tuple-element.63), channel_id=1, source_target_pairs={{0,24},{2,26},{4,28},{6,30},{8,0},{10,2},{12,4},{14,6},{16,8},{18,... | collective-permute-start | bytes 393224 | tf_op jit(solution)/shard_map/ppermute | solution.py:412
  61.8 3.7 %forward_group3.2.refs_3_.refs_1_ = f32[2,2,32,512]{3,2,1,0:T(8,128)S(1)} custom-call(s32[21]{0:T(128)S(1)} %copy-done.4, s32[1]{0:T(128)S(6)} %copy.13.live_ref, s32[21]{0:T(128)S(1)} %get-tuple-element.41.place_ref, s32[21]{0:T(128)S(1)} %get-tuple-element.42.group_ref, f32[6,2,32,256]{3,2,1,0:T(8,128)S(1)} %collective-permute-done.11.refs_0_, ...), custom_call_target="tpu_custom_call" | custom-call | flops 4194304 | bytes 262144 | tf_op jit(solution)/shard_map/forward_group3/pallas_call | solution.py:327
  65.6 3.3 %forward_group4.2.refs_2_ = f32[2,2,32,512]{3,2,1,0:T(8,128)S(1)} custom-call(s32[21]{0:T(128)S(1)} %copy-done.4, s32[1]{0:T(128)S(6)} %copy.13.live_ref, s32[21]{0:T(128)S(1)} %get-tuple-element.41.place_ref, s32[21]{0:T(128)S(1)} %get-tuple-element.42.group_ref, f32[3,2,32,256]{3,2,1,0:T(8,128)S(1)} %collective-permute-done.13.refs_0_, ...), custom_call_target="tpu_custom_call" | custom-call | flops 4194304 | bytes 262144 | tf_op jit(solution)/shard_map/forward_group4/pallas_call | solution.py:327
  69.1 1.5 %collective-permute-done.18.theirs_ref = f32[2,2,32,512]{3,2,1,0:T(8,128)S(1)} collective-permute-done((f32[2,2,32,512]{3,2,1,0:T(8,128)S(1)}, f32[2,2,32,512]{3,2,1,0:T(8,128)S(1)}, u32[]{:S(2)}, u32[]{:S(2)}) %collective-permute-start.18) | collective-permute-done | bytes 262176 | tf_op jit(solution)/shard_map/ppermute | solution.py:401
  72.1 2.0 %collective-permute-start.20 = (f32[2,2,32,256]{3,2,1,0:T(8,128)S(1)}, f32[2,2,32,256]{3,2,1,0:T(8,128)S(1)}, u32[]{:S(2)}, u32[]{:S(2)}) collective-permute-start(f32[2,2,32,256]{3,2,1,0:T(8,128)S(1)} %tmat_apply.4.refs_0_.refs_3_), channel_id=1, source_target_pairs={{0,4},{2,6},{4,0},{6,2},{8,12},{10,14},{12,8},{14,10},{16,20},{18,... | collective-permute-start | bytes 393224 | tf_op jit(solution)/shard_map/ppermute | solution.py:406
  74.1 3.2 %backward_group2.3.refs_0_ = f32[8,2,32,256]{3,2,1,0:T(8,128)S(1)} custom-call(s32[21]{0:T(128)S(1)} %copy-done.4, s32[1]{0:T(128)S(6)} %copy.13.live_ref, s32[21]{0:T(128)S(1)} %get-tuple-element.41.place_ref, s32[21]{0:T(128)S(1)} %get-tuple-element.42.group_ref, s32[1]{0:T(128)} %bitcast.side_ref, f32[2,2,32,256]{3,2,1,0:T(8,128)S(1)} %tmat_apply.4.refs_0_.refs_3_, ...), custom_call_target="tpu_custom_call" | custom-call | flops 4194304 | bytes 131072 | tf_op jit(solution)/shard_map/backward_group2/pallas_call | solution.py:260
  80.0 4.1 %backward_group1.3.refs_0_ = f32[16,2,32,256]{3,2,1,0:T(8,128)S(1)} custom-call(s32[21]{0:T(128)S(1)} %copy-done.4, s32[1]{0:T(128)S(6)} %copy.13.live_ref, s32[21]{0:T(128)S(1)} %get-tuple-element.41.place_ref, s32[21]{0:T(128)S(1)} %get-tuple-element.42.group_ref, s32[1]{0:T(128)} %bitcast.side_ref, f32[2,2,32,256]{3,2,1,0:T(8,128)S(1)} %tmat_apply.4.refs_0_.refs_3_, ...), custom_call_target="tpu_custom_call" | custom-call | flops 4194304 | bytes 131072 | tf_op jit(solution)/shard_map/backward_group1/pallas_call | solution.py:260
  84.1 3.1 %collective-permute-done.22.refs_1_.refs_2_ = f32[5,2,32,256]{3,2,1,0:T(8,128)S(1)} collective-permute-done((f32[5,2,32,256]{3,2,1,0:T(8,128)S(1)}, f32[5,2,32,256]{3,2,1,0:T(8,128)S(1)}, u32[]{:S(2)}, u32[]{:S(2)}) %collective-permute-start.22) | collective-permute-done | bytes 327712 | tf_op jit(solution)/shard_map/ppermute | solution.py:406
  90.5 1.6 %collective-permute-start.24 = (f32[2,2,32,256]{3,2,1,0:T(8,128)S(1)}, f32[2,2,32,256]{3,2,1,0:T(8,128)S(1)}, u32[]{:S(2)}, u32[]{:S(2)}) collective-permute-start(f32[2,2,32,256]{3,2,1,0:T(8,128)S(1)} %get-tuple-element.66.refs_0_), channel_id=1, source_target_pairs={{0,24},{2,26},{4,28},{6,30},{8,0},{10,2},{12,4},{14,6},{16,8},{18,... | collective-permute-start | bytes 393224 | tf_op jit(solution)/shard_map/ppermute | solution.py:412
  92.6 3.8 %backward_group0.3.refs_0_.refs_3_ = f32[8,2,32,256]{3,2,1,0:T(8,128)S(1)} custom-call(s32[21]{0:T(128)S(1)} %copy-done.4, s32[1]{0:T(128)S(6)} %copy.13.live_ref, s32[21]{0:T(128)S(1)} %get-tuple-element.41.place_ref, s32[21]{0:T(128)S(1)} %get-tuple-element.42.group_ref, s32[1]{0:T(128)} %bitcast.side_ref, ...), custom_call_target="tpu_custom_call" | custom-call | flops 4194304 | bytes 131072 | tf_op jit(solution)/shard_map/backward_group0/pallas_call | solution.py:260
  97.4 5.0 %collective-permute-done.25.refs_4_.refs_5_ = f32[2,2,32,256]{3,2,1,0:T(8,128)S(1)} collective-permute-done((f32[2,2,32,256]{3,2,1,0:T(8,128)S(1)}, f32[2,2,32,256]{3,2,1,0:T(8,128)S(1)}, u32[]{:S(2)}, u32[]{:S(2)}) %collective-permute-start.25) | collective-permute-done | bytes 131104 | tf_op jit(solution)/shard_map/ppermute | solution.py:412
  104.3 5.6 %forward_group0.3.refs_2_.refs_0_ = f32[2,2,32,512]{3,2,1,0:T(8,128)S(1)} custom-call(s32[21]{0:T(128)S(1)} %copy-done.4, s32[1]{0:T(128)S(6)} %copy.13.live_ref, s32[21]{0:T(128)S(1)} %get-tuple-element.41.place_ref, s32[21]{0:T(128)S(1)} %get-tuple-element.42.group_ref, f32[2,2,32,256]{3,2,1,0:T(8,128)S(1)} %collective-permute-done.19.refs_1_.refs_0_, ...), custom_call_target="tpu_custom_call" | custom-call | flops 4194304 | bytes 262144 | tf_op jit(solution)/shard_map/forward_group0/pallas_call | solution.py:327
  109.9 2.2 %collective-permute-done.29.refs_0_ = f32[6,2,32,256]{3,2,1,0:T(8,128)S(1)} collective-permute-done((f32[6,2,32,256]{3,2,1,0:T(8,128)S(1)}, f32[6,2,32,256]{3,2,1,0:T(8,128)S(1)}, u32[]{:S(2)}, u32[]{:S(2)}) %collective-permute-start.29) | collective-permute-done | bytes 393248 | tf_op jit(solution)/shard_map/ppermute | solution.py:406
  115.0 1.9 %collective-permute-start.34 = (f32[2,2,32,256]{3,2,1,0:T(8,128)S(1)}, f32[2,2,32,256]{3,2,1,0:T(8,128)S(1)}, u32[]{:S(2)}, u32[]{:S(2)}) collective-permute-start(f32[2,2,32,256]{3,2,1,0:T(8,128)S(1)} %get-tuple-element.76), channel_id=1, source_target_pairs={{0,16},{2,18},{4,20},{6,22},{8,24},{10,26},{12,28},{14,30},{16,0},... | collective-permute-start | bytes 393224 | tf_op jit(solution)/shard_map/ppermute | solution.py:412
  116.9 2.9 %collective-permute-start.35 = (f32[2,2,32,256]{3,2,1,0:T(8,128)S(1)}, f32[2,2,32,256]{3,2,1,0:T(8,128)S(1)}, u32[]{:S(2)}, u32[]{:S(2)}) collective-permute-start(f32[2,2,32,256]{3,2,1,0:T(8,128)S(1)} %get-tuple-element.77), channel_id=1, source_target_pairs={{0,24},{2,26},{4,28},{6,30},{8,0},{10,2},{12,4},{14,6},{16,8},{18,... | collective-permute-start | bytes 393224 | tf_op jit(solution)/shard_map/ppermute | solution.py:412
  119.8 3.7 %forward_group3.3.refs_3_.refs_1_ = f32[2,2,32,512]{3,2,1,0:T(8,128)S(1)} custom-call(s32[21]{0:T(128)S(1)} %copy-done.4, s32[1]{0:T(128)S(6)} %copy.13.live_ref, s32[21]{0:T(128)S(1)} %get-tuple-element.41.place_ref, s32[21]{0:T(128)S(1)} %get-tuple-element.42.group_ref, f32[6,2,32,256]{3,2,1,0:T(8,128)S(1)} %collective-permute-done.29.refs_0_, ...), custom_call_target="tpu_custom_call" | custom-call | flops 4194304 | bytes 262144 | tf_op jit(solution)/shard_map/forward_group3/pallas_call | solution.py:327
  123.6 3.3 %forward_group4.3.refs_2_ = f32[2,2,32,512]{3,2,1,0:T(8,128)S(1)} custom-call(s32[21]{0:T(128)S(1)} %copy-done.4, s32[1]{0:T(128)S(6)} %copy.13.live_ref, s32[21]{0:T(128)S(1)} %get-tuple-element.41.place_ref, s32[21]{0:T(128)S(1)} %get-tuple-element.42.group_ref, f32[3,2,32,256]{3,2,1,0:T(8,128)S(1)} %collective-permute-done.31.refs_0_, ...), custom_call_target="tpu_custom_call" | custom-call | flops 4194304 | bytes 262144 | tf_op jit(solution)/shard_map/forward_group4/pallas_call | solution.py:327
  127.1 1.5 %collective-permute-done.36.theirs_ref = f32[2,2,32,512]{3,2,1,0:T(8,128)S(1)} collective-permute-done((f32[2,2,32,512]{3,2,1,0:T(8,128)S(1)}, f32[2,2,32,512]{3,2,1,0:T(8,128)S(1)}, u32[]{:S(2)}, u32[]{:S(2)}) %collective-permute-start.36) | collective-permute-done | bytes 262176 | tf_op jit(solution)/shard_map/ppermute | solution.py:401
  128.6 1.5 %tmat_apply.5 = (f32[2,2,32,256]{3,2,1,0:T(8,128)}, f32[2,2,32,256]{3,2,1,0:T(8,128)}) custom-call(s32[1]{0:T(128)} %bitcast.side_ref, f32[2,2,32,512]{3,2,1,0:T(8,128)S(1)} %total.3.mine_ref, f32[2,2,32,512]{3,2,1,0:T(8,128)S(1)} %collective-permute-done.36.theirs_ref, bf16[2,256,2048]{2,1,0:T(8,128)(2,1)S(1)} %get-tuple-element.43.parts_ref), custom_call_target="tpu_custom_call" | custom-call | tf_op jit(solution)/shard_map/tmat_apply/pallas_call | solution.py:135
  (82 shorter events, 28.6 us)
Async XLA Ops:
  8.0 10.5 %collective-permute-start.1 = (f32[2,2,32,256]{3,2,1,0:T(8,128)S(1)}, f32[2,2,32,256]{3,2,1,0:T(8,128)S(1)}, u32[]{:S(2)}, u32[]{:S(2)}) collective-permute-start(f32[2,2,32,256]{3,2,1,0:T(8,128)S(1)} %tmat_apply.3.refs_0_.refs_3_), channel_id=1, source_target_pairs={{0,2},{2,0},{4,6},{6,4},{8,10},{10,8},{12,14},{14,12},{16,18},{18,... | collective-permute-start | bytes 393224 | tf_op jit(solution)/shard_map/ppermute | solution.py:406
  10.9 7.5 %collective-permute-start.2 = (f32[2,2,32,256]{3,2,1,0:T(8,128)S(1)}, f32[2,2,32,256]{3,2,1,0:T(8,128)S(1)}, u32[]{:S(2)}, u32[]{:S(2)}) collective-permute-start(f32[2,2,32,256]{3,2,1,0:T(8,128)S(1)} %tmat_apply.3.refs_0_.refs_3_), channel_id=1, source_target_pairs={{0,4},{2,6},{4,0},{6,2},{8,12},{10,14},{12,8},{14,10},{16,20},{18,... | collective-permute-start | bytes 393224 | tf_op jit(solution)/shard_map/ppermute | solution.py:406
  18.5 9.2 %collective-permute-start.4 = (f32[5,2,32,256]{3,2,1,0:T(8,128)S(1)}, f32[5,2,32,256]{3,2,1,0:T(8,128)S(1)}, u32[]{:S(2)}, u32[]{:S(2)}) collective-permute-start(f32[5,2,32,256]{3,2,1,0:T(8,128)S(1)} %get-tuple-element.45), channel_id=1, source_target_pairs={{0,2},{2,0},{4,6},{6,4},{8,10},{10,8},{12,14},{14,12},{16,18},{18,... | collective-permute-start | bytes 983048 | tf_op jit(solution)/shard_map/ppermute | solution.py:406
  18.6 9.2 %collective-permute-start.5 = (f32[5,2,32,256]{3,2,1,0:T(8,128)S(1)}, f32[5,2,32,256]{3,2,1,0:T(8,128)S(1)}, u32[]{:S(2)}, u32[]{:S(2)}) collective-permute-start(f32[5,2,32,256]{3,2,1,0:T(8,128)S(1)} %get-tuple-element.46), channel_id=1, source_target_pairs={{0,4},{2,6},{4,0},{6,2},{8,12},{10,14},{12,8},{14,10},{16,20},{18,... | collective-permute-start | bytes 983048 | tf_op jit(solution)/shard_map/ppermute | solution.py:406
  27.9 15.8 %collective-permute-start.10 = (f32[8,2,32,256]{3,2,1,0:T(8,128)S(1)}, f32[8,2,32,256]{3,2,1,0:T(8,128)S(1)}, u32[]{:S(2)}, u32[]{:S(2)}) collective-permute-start(f32[8,2,32,256]{3,2,1,0:T(8,128)S(1)} %get-tuple-element.54), channel_id=1, source_target_pairs={{0,4},{2,6},{4,0},{6,2},{8,12},{10,14},{12,8},{14,10},{16,20},{18,... | collective-permute-start | bytes 1572872 | tf_op jit(solution)/shard_map/ppermute | solution.py:406
  28.3 15.4 %collective-permute-start.9 = (f32[8,2,32,256]{3,2,1,0:T(8,128)S(1)}, f32[8,2,32,256]{3,2,1,0:T(8,128)S(1)}, u32[]{:S(2)}, u32[]{:S(2)}) collective-permute-start(f32[8,2,32,256]{3,2,1,0:T(8,128)S(1)} %get-tuple-element.53), channel_id=1, source_target_pairs={{0,2},{2,0},{4,6},{6,4},{8,10},{10,8},{12,14},{14,12},{16,18},{18,... | collective-permute-start | bytes 1572872 | tf_op jit(solution)/shard_map/ppermute | solution.py:406
  29.9 10.3 %collective-permute-start.6 = (f32[2,2,32,256]{3,2,1,0:T(8,128)S(1)}, f32[2,2,32,256]{3,2,1,0:T(8,128)S(1)}, u32[]{:S(2)}, u32[]{:S(2)}) collective-permute-start(f32[2,2,32,256]{3,2,1,0:T(8,128)S(1)} %get-tuple-element.49.refs_0_), channel_id=1, source_target_pairs={{0,24},{2,26},{4,28},{6,30},{8,0},{10,2},{12,4},{14,6},{16,8},{18,... | collective-permute-start | bytes 393224 | tf_op jit(solution)/shard_map/ppermute | solution.py:412
  33.2 10.6 %collective-permute-start.7 = (f32[2,2,32,256]{3,2,1,0:T(8,128)S(1)}, f32[2,2,32,256]{3,2,1,0:T(8,128)S(1)}, u32[]{:S(2)}, u32[]{:S(2)}) collective-permute-start(f32[2,2,32,256]{3,2,1,0:T(8,128)S(1)} %get-tuple-element.49.refs_0_), channel_id=1, source_target_pairs={{0,16},{2,18},{4,20},{6,22},{8,24},{10,26},{12,28},{14,30},{16,0},... | collective-permute-start | bytes 393224 | tf_op jit(solution)/shard_map/ppermute | solution.py:412
  33.3 10.5 %collective-permute-start.8 = (f32[2,2,32,256]{3,2,1,0:T(8,128)S(1)}, f32[2,2,32,256]{3,2,1,0:T(8,128)S(1)}, u32[]{:S(2)}, u32[]{:S(2)}) collective-permute-start(f32[2,2,32,256]{3,2,1,0:T(8,128)S(1)} %get-tuple-element.49.refs_0_), channel_id=1, source_target_pairs={{0,8},{2,10},{4,12},{6,14},{8,16},{10,18},{12,20},{14,22},{16,24},... | collective-permute-start | bytes 393224 | tf_op jit(solution)/shard_map/ppermute | solution.py:412
  43.9 9.5 %collective-permute-start.11 = (f32[6,2,32,256]{3,2,1,0:T(8,128)S(1)}, f32[6,2,32,256]{3,2,1,0:T(8,128)S(1)}, u32[]{:S(2)}, u32[]{:S(2)}) collective-permute-start(f32[6,2,32,256]{3,2,1,0:T(8,128)S(1)} %get-tuple-element.56), channel_id=1, source_target_pairs={{0,2},{2,0},{4,6},{6,4},{8,10},{10,8},{12,14},{14,12},{16,18},{18,... | collective-permute-start | bytes 1179656 | tf_op jit(solution)/shard_map/ppermute | solution.py:406
  45.2 9.3 %collective-permute-start.12 = (f32[6,2,32,256]{3,2,1,0:T(8,128)S(1)}, f32[6,2,32,256]{3,2,1,0:T(8,128)S(1)}, u32[]{:S(2)}, u32[]{:S(2)}) collective-permute-start(f32[6,2,32,256]{3,2,1,0:T(8,128)S(1)} %get-tuple-element.57), channel_id=1, source_target_pairs={{0,4},{2,6},{4,0},{6,2},{8,12},{10,14},{12,8},{14,10},{16,20},{18,... | collective-permute-start | bytes 1179656 | tf_op jit(solution)/shard_map/ppermute | solution.py:406
  54.5 11.1 %collective-permute-start.13 = (f32[3,2,32,256]{3,2,1,0:T(8,128)S(1)}, f32[3,2,32,256]{3,2,1,0:T(8,128)S(1)}, u32[]{:S(2)}, u32[]{:S(2)}) collective-permute-start(f32[3,2,32,256]{3,2,1,0:T(8,128)S(1)} %get-tuple-element.59), channel_id=1, source_target_pairs={{0,2},{2,0},{4,6},{6,4},{8,10},{10,8},{12,14},{14,12},{16,18},{18,... | collective-permute-start | bytes 589832 | tf_op jit(solution)/shard_map/ppermute | solution.py:406
  55.2 10.4 %collective-permute-start.14 = (f32[3,2,32,256]{3,2,1,0:T(8,128)S(1)}, f32[3,2,32,256]{3,2,1,0:T(8,128)S(1)}, u32[]{:S(2)}, u32[]{:S(2)}) collective-permute-start(f32[3,2,32,256]{3,2,1,0:T(8,128)S(1)} %get-tuple-element.60), channel_id=1, source_target_pairs={{0,4},{2,6},{4,0},{6,2},{8,12},{10,14},{12,8},{14,10},{16,20},{18,... | collective-permute-start | bytes 589832 | tf_op jit(solution)/shard_map/ppermute | solution.py:406
  56.9 12.0 %collective-permute-start.15 = (f32[2,2,32,256]{3,2,1,0:T(8,128)S(1)}, f32[2,2,32,256]{3,2,1,0:T(8,128)S(1)}, u32[]{:S(2)}, u32[]{:S(2)}) collective-permute-start(f32[2,2,32,256]{3,2,1,0:T(8,128)S(1)} %get-tuple-element.61), channel_id=1, source_target_pairs={{0,8},{2,10},{4,12},{6,14},{8,16},{10,18},{12,20},{14,22},{16,24},... | collective-permute-start | bytes 393224 | tf_op jit(solution)/shard_map/ppermute | solution.py:412
  57.0 11.9 %collective-permute-start.16 = (f32[2,2,32,256]{3,2,1,0:T(8,128)S(1)}, f32[2,2,32,256]{3,2,1,0:T(8,128)S(1)}, u32[]{:S(2)}, u32[]{:S(2)}) collective-permute-start(f32[2,2,32,256]{3,2,1,0:T(8,128)S(1)} %get-tuple-element.62), channel_id=1, source_target_pairs={{0,16},{2,18},{4,20},{6,22},{8,24},{10,26},{12,28},{14,30},{16,0},... | collective-permute-start | bytes 393224 | tf_op jit(solution)/shard_map/ppermute | solution.py:412
  58.9 10.0 %collective-permute-start.17 = (f32[2,2,32,256]{3,2,1,0:T(8,128)S(1)}, f32[2,2,32,256]{3,2,1,0:T(8,128)S(1)}, u32[]{:S(2)}, u32[]{:S(2)}) collective-permute-start(f32[2,2,32,256]{3,2,1,0:T(8,128)S(1)} %get-tuple-element.63), channel_id=1, source_target_pairs={{0,24},{2,26},{4,28},{6,30},{8,0},{10,2},{12,4},{14,6},{16,8},{18,... | collective-permute-start | bytes 393224 | tf_op jit(solution)/shard_map/ppermute | solution.py:412
  71.7 5.8 %collective-permute-start.19 = (f32[2,2,32,256]{3,2,1,0:T(8,128)S(1)}, f32[2,2,32,256]{3,2,1,0:T(8,128)S(1)}, u32[]{:S(2)}, u32[]{:S(2)}) collective-permute-start(f32[2,2,32,256]{3,2,1,0:T(8,128)S(1)} %tmat_apply.4.refs_0_.refs_3_), channel_id=1, source_target_pairs={{0,2},{2,0},{4,6},{6,4},{8,10},{10,8},{12,14},{14,12},{16,18},{18,... | collective-permute-start | bytes 393224 | tf_op jit(solution)/shard_map/ppermute | solution.py:406
  72.1 5.8 %collective-permute-start.20 = (f32[2,2,32,256]{3,2,1,0:T(8,128)S(1)}, f32[2,2,32,256]{3,2,1,0:T(8,128)S(1)}, u32[]{:S(2)}, u32[]{:S(2)}) collective-permute-start(f32[2,2,32,256]{3,2,1,0:T(8,128)S(1)} %tmat_apply.4.refs_0_.refs_3_), channel_id=1, source_target_pairs={{0,4},{2,6},{4,0},{6,2},{8,12},{10,14},{12,8},{14,10},{16,20},{18,... | collective-permute-start | bytes 393224 | tf_op jit(solution)/shard_map/ppermute | solution.py:406
  77.9 9.2 %collective-permute-start.22 = (f32[5,2,32,256]{3,2,1,0:T(8,128)S(1)}, f32[5,2,32,256]{3,2,1,0:T(8,128)S(1)}, u32[]{:S(2)}, u32[]{:S(2)}) collective-permute-start(f32[5,2,32,256]{3,2,1,0:T(8,128)S(1)} %get-tuple-element.64), channel_id=1, source_target_pairs={{0,2},{2,0},{4,6},{6,4},{8,10},{10,8},{12,14},{14,12},{16,18},{18,... | collective-permute-start | bytes 983048 | tf_op jit(solution)/shard_map/ppermute | solution.py:406
  79.3 8.6 %collective-permute-start.23 = (f32[5,2,32,256]{3,2,1,0:T(8,128)S(1)}, f32[5,2,32,256]{3,2,1,0:T(8,128)S(1)}, u32[]{:S(2)}, u32[]{:S(2)}) collective-permute-start(f32[5,2,32,256]{3,2,1,0:T(8,128)S(1)} %get-tuple-element.65), channel_id=1, source_target_pairs={{0,4},{2,6},{4,0},{6,2},{8,12},{10,14},{12,8},{14,10},{16,20},{18,... | collective-permute-start | bytes 983048 | tf_op jit(solution)/shard_map/ppermute | solution.py:406
  88.0 14.5 %collective-permute-start.27 = (f32[8,2,32,256]{3,2,1,0:T(8,128)S(1)}, f32[8,2,32,256]{3,2,1,0:T(8,128)S(1)}, u32[]{:S(2)}, u32[]{:S(2)}) collective-permute-start(f32[8,2,32,256]{3,2,1,0:T(8,128)S(1)} %get-tuple-element.67), channel_id=1, source_target_pairs={{0,2},{2,0},{4,6},{6,4},{8,10},{10,8},{12,14},{14,12},{16,18},{18,... | collective-permute-start | bytes 1572872 | tf_op jit(solution)/shard_map/ppermute | solution.py:406
  89.0 13.4 %collective-permute-start.28 = (f32[8,2,32,256]{3,2,1,0:T(8,128)S(1)}, f32[8,2,32,256]{3,2,1,0:T(8,128)S(1)}, u32[]{:S(2)}, u32[]{:S(2)}) collective-permute-start(f32[8,2,32,256]{3,2,1,0:T(8,128)S(1)} %get-tuple-element.68), channel_id=1, source_target_pairs={{0,4},{2,6},{4,0},{6,2},{8,12},{10,14},{12,8},{14,10},{16,20},{18,... | collective-permute-start | bytes 1572872 | tf_op jit(solution)/shard_map/ppermute | solution.py:406
  90.5 7.0 %collective-permute-start.24 = (f32[2,2,32,256]{3,2,1,0:T(8,128)S(1)}, f32[2,2,32,256]{3,2,1,0:T(8,128)S(1)}, u32[]{:S(2)}, u32[]{:S(2)}) collective-permute-start(f32[2,2,32,256]{3,2,1,0:T(8,128)S(1)} %get-tuple-element.66.refs_0_), channel_id=1, source_target_pairs={{0,24},{2,26},{4,28},{6,30},{8,0},{10,2},{12,4},{14,6},{16,8},{18,... | collective-permute-start | bytes 393224 | tf_op jit(solution)/shard_map/ppermute | solution.py:412
  92.0 10.4 %collective-permute-start.25 = (f32[2,2,32,256]{3,2,1,0:T(8,128)S(1)}, f32[2,2,32,256]{3,2,1,0:T(8,128)S(1)}, u32[]{:S(2)}, u32[]{:S(2)}) collective-permute-start(f32[2,2,32,256]{3,2,1,0:T(8,128)S(1)} %get-tuple-element.66.refs_0_), channel_id=1, source_target_pairs={{0,16},{2,18},{4,20},{6,22},{8,24},{10,26},{12,28},{14,30},{16,0},... | collective-permute-start | bytes 393224 | tf_op jit(solution)/shard_map/ppermute | solution.py:412
  92.0 10.4 %collective-permute-start.26 = (f32[2,2,32,256]{3,2,1,0:T(8,128)S(1)}, f32[2,2,32,256]{3,2,1,0:T(8,128)S(1)}, u32[]{:S(2)}, u32[]{:S(2)}) collective-permute-start(f32[2,2,32,256]{3,2,1,0:T(8,128)S(1)} %get-tuple-element.66.refs_0_), channel_id=1, source_target_pairs={{0,8},{2,10},{4,12},{6,14},{8,16},{10,18},{12,20},{14,22},{16,24},... | collective-permute-start | bytes 393224 | tf_op jit(solution)/shard_map/ppermute | solution.py:412
  102.6 9.4 %collective-permute-start.29 = (f32[6,2,32,256]{3,2,1,0:T(8,128)S(1)}, f32[6,2,32,256]{3,2,1,0:T(8,128)S(1)}, u32[]{:S(2)}, u32[]{:S(2)}) collective-permute-start(f32[6,2,32,256]{3,2,1,0:T(8,128)S(1)} %get-tuple-element.70), channel_id=1, source_target_pairs={{0,2},{2,0},{4,6},{6,4},{8,10},{10,8},{12,14},{14,12},{16,18},{18,... | collective-permute-start | bytes 1179656 | tf_op jit(solution)/shard_map/ppermute | solution.py:406
  103.6 9.1 %collective-permute-start.30 = (f32[6,2,32,256]{3,2,1,0:T(8,128)S(1)}, f32[6,2,32,256]{3,2,1,0:T(8,128)S(1)}, u32[]{:S(2)}, u32[]{:S(2)}) collective-permute-start(f32[6,2,32,256]{3,2,1,0:T(8,128)S(1)} %get-tuple-element.71), channel_id=1, source_target_pairs={{0,4},{2,6},{4,0},{6,2},{8,12},{10,14},{12,8},{14,10},{16,20},{18,... | collective-permute-start | bytes 1179656 | tf_op jit(solution)/shard_map/ppermute | solution.py:406
  112.7 10.9 %collective-permute-start.31 = (f32[3,2,32,256]{3,2,1,0:T(8,128)S(1)}, f32[3,2,32,256]{3,2,1,0:T(8,128)S(1)}, u32[]{:S(2)}, u32[]{:S(2)}) collective-permute-start(f32[3,2,32,256]{3,2,1,0:T(8,128)S(1)} %get-tuple-element.73), channel_id=1, source_target_pairs={{0,2},{2,0},{4,6},{6,4},{8,10},{10,8},{12,14},{14,12},{16,18},{18,... | collective-permute-start | bytes 589832 | tf_op jit(solution)/shard_map/ppermute | solution.py:406
  113.9 9.7 %collective-permute-start.32 = (f32[3,2,32,256]{3,2,1,0:T(8,128)S(1)}, f32[3,2,32,256]{3,2,1,0:T(8,128)S(1)}, u32[]{:S(2)}, u32[]{:S(2)}) collective-permute-start(f32[3,2,32,256]{3,2,1,0:T(8,128)S(1)} %get-tuple-element.74), channel_id=1, source_target_pairs={{0,4},{2,6},{4,0},{6,2},{8,12},{10,14},{12,8},{14,10},{16,20},{18,... | collective-permute-start | bytes 589832 | tf_op jit(solution)/shard_map/ppermute | solution.py:406
  114.6 12.3 %collective-permute-start.33 = (f32[2,2,32,256]{3,2,1,0:T(8,128)S(1)}, f32[2,2,32,256]{3,2,1,0:T(8,128)S(1)}, u32[]{:S(2)}, u32[]{:S(2)}) collective-permute-start(f32[2,2,32,256]{3,2,1,0:T(8,128)S(1)} %get-tuple-element.75), channel_id=1, source_target_pairs={{0,8},{2,10},{4,12},{6,14},{8,16},{10,18},{12,20},{14,22},{16,24},... | collective-permute-start | bytes 393224 | tf_op jit(solution)/shard_map/ppermute | solution.py:412
  115.0 11.9 %collective-permute-start.34 = (f32[2,2,32,256]{3,2,1,0:T(8,128)S(1)}, f32[2,2,32,256]{3,2,1,0:T(8,128)S(1)}, u32[]{:S(2)}, u32[]{:S(2)}) collective-permute-start(f32[2,2,32,256]{3,2,1,0:T(8,128)S(1)} %get-tuple-element.76), channel_id=1, source_target_pairs={{0,16},{2,18},{4,20},{6,22},{8,24},{10,26},{12,28},{14,30},{16,0},... | collective-permute-start | bytes 393224 | tf_op jit(solution)/shard_map/ppermute | solution.py:412
  116.9 10.0 %collective-permute-start.35 = (f32[2,2,32,256]{3,2,1,0:T(8,128)S(1)}, f32[2,2,32,256]{3,2,1,0:T(8,128)S(1)}, u32[]{:S(2)}, u32[]{:S(2)}) collective-permute-start(f32[2,2,32,256]{3,2,1,0:T(8,128)S(1)} %get-tuple-element.77), channel_id=1, source_target_pairs={{0,24},{2,26},{4,28},{6,30},{8,0},{10,2},{12,4},{14,6},{16,8},{18,... | collective-permute-start | bytes 393224 | tf_op jit(solution)/shard_map/ppermute | solution.py:412
  (12 other events, 39.7 us)

commit v2 on v1

--- a/solution.py
+++ b/solution.py
@@ -14,6 +14,8 @@
 BF16 = jnp.bfloat16
 MIB = 1 << 20
 STREAM_LIMIT = 48 * MIB
+ALONE_LIMIT = 63 * MIB
+GROUPS = 5
 VMEM = pl.BlockSpec(memory_space=pltpu.VMEM)
 SMEM = pl.BlockSpec(memory_space=pltpu.SMEM)
 ANY = pl.BlockSpec(memory_space=pl.ANY)
@@ -54,10 +56,12 @@
     return (column * particles + particle) * layers + layer
 
 
-def prepare_kernel(layers, owner_ref, partners_ref, rows_of_ref, tmat_ref, *refs):
-    parts_ref, place_ref, group_ref, buf_ref, sems = refs
+def prepare_kernel(
+    layers, slots, owner_ref, side_ref, partners_ref, rows_of_ref, holders_ref, live_ref, tmat_ref, *refs
+):
+    parts_ref, index_ref, buf_ref, sems = refs
     particles, _, half, width = tmat_ref.shape
-    slots = place_ref.shape[0]
+    stride, counts = GROUPS * slots, 3 * GROUPS * slots
 
     def fetch(row):
         return pltpu.make_async_copy(tmat_ref.at[row], buf_ref.at[row], sems.at[row])
@@ -66,19 +70,27 @@
         fetch(row).start()
     me = owner_ref[0]
     my_column, my_layer = lax.rem(me, COLUMNS), lax.div(me, COLUMNS)
+    for group in range(GROUPS):
+        index_ref[counts + group] = 0
+    index_ref[counts + GROUPS] = side_ref[0]
 
     def step(slot, carry):
         row = rows_of_ref[partners_ref[me * slots + slot]]
         owner, particle = lax.div(row, particles), lax.rem(row, particles)
         column = lax.bitwise_xor(lax.rem(owner, COLUMNS), my_column)
         layer = lax.rem(lax.div(owner, COLUMNS) - my_layer + layers, layers)
-        place_ref[slot] = place_of(column, particle, layer, particles, layers)
         near = jnp.where(column == COLUMNS - 1, 2, 1)
         far = jnp.where(column == COLUMNS - 1, 4, 3)
-        group_ref[slot] = jnp.where(column == 0, 0, jnp.where(layer == 0, near, far))
+        group = jnp.where(column == 0, 0, jnp.where(layer == 0, near, far))
+        found = index_ref[counts + group]
+        index_ref[counts + group] = found + 1
+        position = group * slots + found
+        index_ref[position] = slot
+        index_ref[stride + position] = place_of(column, particle, layer, particles, layers)
+        index_ref[2 * stride + position] = holders_ref[slot]
         return carry
 
-    lax.fori_loop(0, slots, step, 0)
+    lax.fori_loop(0, live_ref[0], step, 0)
     for row in range(particles):
         fetch(row).wait()
         for part in range(2):
@@ -87,22 +99,21 @@
             parts_ref[row, :, (2 + part) * width : (3 + part) * width] = low
 
 
-def prepare(my_owner, partners, owner_of, tmat, slots, layers):
+def prepare(my_owner, side, partners, owner_of, block_rows, live, tmat, layers):
     particles, _, half, width = tmat.shape
-    index_shape = jax.ShapeDtypeStruct((slots,), jnp.int32)
+    slots = block_rows.shape[0]
     return pl.pallas_call(
-        functools.partial(prepare_kernel, layers),
+        functools.partial(prepare_kernel, layers, slots),
         out_shape=(
             jax.ShapeDtypeStruct((particles, half, 4 * width), BF16),
-            index_shape,
-            index_shape,
+            jax.ShapeDtypeStruct((3 * GROUPS * slots + GROUPS + 1,), jnp.int32),
         ),
-        in_specs=[SMEM, SMEM, SMEM, HBM],
-        out_specs=(VMEM, SMEM, SMEM),
+        in_specs=[SMEM] * 6 + [HBM],
+        out_specs=(VMEM, SMEM),
         scratch_shapes=[pltpu.VMEM(tmat.shape, F32), pltpu.SemaphoreType.DMA((particles,))],
-        compiler_params=params(3 * size_of(tmat)),
+        compiler_params=pltpu.CompilerParams(vmem_limit_bytes=ALONE_LIMIT),
         name="prepare",
-    )(my_owner, partners, owner_of, tmat)
+    )(my_owner, side, partners, owner_of, block_rows, live, tmat)
 
 
 def tmat_kernel(halves, side_ref, mine_ref, theirs_ref, parts_ref, *refs):
@@ -138,40 +149,50 @@
         in_specs=[SMEM, VMEM, VMEM, VMEM],
         out_specs=[VMEM] * count,
         scratch_shapes=[pltpu.VMEM((particles, 2, directions, 2 * half), F32)],
-        compiler_params=params(3 * size_of(mine, theirs), size_of(parts)),
+        compiler_params=(
+            pltpu.CompilerParams(vmem_limit_bytes=ALONE_LIMIT - size_of(parts, theirs))
+            if halves
+            else params(3 * size_of(mine, theirs), size_of(parts))
+        ),
         name="tmat_apply",
     )(side, mine, theirs, parts)
 
 
-def chosen_slots(group_ref, alive, groups, list_ref):
-    mask = sum(1 << group for group in groups)
-
-    def step(slot, found):
-        list_ref[found] = slot
-        return found + (lax.shift_right_logical(mask, group_ref[slot]) & 1)
-
-    return lax.fori_loop(0, alive, step, 0)
-
-
-def backward_kernel(first, groups, base, rows_ref, live_ref, place_ref, group_ref, side_ref, *refs):
-    own_ref, other_ref, blocks_ref = refs[:3]
-    refs = refs[3:]
+def chosen_slots(index_ref, groups, slots):
+    stride, counts = GROUPS * slots, 3 * GROUPS * slots
+    starts, total = [], 0
+    for group in groups:
+        starts.append(total)
+        total = total + index_ref[counts + group]
+
+    def at_turn(turn):
+        position = groups[0] * slots + turn
+        for group, start in zip(groups[1:], starts[1:]):
+            position = jnp.where(turn >= start, group * slots + turn - start, position)
+        return [index_ref[number * stride + position] for number in range(3)]
+
+    return total, at_turn
+
+
+def backward_kernel(first, groups, base, index_ref, own_ref, other_ref, blocks_ref, *refs):
     if first:
-        out_ref, parts_ref, list_ref, left_ref, buf_ref, sems, made_ref, made_sems = refs[-8:]
+        out_ref, parts_ref, left_ref, buf_ref, sems, made_ref, made_sems = refs[-7:]
     else:
-        out_ref, list_ref, left_ref, buf_ref, sems = refs
+        out_ref, left_ref, buf_ref, sems = refs
     directions, half = own_ref.shape[2], own_ref.shape[3]
     width = 2 * half
-    wanted = chosen_slots(group_ref, live_ref[0], groups, list_ref)
+    slots = blocks_ref.shape[0]
+    wanted, at_turn = chosen_slots(index_ref, groups, slots)
+    own_side = index_ref[3 * GROUPS * slots + GROUPS]
 
     def fetch(turn, place):
         return pltpu.make_async_copy(
-            blocks_ref.at[list_ref[turn]], buf_ref.at[place], sems.at[place]
+            blocks_ref.at[at_turn(turn)[0]], buf_ref.at[place], sems.at[place]
         )
 
     def keep(turn, place):
         return pltpu.make_async_copy(
-            made_ref.at[place], parts_ref.at[list_ref[turn]], made_sems.at[place]
+            made_ref.at[place], parts_ref.at[at_turn(turn)[0]], made_sems.at[place]
         )
 
     for early in range(BUFFERS):
@@ -180,7 +201,7 @@
         def _():
             fetch(early, early).start()
 
-    for field_ref, side in ((own_ref, side_ref[0]), (other_ref, 1 - side_ref[0])):
+    for field_ref, side in ((own_ref, own_side), (other_ref, 1 - own_side)):
         for row in range(field_ref.shape[0]):
             with_real, with_imag = stacked_parts(field_ref[row, 0], field_ref[row, 1])
             for part, value in enumerate((with_real, with_imag)):
@@ -191,8 +212,8 @@
     def body(turn, carry):
         here = lax.rem(turn, BUFFERS)
         fetch(turn, here).wait()
-        slot = list_ref[turn]
-        holder = rows_ref[slot]
+        _, place, holder = at_turn(turn)
+        place = place - base
         if first:
             spot = lax.rem(turn, 2)
 
@@ -210,7 +231,6 @@
         total = dot_nn(left_ref[holder], high)
         rest = dot_nn(left_ref[holder, : 2 * directions], low)
         out = total[: 2 * directions] + total[2 * directions :] + rest
-        place = place_ref[slot] - base
         out_ref[place, 0] = out[:directions]
         out_ref[place, 1] = out[directions:]
 
@@ -232,7 +252,7 @@
             keep(wanted - 1, lax.rem(wanted - 1, 2)).wait()
 
 
-def backward(first, groups, base, count, index, side, own_half, other_half, blocks, parts):
+def backward(first, groups, base, count, index, own_half, other_half, blocks, parts):
     particles, _, directions, half = own_half.shape
     width = 2 * half
     slots = blocks.shape[0]
@@ -240,13 +260,12 @@
     out_specs = [VMEM]
     source = blocks if first else parts
     scratch = [
-        pltpu.SMEM((slots + 1,), jnp.int32),
         pltpu.VMEM((particles, 4 * directions, 2 * width), BF16),
         pltpu.VMEM((BUFFERS,) + source.shape[1:], source.dtype),
         pltpu.SemaphoreType.DMA((BUFFERS,)),
     ]
-    operands = [*index, side, own_half, other_half, source]
-    in_specs = [SMEM] * 5 + [VMEM, VMEM, HBM]
+    operands = [index, own_half, other_half, source]
+    in_specs = [SMEM, VMEM, VMEM, HBM]
     aliases = {}
     if first:
         out_shape.append(jax.ShapeDtypeStruct((slots, 2, 2, width, half), BF16))
@@ -274,16 +293,16 @@
     )(*operands)
 
 
-def forward_kernel(groups, copies, count, rows_ref, live_ref, place_ref, group_ref, *refs):
+def forward_kernel(groups, copies, count, index_ref, *refs):
     field_refs = refs[:count]
     parts_ref = refs[count]
-    out_ref, list_ref, every_ref, acc_ref, buf_ref, sems = refs[-6:]
+    out_ref, every_ref, acc_ref, buf_ref, sems = refs[-5:]
     directions = out_ref.shape[2]
-    wanted = chosen_slots(group_ref, live_ref[0], groups, list_ref)
+    wanted, at_turn = chosen_slots(index_ref, groups, parts_ref.shape[0])
 
     def fetch(turn, place):
         return pltpu.make_async_copy(
-            parts_ref.at[list_ref[turn]], buf_ref.at[place], sems.at[place]
+            parts_ref.at[at_turn(turn)[0]], buf_ref.at[place], sems.at[place]
         )
 
     for early in range(BUFFERS):
@@ -298,9 +317,7 @@
 
     def body(turn, carry):
         here = lax.rem(turn, BUFFERS)
-        slot = list_ref[turn]
-        holder = rows_ref[slot]
-        place = place_ref[slot]
+        _, place, holder = at_turn(turn)
         with_real, with_imag = stacked_parts(every_ref[place, 0], every_ref[place, 1])
         fetch(turn, here).wait()
         total = dot_nt(with_real, buf_ref[here, 0, 0]) + dot_nt(with_imag, buf_ref[here, 0, 1])
@@ -327,11 +344,10 @@
     return pl.pallas_call(
         functools.partial(forward_kernel, groups, copies, len(fields)),
         out_shape=out_shape,
-        in_specs=[SMEM] * 4 + [VMEM] * len(fields) + [HBM] + [ANY] * len(after),
+        in_specs=[SMEM] + [VMEM] * len(fields) + [HBM] + [ANY] * len(after),
         out_specs=VMEM,
         scratch_shapes=[
-            pltpu.SMEM((slots + 1,), jnp.int32),
-            pltpu.VMEM((total_rows, 2, directions, half), F32),
+                pltpu.VMEM((total_rows, 2, directions, half), F32),
             pltpu.VMEM((particles, 2 * directions, width), F32),
             pltpu.VMEM((BUFFERS,) + parts.shape[1:], BF16),
             pltpu.SemaphoreType.DMA((BUFFERS,)),
@@ -343,7 +359,7 @@
             transcendentals=0,
         ),
         name="forward_group" + str(groups[0]),
-    )(*index, *fields, parts, *after)
+    )(index, *fields, parts, *after)
 
 
 def pack_kernel(plans, count, *refs):
@@ -431,7 +447,7 @@
     other = from_other(scattered)
     x1 = across(scattered, 1)
     y1 = across(scattered, 2)
-    fetched = (side, scattered, other, blocks)
+    fetched = (scattered, other, blocks)
     products_d, *made = backward(
         first, (2, 4), first_d, total_rows - first_d, index, *fetched, parts
     )
@@ -468,7 +484,7 @@
     x3, y3 = across(x3, 1), across(y3, 2)
     z3 = [along(copied, -shift) for shift in rest]
     products_o, *made = backward(
-        first, (0,), 0, first_n, index, side, copied, other, blocks, parts
+        first, (0,), 0, first_n, index, copied, other, blocks, parts
     )
     if first:
         parts = made[0]
@@ -510,7 +526,7 @@
             [[(0, tail(particle, shift))] for particle in by_x for shift in rest],
             [[(0, 0)]],
         ],
-        [near_first],
+        [near_first, z4[len(z4) // 2]],
     )
     x5, y5 = across(x5, 1), across(y5, 2)
     copies = []
@@ -534,13 +550,13 @@
 
 
 def local(incident, tmat, blocks, block_rows, partners, live, owner_of):
-    slots = blocks.shape[0]
     layers = lax.axis_size("owner") // COLUMNS
     my_owner = lax.axis_index("owner").astype(jnp.int32)[None]
     side = lax.axis_index("pair").astype(jnp.int32)[None]
     theirs = from_other(incident)
-    tmat_parts, place, group = prepare(my_owner, partners, owner_of, tmat, slots, layers)
-    index = (block_rows, live, place, group)
+    tmat_parts, index = prepare(
+        my_owner, side, partners, owner_of, block_rows, live, tmat, layers
+    )
     (scattered,) = apply_tmat(True, False, side, incident, theirs, tmat_parts)
     parts = None
     for turn in range(ITERS):

time: 132 us -> 131 us (level); the launches traced: 130 us -> 133 us
  waiting for transfers between devices: 25.5 us -> 19.5 us
  starting transfers between devices: 40.2 us -> 46 us
  Pallas kernels: 58.4 us -> 63.6 us
  local copies, waits for them, and re-layouts: 4.48 us -> 2.28 us
    ppermute x20, waiting for transfers between devices: 12.8 us -> 3.88 us  [across(): lax.ppermute(value, 'owner', [(source, source ^ bit) for source in range(...]
    ppermute x20, starting transfers between devices: 22.2 us -> 26 us  [across(): lax.ppermute(value, 'owner', [(source, source ^ bit) for source in range(...]
    ppermute x12, waiting for transfers between devices: 9.63 us -> 12.5 us  [along(): lax.ppermute(value, 'owner', [(source, (source + step) % count) for sourc...]
    pallas_call x3, Pallas kernels: 3.29 us -> 5.71 us  [apply_tmat(): pl.pallas_call(functools.partial(tmat_kernel, halves), out_shape=[half_sh...]
    unnamed x14, local copies, waits for them, and re-layouts: 4.48 us -> 2.28 us
    ppermute x12, starting transfers between devices: 17 us -> 19.1 us  [along(): lax.ppermute(value, 'owner', [(source, (source + step) % count) for sourc...]
    pallas_call x1, Pallas kernels: 1.98 us -> 3.73 us  [prepare(): pl.pallas_call(functools.partial(prepare_kernel, layers, slots), out_shap...]
  transfers between devices with their start and end apart: 37 -> 37, of which waited for: 15 -> 12; matrix products, arithmetic and copies ran while one was open for 0% -> 0% of each run, Pallas kernels for 42% -> 43%
where the time goes in v2:
time: 131 us; the launch traced here: 133 us
  Pallas kernels  63.6 us (49%)
  starting transfers between devices  46 us (35%)
  waiting for transfers between devices  19.5 us (15%)
  local copies, waits for them, and re-layouts  2.28 us (2%)
  between operations  1.63 us (1%)
    pallas_call x6, Pallas kernels, backward(): pl.pallas_call(functools.partial(backward_kernel, first, groups, base), o...  27.6 us
    ppermute x20, starting transfers between devices, across(): lax.ppermute(value, 'owner', [(source, source ^ bit) for source in range(...  26 us
    pallas_call x6, Pallas kernels, forward(): pl.pallas_call(functools.partial(forward_kernel, groups, copies, len(fiel...  25.8 us
    ppermute x12, starting transfers between devices, along(): lax.ppermute(value, 'owner', [(source, (source + step) % count) for sourc...  19.1 us
    ppermute x12, waiting for transfers between devices, along(): lax.ppermute(value, 'owner', [(source, (source + step) % count) for sourc...  12.5 us
    pallas_call x3, Pallas kernels, apply_tmat(): pl.pallas_call(functools.partial(tmat_kernel, halves), out_shape=[half_sh...  5.71 us
    ppermute x20, waiting for transfers between devices, across(): lax.ppermute(value, 'owner', [(source, source ^ bit) for source in range(...  3.88 us
    pallas_call x1, Pallas kernels, prepare(): pl.pallas_call(functools.partial(prepare_kernel, layers, slots), out_shap...  3.73 us
  transfers between devices with their start and end apart: 37, of which 12 were waited for; matrix products, arithmetic and copies ran while one was open for 0% of the time, Pallas kernels for 43%

profile of v2, /device:TPU:0, one launch (start us, length us, event | category | flops | bytes accessed | tf_op | source)
XLA Modules:
  0.0 132.9 jit_solution(3956831235037786864)
XLA Ops:
  1.8 3.7 %prepare.1 = (bf16[2,256,2048]{2,1,0:T(8,128)(2,1)}, s32[321]{0:T(512)}) custom-call(s32[1]{0:T(128)} %bitcast.1.owner_ref, s32[1]{0:T(128)} %bitcast.side_ref, s32[336]{0:T(512)} %partners_ref.1, s32[32]{0:T(128)} %rows_of_ref.1, s32[21]{0:T(128)} %holders_ref.1, s32[1]{0:T(128)S(6)} %copy.13.live_ref, f32[2,2,256,512]{3,2,1,0:T(8,128)} %tmat_ref.1), custom_call_target="tpu_custom_call" | custom-call | tf_op jit(solution)/shard_map/prepare/pallas_call | solution.py:105
  6.2 3.3 %tmat_apply.3.own_ref.refs_3_ = f32[2,2,32,256]{3,2,1,0:T(8,128)} custom-call(s32[1]{0:T(128)} %bitcast.side_ref, f32[2,2,32,256]{3,2,1,0:T(8,128)} %incident_ref.3, f32[2,2,32,256]{3,2,1,0:T(8,128)} %copy-done.6, bf16[2,256,2048]{2,1,0:T(8,128)(2,1)} %get-tuple-element.41.parts_ref), custom_call_target="tpu_custom_call" | custom-call | tf_op jit(solution)/shard_map/tmat_apply/pallas_call | solution.py:146
  9.6 2.9 %collective-permute-start.1 = (f32[2,2,32,256]{3,2,1,0:T(8,128)}, f32[2,2,32,256]{3,2,1,0:T(8,128)S(1)}, u32[]{:S(2)}, u32[]{:S(2)}) collective-permute-start(f32[2,2,32,256]{3,2,1,0:T(8,128)} %tmat_apply.3.own_ref.refs_3_), channel_id=1, source_target_pairs={{0,2},{2,0},{4,6},{6,4},{8,10},{10,8},{12,14},{14,12},{16,18},{18,... | collective-permute-start | bytes 393224 | tf_op jit(solution)/shard_map/ppermute | solution.py:422
  15.7 4.5 %backward_group2.2 = (f32[8,2,32,256]{3,2,1,0:T(8,128)S(1)}, bf16[21,2,2,512,256]{4,3,2,1,0:T(8,128)(2,1)}) custom-call(s32[321]{0:T(512)S(1)} %copy-done.4, f32[2,2,32,256]{3,2,1,0:T(8,128)S(1)} %copy-done.1, f32[2,2,32,256]{3,2,1,0:T(8,128)S(1)} %collective-permute-done.3.other_ref, f32[21,2,512,256]{3,2,1,0:T(8,128)} %blocks_ref.5), custom_call_target="tpu_custom_call" | custom-call | flops 4194304 | bytes 131072 | tf_op jit(solution)/shard_map/backward_group2/pallas_call | solution.py:279
  21.8 7.7 %backward_group1.2 = (f32[16,2,32,256]{3,2,1,0:T(8,128)S(1)}, bf16[21,2,2,512,256]{4,3,2,1,0:T(8,128)(2,1)}) custom-call(s32[321]{0:T(512)S(1)} %copy-done.5, f32[2,2,32,256]{3,2,1,0:T(8,128)S(1)} %copy-done.2, f32[2,2,32,256]{3,2,1,0:T(8,128)S(1)} %collective-permute-done.3.other_ref, ...), custom_call_target="tpu_custom_call", output_to_operand_aliasing={{1}: (4, {})} | custom-call | flops 4194304 | bytes 131072 | tf_op jit(solution)/shard_map/backward_group1/pallas_call | solution.py:279
  29.6 2.3 %collective-permute-start.10 = (f32[8,2,32,256]{3,2,1,0:T(8,128)S(1)}, f32[8,2,32,256]{3,2,1,0:T(8,128)S(1)}, u32[]{:S(2)}, u32[]{:S(2)}) collective-permute-start(f32[8,2,32,256]{3,2,1,0:T(8,128)S(1)} %get-tuple-element.52), channel_id=1, source_target_pairs={{0,4},{2,6},{4,0},{6,2},{8,12},{10,14},{12,8},{14,10},{16,20},{18,... | collective-permute-start | bytes 1572872 | tf_op jit(solution)/shard_map/ppermute | solution.py:422
  32.7 3.4 %collective-permute-start.6 = (f32[2,2,32,256]{3,2,1,0:T(8,128)S(1)}, f32[2,2,32,256]{3,2,1,0:T(8,128)S(1)}, u32[]{:S(2)}, u32[]{:S(2)}) collective-permute-start(f32[2,2,32,256]{3,2,1,0:T(8,128)S(1)} %get-tuple-element.47.own_ref), channel_id=1, source_target_pairs={{0,24},{2,26},{4,28},{6,30},{8,0},{10,2},{12,4},{14,6},{16,8},{18,... | collective-permute-start | bytes 393224 | tf_op jit(solution)/shard_map/ppermute | solution.py:428
  36.1 1.9 %collective-permute-start.8 = (f32[2,2,32,256]{3,2,1,0:T(8,128)S(1)}, f32[2,2,32,256]{3,2,1,0:T(8,128)S(1)}, u32[]{:S(2)}, u32[]{:S(2)}) collective-permute-start(f32[2,2,32,256]{3,2,1,0:T(8,128)S(1)} %get-tuple-element.47.own_ref), channel_id=1, source_target_pairs={{0,8},{2,10},{4,12},{6,14},{8,16},{10,18},{12,20},{14,22},{16,24},... | collective-permute-start | bytes 393224 | tf_op jit(solution)/shard_map/ppermute | solution.py:428
  38.1 4.6 %backward_group0.2 = (f32[8,2,32,256]{3,2,1,0:T(8,128)S(1)}, bf16[21,2,2,512,256]{4,3,2,1,0:T(8,128)(2,1)}) custom-call(s32[321]{0:T(512)S(1)} %copy-done.5, f32[2,2,32,256]{3,2,1,0:T(8,128)S(1)} %get-tuple-element.47.own_ref, f32[2,2,32,256]{3,2,1,0:T(8,128)S(1)} %collective-permute-done.3.other_ref, ...), custom_call_target="tpu_custom_call", output_to_operand_aliasing={{1}: (4, {})} | custom-call | flops 4194304 | bytes 131072 | tf_op jit(solution)/shard_map/backward_group0/pallas_call | solution.py:279
  42.7 4.7 %collective-permute-done.7.refs_4_.refs_5_ = f32[2,2,32,256]{3,2,1,0:T(8,128)S(1)} collective-permute-done((f32[2,2,32,256]{3,2,1,0:T(8,128)S(1)}, f32[2,2,32,256]{3,2,1,0:T(8,128)S(1)}, u32[]{:S(2)}, u32[]{:S(2)}) %collective-permute-start.7) | collective-permute-done | bytes 131104 | tf_op jit(solution)/shard_map/ppermute | solution.py:428
  49.7 2.4 %collective-permute-start.13 = (f32[2,2,32,256]{3,2,1,0:T(8,128)S(1)}, f32[2,2,32,256]{3,2,1,0:T(8,128)S(1)}, u32[]{:S(2)}, u32[]{:S(2)}) collective-permute-start(f32[2,2,32,256]{3,2,1,0:T(8,128)S(1)} %get-tuple-element.56), channel_id=1, source_target_pairs={{0,16},{2,18},{4,20},{6,22},{8,24},{10,26},{12,28},{14,30},{16,0},... | collective-permute-start | bytes 393224 | tf_op jit(solution)/shard_map/ppermute | solution.py:428
  52.0 4.6 %forward_group0.2.refs_2_.refs_0_ = f32[2,2,32,512]{3,2,1,0:T(8,128)S(1)} custom-call(s32[321]{0:T(512)S(1)} %copy-done.5, f32[2,2,32,256]{3,2,1,0:T(8,128)S(1)} %collective-permute-done.1.refs_1_.refs_0_, f32[2,2,32,256]{3,2,1,0:T(8,128)S(1)} %collective-permute-done.2.refs_2_.refs_1_, f32[5,2,32,256]{3,2,1,0:T(8,128)S(1)} %collective-permute-done.4.refs_1_.refs_2_, ...), custom_call_target="tpu_custom_call" | custom-call | flops 4194304 | bytes 262144 | tf_op jit(solution)/shard_map/forward_group0/pallas_call | solution.py:344
  61.3 2.7 %collective-permute-start.17 = (f32[2,2,32,256]{3,2,1,0:T(8,128)S(1)}, f32[2,2,32,256]{3,2,1,0:T(8,128)S(1)}, u32[]{:S(2)}, u32[]{:S(2)}) collective-permute-start(f32[2,2,32,256]{3,2,1,0:T(8,128)S(1)} %get-tuple-element.61), channel_id=1, source_target_pairs={{0,24},{2,26},{4,28},{6,30},{8,0},{10,2},{12,4},{14,6},{16,8},{18,... | collective-permute-start | bytes 393224 | tf_op jit(solution)/shard_map/ppermute | solution.py:428
  64.0 5.1 %forward_group3.2.refs_3_.refs_1_ = f32[2,2,32,512]{3,2,1,0:T(8,128)S(1)} custom-call(s32[321]{0:T(512)S(1)} %copy-done.5, f32[6,2,32,256]{3,2,1,0:T(8,128)S(1)} %collective-permute-done.11.refs_0_, f32[6,2,32,256]{3,2,1,0:T(8,128)S(1)} %collective-permute-done.12.refs_1_, bf16[21,2,2,512,256]{4,3,2,1,0:T(8,128)(2,1)} %get-tuple-element.49.refs_7_.refs_2_.blocks_ref, ...), custom_call_target="tpu_custom_call" | custom-call | flops 4194304 | bytes 262144 | tf_op jit(solution)/shard_map/forward_group3/pallas_call | solution.py:344
  69.2 3.2 %forward_group4.2.refs_2_ = f32[2,2,32,512]{3,2,1,0:T(8,128)S(1)} custom-call(s32[321]{0:T(512)S(1)} %copy-done.5, f32[3,2,32,256]{3,2,1,0:T(8,128)S(1)} %collective-permute-done.14.refs_0_, f32[3,2,32,256]{3,2,1,0:T(8,128)S(1)} %collective-permute-done.15.refs_1_, bf16[21,2,2,512,256]{4,3,2,1,0:T(8,128)(2,1)} %get-tuple-element.49.refs_7_.refs_2_.blocks_ref, ...), custom_call_target="tpu_custom_call" | custom-call | flops 4194304 | bytes 262144 | tf_op jit(solution)/shard_map/forward_group4/pallas_call | solution.py:344
  72.6 1.5 %collective-permute-done.18.theirs_ref = f32[2,2,32,512]{3,2,1,0:T(8,128)S(1)} collective-permute-done((f32[2,2,32,512]{3,2,1,0:T(8,128)S(1)}, f32[2,2,32,512]{3,2,1,0:T(8,128)S(1)}, u32[]{:S(2)}, u32[]{:S(2)}) %collective-permute-start.18) | collective-permute-done | bytes 262176 | tf_op jit(solution)/shard_map/ppermute | solution.py:417
  75.2 2.6 %collective-permute-start.20 = (f32[2,2,32,256]{3,2,1,0:T(8,128)S(1)}, f32[2,2,32,256]{3,2,1,0:T(8,128)S(1)}, u32[]{:S(2)}, u32[]{:S(2)}) collective-permute-start(f32[2,2,32,256]{3,2,1,0:T(8,128)S(1)} %tmat_apply.4.own_ref.refs_3_), channel_id=1, source_target_pairs={{0,4},{2,6},{4,0},{6,2},{8,12},{10,14},{12,8},{14,10},{16,20},{18,... | collective-permute-start | bytes 393224 | tf_op jit(solution)/shard_map/ppermute | solution.py:422
  77.8 3.1 %backward_group2.3.refs_0_ = f32[8,2,32,256]{3,2,1,0:T(8,128)S(1)} custom-call(s32[321]{0:T(512)S(1)} %copy-done.5, f32[2,2,32,256]{3,2,1,0:T(8,128)S(1)} %tmat_apply.4.own_ref.refs_3_, f32[2,2,32,256]{3,2,1,0:T(8,128)S(1)} %collective-permute-done.21.other_ref, bf16[21,2,2,512,256]{4,3,2,1,0:T(8,128)(2,1)} %get-tuple-element.49.refs_7_.refs_2_.blocks_ref), custom_call_target="tpu_custom_call" | custom-call | flops 4194304 | bytes 131072 | tf_op jit(solution)/shard_map/backward_group2/pallas_call | solution.py:279
  81.6 1.7 %collective-permute-start.22 = (f32[5,2,32,256]{3,2,1,0:T(8,128)S(1)}, f32[5,2,32,256]{3,2,1,0:T(8,128)S(1)}, u32[]{:S(2)}, u32[]{:S(2)}) collective-permute-start(f32[5,2,32,256]{3,2,1,0:T(8,128)S(1)} %get-tuple-element.62), channel_id=1, source_target_pairs={{0,2},{2,0},{4,6},{6,4},{8,10},{10,8},{12,14},{14,12},{16,18},{18,... | collective-permute-start | bytes 983048 | tf_op jit(solution)/shard_map/ppermute | solution.py:422
  83.3 1.7 %collective-permute-start.23 = (f32[5,2,32,256]{3,2,1,0:T(8,128)S(1)}, f32[5,2,32,256]{3,2,1,0:T(8,128)S(1)}, u32[]{:S(2)}, u32[]{:S(2)}) collective-permute-start(f32[5,2,32,256]{3,2,1,0:T(8,128)S(1)} %get-tuple-element.63), channel_id=1, source_target_pairs={{0,4},{2,6},{4,0},{6,2},{8,12},{10,14},{12,8},{14,10},{16,20},{18,... | collective-permute-start | bytes 983048 | tf_op jit(solution)/shard_map/ppermute | solution.py:422
  85.1 4.6 %backward_group1.3.refs_0_ = f32[16,2,32,256]{3,2,1,0:T(8,128)S(1)} custom-call(s32[321]{0:T(512)S(1)} %copy-done.5, f32[2,2,32,256]{3,2,1,0:T(8,128)S(1)} %tmat_apply.4.own_ref.refs_3_, f32[2,2,32,256]{3,2,1,0:T(8,128)S(1)} %collective-permute-done.21.other_ref, bf16[21,2,2,512,256]{4,3,2,1,0:T(8,128)(2,1)} %get-tuple-element.49.refs_7_.refs_2_.blocks_ref), custom_call_target="tpu_custom_call" | custom-call | flops 4194304 | bytes 131072 | tf_op jit(solution)/shard_map/backward_group1/pallas_call | solution.py:279
  92.8 1.7 %collective-permute-start.28 = (f32[8,2,32,256]{3,2,1,0:T(8,128)S(1)}, f32[8,2,32,256]{3,2,1,0:T(8,128)S(1)}, u32[]{:S(2)}, u32[]{:S(2)}) collective-permute-start(f32[8,2,32,256]{3,2,1,0:T(8,128)S(1)} %get-tuple-element.66), channel_id=1, source_target_pairs={{0,4},{2,6},{4,0},{6,2},{8,12},{10,14},{12,8},{14,10},{16,20},{18,... | collective-permute-start | bytes 1572872 | tf_op jit(solution)/shard_map/ppermute | solution.py:422
  96.5 3.1 %backward_group0.3.refs_0_.refs_3_ = f32[8,2,32,256]{3,2,1,0:T(8,128)S(1)} custom-call(s32[321]{0:T(512)S(1)} %copy-done.5, f32[2,2,32,256]{3,2,1,0:T(8,128)S(1)} %get-tuple-element.64.own_ref, f32[2,2,32,256]{3,2,1,0:T(8,128)S(1)} %collective-permute-done.21.other_ref, bf16[21,2,2,512,256]{4,3,2,1,0:T(8,128)(2,1)} %get-tuple-element.49.refs_7_.refs_2_.blocks_ref), custom_call_target="tpu_custom_call" | custom-call | flops 4194304 | bytes 131072 | tf_op jit(solution)/shard_map/backward_group0/pallas_call | solution.py:279
  99.9 5.7 %collective-permute-done.25.refs_4_.refs_5_ = f32[2,2,32,256]{3,2,1,0:T(8,128)S(1)} collective-permute-done((f32[2,2,32,256]{3,2,1,0:T(8,128)S(1)}, f32[2,2,32,256]{3,2,1,0:T(8,128)S(1)}, u32[]{:S(2)}, u32[]{:S(2)}) %collective-permute-start.25) | collective-permute-done | bytes 131104 | tf_op jit(solution)/shard_map/ppermute | solution.py:428
  107.9 1.7 %collective-permute-start.31 = (f32[2,2,32,256]{3,2,1,0:T(8,128)S(1)}, f32[2,2,32,256]{3,2,1,0:T(8,128)S(1)}, u32[]{:S(2)}, u32[]{:S(2)}) collective-permute-start(f32[2,2,32,256]{3,2,1,0:T(8,128)S(1)} %get-tuple-element.70), channel_id=1, source_target_pairs={{0,16},{2,18},{4,20},{6,22},{8,24},{10,26},{12,28},{14,30},{16,0},... | collective-permute-start | bytes 393224 | tf_op jit(solution)/shard_map/ppermute | solution.py:428
  109.5 4.6 %forward_group0.3.refs_2_.refs_0_ = f32[2,2,32,512]{3,2,1,0:T(8,128)S(1)} custom-call(s32[321]{0:T(512)S(1)} %copy-done.5, f32[2,2,32,256]{3,2,1,0:T(8,128)S(1)} %collective-permute-done.19.refs_1_.refs_0_, f32[2,2,32,256]{3,2,1,0:T(8,128)S(1)} %collective-permute-done.20.refs_2_.refs_1_, f32[5,2,32,256]{3,2,1,0:T(8,128)S(1)} %collective-permute-done.22.refs_1_.refs_2_, ...), custom_call_target="tpu_custom_call" | custom-call | flops 4194304 | bytes 262144 | tf_op jit(solution)/shard_map/forward_group0/pallas_call | solution.py:344
  115.7 1.9 %collective-permute-start.33 = (f32[3,2,32,256]{3,2,1,0:T(8,128)S(1)}, f32[3,2,32,256]{3,2,1,0:T(8,128)S(1)}, u32[]{:S(2)}, u32[]{:S(2)}) collective-permute-start(f32[3,2,32,256]{3,2,1,0:T(8,128)S(1)} %get-tuple-element.73), channel_id=1, source_target_pairs={{0,4},{2,6},{4,0},{6,2},{8,12},{10,14},{12,8},{14,10},{16,20},{18,... | collective-permute-start | bytes 589832 | tf_op jit(solution)/shard_map/ppermute | solution.py:422
  118.3 3.1 %collective-permute-start.35 = (f32[2,2,32,256]{3,2,1,0:T(8,128)S(1)}, f32[2,2,32,256]{3,2,1,0:T(8,128)S(1)}, u32[]{:S(2)}, u32[]{:S(2)}) collective-permute-start(f32[2,2,32,256]{3,2,1,0:T(8,128)S(1)} %get-tuple-element.75), channel_id=1, source_target_pairs={{0,24},{2,26},{4,28},{6,30},{8,0},{10,2},{12,4},{14,6},{16,8},{18,... | collective-permute-start | bytes 393224 | tf_op jit(solution)/shard_map/ppermute | solution.py:428
  121.4 5.0 %forward_group3.3.refs_3_.refs_1_ = f32[2,2,32,512]{3,2,1,0:T(8,128)S(1)} custom-call(s32[321]{0:T(512)S(1)} %copy-done.5, f32[6,2,32,256]{3,2,1,0:T(8,128)S(1)} %collective-permute-done.29.refs_0_, f32[6,2,32,256]{3,2,1,0:T(8,128)S(1)} %collective-permute-done.30.refs_1_, bf16[21,2,2,512,256]{4,3,2,1,0:T(8,128)(2,1)} %get-tuple-element.49.refs_7_.refs_2_.blocks_ref, ...), custom_call_target="tpu_custom_call" | custom-call | flops 4194304 | bytes 262144 | tf_op jit(solution)/shard_map/forward_group3/pallas_call | solution.py:344
  126.5 3.2 %forward_group4.3.refs_2_ = f32[2,2,32,512]{3,2,1,0:T(8,128)S(1)} custom-call(s32[321]{0:T(512)S(1)} %copy-done.5, f32[3,2,32,256]{3,2,1,0:T(8,128)S(1)} %collective-permute-done.32.refs_0_, f32[3,2,32,256]{3,2,1,0:T(8,128)S(1)} %collective-permute-done.33.refs_1_, bf16[21,2,2,512,256]{4,3,2,1,0:T(8,128)(2,1)} %get-tuple-element.49.refs_7_.refs_2_.blocks_ref, ...), custom_call_target="tpu_custom_call" | custom-call | flops 4194304 | bytes 262144 | tf_op jit(solution)/shard_map/forward_group4/pallas_call | solution.py:344
  129.9 1.5 %collective-permute-done.36.theirs_ref = f32[2,2,32,512]{3,2,1,0:T(8,128)S(1)} collective-permute-done((f32[2,2,32,512]{3,2,1,0:T(8,128)S(1)}, f32[2,2,32,512]{3,2,1,0:T(8,128)S(1)}, u32[]{:S(2)}, u32[]{:S(2)}) %collective-permute-start.36) | collective-permute-done | bytes 262176 | tf_op jit(solution)/shard_map/ppermute | solution.py:417
  131.4 1.5 %tmat_apply.5 = (f32[2,2,32,256]{3,2,1,0:T(8,128)}, f32[2,2,32,256]{3,2,1,0:T(8,128)}) custom-call(s32[1]{0:T(128)} %bitcast.side_ref, f32[2,2,32,512]{3,2,1,0:T(8,128)S(1)} %total.3.mine_ref, f32[2,2,32,512]{3,2,1,0:T(8,128)S(1)} %collective-permute-done.36.theirs_ref, bf16[2,256,2048]{2,1,0:T(8,128)(2,1)S(1)} %copy-done), custom_call_target="tpu_custom_call" | custom-call | tf_op jit(solution)/shard_map/tmat_apply/pallas_call | solution.py:146
  (82 shorter events, 25.9 us)
Async XLA Ops:
  9.6 10.6 %collective-permute-start.1 = (f32[2,2,32,256]{3,2,1,0:T(8,128)}, f32[2,2,32,256]{3,2,1,0:T(8,128)S(1)}, u32[]{:S(2)}, u32[]{:S(2)}) collective-permute-start(f32[2,2,32,256]{3,2,1,0:T(8,128)} %tmat_apply.3.own_ref.refs_3_), channel_id=1, source_target_pairs={{0,2},{2,0},{4,6},{6,4},{8,10},{10,8},{12,14},{14,12},{16,18},{18,... | collective-permute-start | bytes 393224 | tf_op jit(solution)/shard_map/ppermute | solution.py:422
  12.5 7.7 %collective-permute-start.2 = (f32[2,2,32,256]{3,2,1,0:T(8,128)}, f32[2,2,32,256]{3,2,1,0:T(8,128)S(1)}, u32[]{:S(2)}, u32[]{:S(2)}) collective-permute-start(f32[2,2,32,256]{3,2,1,0:T(8,128)} %tmat_apply.3.own_ref.refs_3_), channel_id=1, source_target_pairs={{0,4},{2,6},{4,0},{6,2},{8,12},{10,14},{12,8},{14,10},{16,20},{18,... | collective-permute-start | bytes 393224 | tf_op jit(solution)/shard_map/ppermute | solution.py:422
  20.2 9.2 %collective-permute-start.4 = (f32[5,2,32,256]{3,2,1,0:T(8,128)S(1)}, f32[5,2,32,256]{3,2,1,0:T(8,128)S(1)}, u32[]{:S(2)}, u32[]{:S(2)}) collective-permute-start(f32[5,2,32,256]{3,2,1,0:T(8,128)S(1)} %get-tuple-element.43), channel_id=1, source_target_pairs={{0,2},{2,0},{4,6},{6,4},{8,10},{10,8},{12,14},{14,12},{16,18},{18,... | collective-permute-start | bytes 983048 | tf_op jit(solution)/shard_map/ppermute | solution.py:422
  20.3 9.1 %collective-permute-start.5 = (f32[5,2,32,256]{3,2,1,0:T(8,128)S(1)}, f32[5,2,32,256]{3,2,1,0:T(8,128)S(1)}, u32[]{:S(2)}, u32[]{:S(2)}) collective-permute-start(f32[5,2,32,256]{3,2,1,0:T(8,128)S(1)} %get-tuple-element.44), channel_id=1, source_target_pairs={{0,4},{2,6},{4,0},{6,2},{8,12},{10,14},{12,8},{14,10},{16,20},{18,... | collective-permute-start | bytes 983048 | tf_op jit(solution)/shard_map/ppermute | solution.py:422
  29.6 17.8 %collective-permute-start.10 = (f32[8,2,32,256]{3,2,1,0:T(8,128)S(1)}, f32[8,2,32,256]{3,2,1,0:T(8,128)S(1)}, u32[]{:S(2)}, u32[]{:S(2)}) collective-permute-start(f32[8,2,32,256]{3,2,1,0:T(8,128)S(1)} %get-tuple-element.52), channel_id=1, source_target_pairs={{0,4},{2,6},{4,0},{6,2},{8,12},{10,14},{12,8},{14,10},{16,20},{18,... | collective-permute-start | bytes 1572872 | tf_op jit(solution)/shard_map/ppermute | solution.py:422
  31.9 15.5 %collective-permute-start.9 = (f32[8,2,32,256]{3,2,1,0:T(8,128)S(1)}, f32[8,2,32,256]{3,2,1,0:T(8,128)S(1)}, u32[]{:S(2)}, u32[]{:S(2)}) collective-permute-start(f32[8,2,32,256]{3,2,1,0:T(8,128)S(1)} %get-tuple-element.51), channel_id=1, source_target_pairs={{0,2},{2,0},{4,6},{6,4},{8,10},{10,8},{12,14},{14,12},{16,18},{18,... | collective-permute-start | bytes 1572872 | tf_op jit(solution)/shard_map/ppermute | solution.py:422
  32.7 9.9 %collective-permute-start.6 = (f32[2,2,32,256]{3,2,1,0:T(8,128)S(1)}, f32[2,2,32,256]{3,2,1,0:T(8,128)S(1)}, u32[]{:S(2)}, u32[]{:S(2)}) collective-permute-start(f32[2,2,32,256]{3,2,1,0:T(8,128)S(1)} %get-tuple-element.47.own_ref), channel_id=1, source_target_pairs={{0,24},{2,26},{4,28},{6,30},{8,0},{10,2},{12,4},{14,6},{16,8},{18,... | collective-permute-start | bytes 393224 | tf_op jit(solution)/shard_map/ppermute | solution.py:428
  36.1 11.3 %collective-permute-start.7 = (f32[2,2,32,256]{3,2,1,0:T(8,128)S(1)}, f32[2,2,32,256]{3,2,1,0:T(8,128)S(1)}, u32[]{:S(2)}, u32[]{:S(2)}) collective-permute-start(f32[2,2,32,256]{3,2,1,0:T(8,128)S(1)} %get-tuple-element.47.own_ref), channel_id=1, source_target_pairs={{0,16},{2,18},{4,20},{6,22},{8,24},{10,26},{12,28},{14,30},{16,0},... | collective-permute-start | bytes 393224 | tf_op jit(solution)/shard_map/ppermute | solution.py:428
  36.1 11.3 %collective-permute-start.8 = (f32[2,2,32,256]{3,2,1,0:T(8,128)S(1)}, f32[2,2,32,256]{3,2,1,0:T(8,128)S(1)}, u32[]{:S(2)}, u32[]{:S(2)}) collective-permute-start(f32[2,2,32,256]{3,2,1,0:T(8,128)S(1)} %get-tuple-element.47.own_ref), channel_id=1, source_target_pairs={{0,8},{2,10},{4,12},{6,14},{8,16},{10,18},{12,20},{14,22},{16,24},... | collective-permute-start | bytes 393224 | tf_op jit(solution)/shard_map/ppermute | solution.py:428
  47.5 10.4 %collective-permute-start.11 = (f32[6,2,32,256]{3,2,1,0:T(8,128)S(1)}, f32[6,2,32,256]{3,2,1,0:T(8,128)S(1)}, u32[]{:S(2)}, u32[]{:S(2)}) collective-permute-start(f32[6,2,32,256]{3,2,1,0:T(8,128)S(1)} %get-tuple-element.54), channel_id=1, source_target_pairs={{0,2},{2,0},{4,6},{6,4},{8,10},{10,8},{12,14},{14,12},{16,18},{18,... | collective-permute-start | bytes 1179656 | tf_op jit(solution)/shard_map/ppermute | solution.py:422
  48.4 10.2 %collective-permute-start.12 = (f32[6,2,32,256]{3,2,1,0:T(8,128)S(1)}, f32[6,2,32,256]{3,2,1,0:T(8,128)S(1)}, u32[]{:S(2)}, u32[]{:S(2)}) collective-permute-start(f32[6,2,32,256]{3,2,1,0:T(8,128)S(1)} %get-tuple-element.55), channel_id=1, source_target_pairs={{0,4},{2,6},{4,0},{6,2},{8,12},{10,14},{12,8},{14,10},{16,20},{18,... | collective-permute-start | bytes 1179656 | tf_op jit(solution)/shard_map/ppermute | solution.py:422
  49.7 8.3 %collective-permute-start.13 = (f32[2,2,32,256]{3,2,1,0:T(8,128)S(1)}, f32[2,2,32,256]{3,2,1,0:T(8,128)S(1)}, u32[]{:S(2)}, u32[]{:S(2)}) collective-permute-start(f32[2,2,32,256]{3,2,1,0:T(8,128)S(1)} %get-tuple-element.56), channel_id=1, source_target_pairs={{0,16},{2,18},{4,20},{6,22},{8,24},{10,26},{12,28},{14,30},{16,0},... | collective-permute-start | bytes 393224 | tf_op jit(solution)/shard_map/ppermute | solution.py:428
  58.7 10.5 %collective-permute-start.14 = (f32[3,2,32,256]{3,2,1,0:T(8,128)S(1)}, f32[3,2,32,256]{3,2,1,0:T(8,128)S(1)}, u32[]{:S(2)}, u32[]{:S(2)}) collective-permute-start(f32[3,2,32,256]{3,2,1,0:T(8,128)S(1)} %get-tuple-element.58), channel_id=1, source_target_pairs={{0,2},{2,0},{4,6},{6,4},{8,10},{10,8},{12,14},{14,12},{16,18},{18,... | collective-permute-start | bytes 589832 | tf_op jit(solution)/shard_map/ppermute | solution.py:422
  59.5 9.7 %collective-permute-start.15 = (f32[3,2,32,256]{3,2,1,0:T(8,128)S(1)}, f32[3,2,32,256]{3,2,1,0:T(8,128)S(1)}, u32[]{:S(2)}, u32[]{:S(2)}) collective-permute-start(f32[3,2,32,256]{3,2,1,0:T(8,128)S(1)} %get-tuple-element.59), channel_id=1, source_target_pairs={{0,4},{2,6},{4,0},{6,2},{8,12},{10,14},{12,8},{14,10},{16,20},{18,... | collective-permute-start | bytes 589832 | tf_op jit(solution)/shard_map/ppermute | solution.py:422
  60.2 12.2 %collective-permute-start.16 = (f32[2,2,32,256]{3,2,1,0:T(8,128)S(1)}, f32[2,2,32,256]{3,2,1,0:T(8,128)S(1)}, u32[]{:S(2)}, u32[]{:S(2)}) collective-permute-start(f32[2,2,32,256]{3,2,1,0:T(8,128)S(1)} %get-tuple-element.60), channel_id=1, source_target_pairs={{0,8},{2,10},{4,12},{6,14},{8,16},{10,18},{12,20},{14,22},{16,24},... | collective-permute-start | bytes 393224 | tf_op jit(solution)/shard_map/ppermute | solution.py:428
  61.3 11.1 %collective-permute-start.17 = (f32[2,2,32,256]{3,2,1,0:T(8,128)S(1)}, f32[2,2,32,256]{3,2,1,0:T(8,128)S(1)}, u32[]{:S(2)}, u32[]{:S(2)}) collective-permute-start(f32[2,2,32,256]{3,2,1,0:T(8,128)S(1)} %get-tuple-element.61), channel_id=1, source_target_pairs={{0,24},{2,26},{4,28},{6,30},{8,0},{10,2},{12,4},{14,6},{16,8},{18,... | collective-permute-start | bytes 393224 | tf_op jit(solution)/shard_map/ppermute | solution.py:428
  75.2 5.8 %collective-permute-start.19 = (f32[2,2,32,256]{3,2,1,0:T(8,128)S(1)}, f32[2,2,32,256]{3,2,1,0:T(8,128)S(1)}, u32[]{:S(2)}, u32[]{:S(2)}) collective-permute-start(f32[2,2,32,256]{3,2,1,0:T(8,128)S(1)} %tmat_apply.4.own_ref.refs_3_), channel_id=1, source_target_pairs={{0,2},{2,0},{4,6},{6,4},{8,10},{10,8},{12,14},{14,12},{16,18},{18,... | collective-permute-start | bytes 393224 | tf_op jit(solution)/shard_map/ppermute | solution.py:422
  75.2 6.4 %collective-permute-start.20 = (f32[2,2,32,256]{3,2,1,0:T(8,128)S(1)}, f32[2,2,32,256]{3,2,1,0:T(8,128)S(1)}, u32[]{:S(2)}, u32[]{:S(2)}) collective-permute-start(f32[2,2,32,256]{3,2,1,0:T(8,128)S(1)} %tmat_apply.4.own_ref.refs_3_), channel_id=1, source_target_pairs={{0,4},{2,6},{4,0},{6,2},{8,12},{10,14},{12,8},{14,10},{16,20},{18,... | collective-permute-start | bytes 393224 | tf_op jit(solution)/shard_map/ppermute | solution.py:422
  81.6 9.2 %collective-permute-start.22 = (f32[5,2,32,256]{3,2,1,0:T(8,128)S(1)}, f32[5,2,32,256]{3,2,1,0:T(8,128)S(1)}, u32[]{:S(2)}, u32[]{:S(2)}) collective-permute-start(f32[5,2,32,256]{3,2,1,0:T(8,128)S(1)} %get-tuple-element.62), channel_id=1, source_target_pairs={{0,2},{2,0},{4,6},{6,4},{8,10},{10,8},{12,14},{14,12},{16,18},{18,... | collective-permute-start | bytes 983048 | tf_op jit(solution)/shard_map/ppermute | solution.py:422
  83.3 8.9 %collective-permute-start.23 = (f32[5,2,32,256]{3,2,1,0:T(8,128)S(1)}, f32[5,2,32,256]{3,2,1,0:T(8,128)S(1)}, u32[]{:S(2)}, u32[]{:S(2)}) collective-permute-start(f32[5,2,32,256]{3,2,1,0:T(8,128)S(1)} %get-tuple-element.63), channel_id=1, source_target_pairs={{0,4},{2,6},{4,0},{6,2},{8,12},{10,14},{12,8},{14,10},{16,20},{18,... | collective-permute-start | bytes 983048 | tf_op jit(solution)/shard_map/ppermute | solution.py:422
  92.4 13.2 %collective-permute-start.27 = (f32[8,2,32,256]{3,2,1,0:T(8,128)S(1)}, f32[8,2,32,256]{3,2,1,0:T(8,128)S(1)}, u32[]{:S(2)}, u32[]{:S(2)}) collective-permute-start(f32[8,2,32,256]{3,2,1,0:T(8,128)S(1)} %get-tuple-element.65), channel_id=1, source_target_pairs={{0,2},{2,0},{4,6},{6,4},{8,10},{10,8},{12,14},{14,12},{16,18},{18,... | collective-permute-start | bytes 1572872 | tf_op jit(solution)/shard_map/ppermute | solution.py:422
  92.8 12.8 %collective-permute-start.28 = (f32[8,2,32,256]{3,2,1,0:T(8,128)S(1)}, f32[8,2,32,256]{3,2,1,0:T(8,128)S(1)}, u32[]{:S(2)}, u32[]{:S(2)}) collective-permute-start(f32[8,2,32,256]{3,2,1,0:T(8,128)S(1)} %get-tuple-element.66), channel_id=1, source_target_pairs={{0,4},{2,6},{4,0},{6,2},{8,12},{10,14},{12,8},{14,10},{16,20},{18,... | collective-permute-start | bytes 1572872 | tf_op jit(solution)/shard_map/ppermute | solution.py:422
  94.4 5.4 %collective-permute-start.24 = (f32[2,2,32,256]{3,2,1,0:T(8,128)S(1)}, f32[2,2,32,256]{3,2,1,0:T(8,128)S(1)}, u32[]{:S(2)}, u32[]{:S(2)}) collective-permute-start(f32[2,2,32,256]{3,2,1,0:T(8,128)S(1)} %get-tuple-element.64.own_ref), channel_id=1, source_target_pairs={{0,24},{2,26},{4,28},{6,30},{8,0},{10,2},{12,4},{14,6},{16,8},{18,... | collective-permute-start | bytes 393224 | tf_op jit(solution)/shard_map/ppermute | solution.py:428
  94.4 11.1 %collective-permute-start.25 = (f32[2,2,32,256]{3,2,1,0:T(8,128)S(1)}, f32[2,2,32,256]{3,2,1,0:T(8,128)S(1)}, u32[]{:S(2)}, u32[]{:S(2)}) collective-permute-start(f32[2,2,32,256]{3,2,1,0:T(8,128)S(1)} %get-tuple-element.64.own_ref), channel_id=1, source_target_pairs={{0,16},{2,18},{4,20},{6,22},{8,24},{10,26},{12,28},{14,30},{16,0},... | collective-permute-start | bytes 393224 | tf_op jit(solution)/shard_map/ppermute | solution.py:428
  95.6 9.9 %collective-permute-start.26 = (f32[2,2,32,256]{3,2,1,0:T(8,128)S(1)}, f32[2,2,32,256]{3,2,1,0:T(8,128)S(1)}, u32[]{:S(2)}, u32[]{:S(2)}) collective-permute-start(f32[2,2,32,256]{3,2,1,0:T(8,128)S(1)} %get-tuple-element.64.own_ref), channel_id=1, source_target_pairs={{0,8},{2,10},{4,12},{6,14},{8,16},{10,18},{12,20},{14,22},{16,24},... | collective-permute-start | bytes 393224 | tf_op jit(solution)/shard_map/ppermute | solution.py:428
  105.7 9.0 %collective-permute-start.29 = (f32[6,2,32,256]{3,2,1,0:T(8,128)S(1)}, f32[6,2,32,256]{3,2,1,0:T(8,128)S(1)}, u32[]{:S(2)}, u32[]{:S(2)}) collective-permute-start(f32[6,2,32,256]{3,2,1,0:T(8,128)S(1)} %get-tuple-element.68), channel_id=1, source_target_pairs={{0,2},{2,0},{4,6},{6,4},{8,10},{10,8},{12,14},{14,12},{16,18},{18,... | collective-permute-start | bytes 1179656 | tf_op jit(solution)/shard_map/ppermute | solution.py:422
  106.9 7.8 %collective-permute-start.30 = (f32[6,2,32,256]{3,2,1,0:T(8,128)S(1)}, f32[6,2,32,256]{3,2,1,0:T(8,128)S(1)}, u32[]{:S(2)}, u32[]{:S(2)}) collective-permute-start(f32[6,2,32,256]{3,2,1,0:T(8,128)S(1)} %get-tuple-element.69), channel_id=1, source_target_pairs={{0,4},{2,6},{4,0},{6,2},{8,12},{10,14},{12,8},{14,10},{16,20},{18,... | collective-permute-start | bytes 1179656 | tf_op jit(solution)/shard_map/ppermute | solution.py:422
  107.9 6.8 %collective-permute-start.31 = (f32[2,2,32,256]{3,2,1,0:T(8,128)S(1)}, f32[2,2,32,256]{3,2,1,0:T(8,128)S(1)}, u32[]{:S(2)}, u32[]{:S(2)}) collective-permute-start(f32[2,2,32,256]{3,2,1,0:T(8,128)S(1)} %get-tuple-element.70), channel_id=1, source_target_pairs={{0,16},{2,18},{4,20},{6,22},{8,24},{10,26},{12,28},{14,30},{16,0},... | collective-permute-start | bytes 393224 | tf_op jit(solution)/shard_map/ppermute | solution.py:428
  114.7 11.7 %collective-permute-start.32 = (f32[3,2,32,256]{3,2,1,0:T(8,128)S(1)}, f32[3,2,32,256]{3,2,1,0:T(8,128)S(1)}, u32[]{:S(2)}, u32[]{:S(2)}) collective-permute-start(f32[3,2,32,256]{3,2,1,0:T(8,128)S(1)} %get-tuple-element.72), channel_id=1, source_target_pairs={{0,2},{2,0},{4,6},{6,4},{8,10},{10,8},{12,14},{14,12},{16,18},{18,... | collective-permute-start | bytes 589832 | tf_op jit(solution)/shard_map/ppermute | solution.py:422
  115.7 10.8 %collective-permute-start.33 = (f32[3,2,32,256]{3,2,1,0:T(8,128)S(1)}, f32[3,2,32,256]{3,2,1,0:T(8,128)S(1)}, u32[]{:S(2)}, u32[]{:S(2)}) collective-permute-start(f32[3,2,32,256]{3,2,1,0:T(8,128)S(1)} %get-tuple-element.73), channel_id=1, source_target_pairs={{0,4},{2,6},{4,0},{6,2},{8,12},{10,14},{12,8},{14,10},{16,20},{18,... | collective-permute-start | bytes 589832 | tf_op jit(solution)/shard_map/ppermute | solution.py:422
  117.6 12.1 %collective-permute-start.34 = (f32[2,2,32,256]{3,2,1,0:T(8,128)S(1)}, f32[2,2,32,256]{3,2,1,0:T(8,128)S(1)}, u32[]{:S(2)}, u32[]{:S(2)}) collective-permute-start(f32[2,2,32,256]{3,2,1,0:T(8,128)S(1)} %get-tuple-element.74), channel_id=1, source_target_pairs={{0,8},{2,10},{4,12},{6,14},{8,16},{10,18},{12,20},{14,22},{16,24},... | collective-permute-start | bytes 393224 | tf_op jit(solution)/shard_map/ppermute | solution.py:428
  118.3 11.4 %collective-permute-start.35 = (f32[2,2,32,256]{3,2,1,0:T(8,128)S(1)}, f32[2,2,32,256]{3,2,1,0:T(8,128)S(1)}, u32[]{:S(2)}, u32[]{:S(2)}) collective-permute-start(f32[2,2,32,256]{3,2,1,0:T(8,128)S(1)} %get-tuple-element.75), channel_id=1, source_target_pairs={{0,24},{2,26},{4,28},{6,30},{8,0},{10,2},{12,4},{14,6},{16,8},{18,... | collective-permute-start | bytes 393224 | tf_op jit(solution)/shard_map/ppermute | solution.py:428
  (12 other events, 58.6 us)

commit v3 on v2

--- a/solution.py
+++ b/solution.py
@@ -14,7 +14,7 @@
 BF16 = jnp.bfloat16
 MIB = 1 << 20
 STREAM_LIMIT = 48 * MIB
-ALONE_LIMIT = 63 * MIB
+ALONE_LIMIT = 61 * MIB
 GROUPS = 5
 VMEM = pl.BlockSpec(memory_space=pltpu.VMEM)
 SMEM = pl.BlockSpec(memory_space=pltpu.SMEM)
@@ -78,7 +78,7 @@
         row = rows_of_ref[partners_ref[me * slots + slot]]
         owner, particle = lax.div(row, particles), lax.rem(row, particles)
         column = lax.bitwise_xor(lax.rem(owner, COLUMNS), my_column)
-        layer = lax.rem(lax.div(owner, COLUMNS) - my_layer + layers, layers)
+        layer = lax.bitwise_xor(lax.div(owner, COLUMNS), my_layer)
         near = jnp.where(column == COLUMNS - 1, 2, 1)
         far = jnp.where(column == COLUMNS - 1, 4, 3)
         group = jnp.where(column == 0, 0, jnp.where(layer == 0, near, far))
@@ -149,11 +149,7 @@
         in_specs=[SMEM, VMEM, VMEM, VMEM],
         out_specs=[VMEM] * count,
         scratch_shapes=[pltpu.VMEM((particles, 2, directions, 2 * half), F32)],
-        compiler_params=(
-            pltpu.CompilerParams(vmem_limit_bytes=ALONE_LIMIT - size_of(parts, theirs))
-            if halves
-            else params(3 * size_of(mine, theirs), size_of(parts))
-        ),
+        compiler_params=params(3 * size_of(mine, theirs), size_of(parts)),
         name="tmat_apply",
     )(side, mine, theirs, parts)
 
@@ -202,7 +198,7 @@
             fetch(early, early).start()
 
     for field_ref, side in ((own_ref, own_side), (other_ref, 1 - own_side)):
-        for row in range(field_ref.shape[0]):
+        for row in range(other_ref.shape[0]):
             with_real, with_imag = stacked_parts(field_ref[row, 0], field_ref[row, 1])
             for part, value in enumerate((with_real, with_imag)):
                 start = pl.multiple_of(part * width + side * half, half)
@@ -253,7 +249,7 @@
 
 
 def backward(first, groups, base, count, index, own_half, other_half, blocks, parts):
-    particles, _, directions, half = own_half.shape
+    particles, _, directions, half = other_half.shape
     width = 2 * half
     slots = blocks.shape[0]
     out_shape = [jax.ShapeDtypeStruct((count, 2, directions, half), F32)]
@@ -422,20 +418,13 @@
     return lax.ppermute(value, "owner", [(source, source ^ bit) for source in range(count)])
 
 
-def along(value, shift):
-    count = lax.axis_size("owner")
-    step = shift * COLUMNS
-    return lax.ppermute(
-        value, "owner", [(source, (source + step) % count) for source in range(count)]
-    )
-
-
 def scatter_step(incident, scattered, blocks, parts, index, side, layers):
     particles = incident.shape[0]
     every = range(particles)
     by_x = range((particles + 1) // 2)
     by_y = range((particles + 1) // 2, particles)
     rest = range(1, layers)
+    powers = [1 << step for step in range(layers.bit_length() - 1)]
     at = functools.partial(place_of, particles=particles, layers=layers)
     total_rows = COLUMNS * particles * layers
     first_n, first_d = at(1, 0, 0), at(3, 0, 0)
@@ -454,19 +443,37 @@
     if first:
         parts = made[0]
 
-    inputs = [products_d, x1, y1]
+    inputs = [products_d, x1, y1, scattered]
     x_plan = [[(0, row_of(particle, layer))] for particle in by_x for layer in range(layers)]
     y_plan = [[(0, row_of(particle, layer))] for particle in by_y for layer in range(layers)]
     x_head, y_head = len(x_plan), len(y_plan)
     x_plan += [[(2, particle)] for particle in by_y]
     y_plan += [[(1, particle)] for particle in by_x]
-    x2, y2 = pack("pack_second", inputs, [x_plan, y_plan])
+    x2, y2, copied = pack(
+        "pack_second", inputs, [x_plan, y_plan, [[(3, particle)] for particle in every]]
+    )
     x2, y2 = across(x2, 1), across(y2, 2)
+    reached = [across(copied, COLUMNS)]
     products_n, *made = backward(first, (1, 3), first_n, first_d - first_n, index, *fetched, parts)
     if first:
         parts = made[0]
 
-    inputs = [products_n, x2, y2, scattered]
+    def z_row(particle, layer):
+        step = layer.bit_length() - 1
+        return step, (layer - (1 << step)) * particles + particle
+
+    def z_rows(offset, own, count):
+        rows = []
+        for layer in range(count):
+            for particle in every:
+                if layer == 0:
+                    rows.append([(own, particle)])
+                else:
+                    step, row = z_row(particle, layer)
+                    rows.append([(offset + step, row)])
+        return rows
+
+    inputs = [products_n, x2, y2, scattered] + reached
     x_plan, y_plan = [], []
     for particle in every:
         for layer in range(layers):
@@ -478,29 +485,15 @@
                 x_terms.append((2, row_of(particle - len(by_x), layer)))
             x_plan.append(x_terms)
             y_plan.append(y_terms)
-    x3, y3, copied = pack(
-        "pack_third", inputs, [x_plan, y_plan, [[(3, particle)] for particle in every]]
-    )
+    x3, y3, known = pack("pack_third", inputs, [x_plan, y_plan, z_rows(4, 3, 2)])
     x3, y3 = across(x3, 1), across(y3, 2)
-    z3 = [along(copied, -shift) for shift in rest]
-    products_o, *made = backward(
-        first, (0,), 0, first_n, index, copied, other, blocks, parts
-    )
+    for bit in powers[1:]:
+        if bit > 2:
+            (known,) = pack("pack_layers", [scattered] + reached, [z_rows(1, 0, bit)])
+        reached.append(across(known, bit * COLUMNS))
+    products_o, *made = backward(first, (0,), 0, first_n, index, known, other, blocks, parts)
     if first:
         parts = made[0]
-
-    inputs = [products_o, x3, y3] + z3
-    tails = [[(2 + shift, particle)] for particle in every for shift in rest]
-    z_plans = [
-        [
-            [(number, row_of(particle, shift)) for number in range(3)]
-            for particle in every
-        ]
-        for shift in rest
-    ]
-    x4, y4, mark, *z4 = pack("pack_fourth", inputs, [tails, tails, [[(1, 0)]]] + z_plans)
-    x4, y4 = across(x4, 1), across(y4, 2)
-    z4 = [along(value, shift) for shift, value in zip(rest, z4)]
     copies = []
     for particle in every:
         copies.append((0, particle, at(1, particle, 0)))
@@ -509,44 +502,79 @@
             copies.append((3, y_head + particle, at(3, particle, 0)))
         else:
             copies.append((2, x_head + particle - len(by_x), at(3, particle, 0)))
-        for shift in rest:
-            copies.append((3 + shift, particle, at(0, particle, shift)))
-    near_first = forward(
-        (0, 1, 2), index, [x1, y1, x2, y2] + z3, tuple(copies), parts, particles, total_rows, [mark]
-    )
-
-    def tail(particle, shift):
-        return particle * len(rest) + shift - 1
+    near_level = forward(
+        (1, 2), index, [x1, y1, x2, y2], tuple(copies), parts, particles, total_rows, [known]
+    )
+
+    def summed(layer, particle, arrived):
+        terms = [(number, row_of(particle, layer)) for number in range(3)]
+        return terms + [(number, layer * particles + particle) for number in arrived]
+
+    def half_sums(bit, arrived):
+        return [summed(layer, particle, arrived) for layer in range(bit, 2 * bit) for particle in every]
+
+    inputs = [products_o, x3, y3] + reached
+    tails = []
+    for particle in every:
+        for layer in rest:
+            step, row = z_row(particle, layer)
+            tails.append([(3 + step, row)])
+    x4, y4, sums, mark = pack(
+        "pack_fourth",
+        inputs,
+        [tails, tails, half_sums(powers[-1], ()), [[(1, 0)]]],
+        [near_level],
+    )
+    x4, y4 = across(x4, 1), across(y4, 2)
+    arrived = [across(sums, powers[-1] * COLUMNS)]
+    copies = []
+    for particle in every:
+        for layer in rest:
+            step, row = z_row(particle, layer)
+            copies.append((step, row, at(0, particle, layer)))
+    near_column = forward(
+        (0,), index, reached, tuple(copies), parts, particles, total_rows, [mark]
+    )
+
+    def tail(particle, layer):
+        return particle * len(rest) + layer - 1
 
     x5, y5, mark = pack(
         "pack_fifth",
         [x4, y4],
         [
-            [[(1, tail(particle, shift))] for particle in by_y for shift in rest],
-            [[(0, tail(particle, shift))] for particle in by_x for shift in rest],
+            [[(1, tail(particle, layer))] for particle in by_y for layer in rest],
+            [[(0, tail(particle, layer))] for particle in by_x for layer in rest],
             [[(0, 0)]],
         ],
-        [near_first, z4[len(z4) // 2]],
+        [near_column],
     )
     x5, y5 = across(x5, 1), across(y5, 2)
+    for bit in powers[-2::-1]:
+        numbers = range(3, 3 + len(arrived))
+        (sums,) = pack(
+            "pack_sums", [products_o, x3, y3] + arrived, [half_sums(bit, numbers)], [mark]
+        )
+        arrived.append(across(sums, bit * COLUMNS))
     copies = []
     for particle in every:
-        for shift in rest:
-            copies.append((0, tail(particle, shift), at(1, particle, shift)))
-            copies.append((1, tail(particle, shift), at(2, particle, shift)))
+        for layer in rest:
+            copies.append((0, tail(particle, layer), at(1, particle, layer)))
+            copies.append((1, tail(particle, layer), at(2, particle, layer)))
     near_second = forward(
-        (3,), index, [x4, y4], tuple(copies), parts, particles, total_rows, [mark]
+        (3,), index, [x4, y4], tuple(copies), parts, particles, total_rows, [mark, sums]
     )
     copies = []
     for number, group in ((0, by_y), (1, by_x)):
         for order, particle in enumerate(group):
-            for shift in rest:
-                copies.append((number, tail(order, shift), at(3, particle, shift)))
+            for layer in rest:
+                copies.append((number, tail(order, layer), at(3, particle, layer)))
     near_last = forward(
         (4,), index, [x5, y5], tuple(copies), parts, particles, total_rows, [near_second]
     )
-    halves = [(products_o, layers), (x3, layers), (y3, layers)] + [(value, 1) for value in z4]
-    return whole_total(side, incident, [near_first, near_second, near_last], halves), parts
+    nears = [near_level, near_column, near_second, near_last]
+    halves = [(products_o, layers), (x3, layers), (y3, layers)] + [(value, 1) for value in arrived]
+    return whole_total(side, incident, nears, halves), parts
 
 
 def local(incident, tmat, blocks, block_rows, partners, live, owner_of):

time: 131 us -> 129 us (0.985); the launches traced: 133 us -> 127 us
  Pallas kernels: 63.6 us -> 42.5 us
  waiting for transfers between devices: 19.5 us -> 40.6 us
  starting transfers between devices: 46 us -> 39 us
    ppermute x20 -> x28, waiting for transfers between devices: 3.88 us -> 37.6 us  [across(): lax.ppermute(value, 'owner', [(source, source ^ bit) for source in range(...]
    ppermute x12 -> x0, starting transfers between devices: 19.1 us -> none  [along(): lax.ppermute(value, 'owner', [(source, (source + step) % count) for sourc...]
    ppermute x12 -> x0, waiting for transfers between devices: 12.5 us -> none  [along(): lax.ppermute(value, 'owner', [(source, (source + step) % count) for sourc...]
    ppermute x20 -> x28, starting transfers between devices: 26 us -> 38 us  [across(): lax.ppermute(value, 'owner', [(source, source ^ bit) for source in range(...]
    pallas_call x6, Pallas kernels: 27.6 us -> 16 us  [backward(): pl.pallas_call(functools.partial(backward_kernel, first, groups, base), o...]
    pallas_call x6 -> x8, Pallas kernels: 25.8 us -> 18.7 us  [forward(): pl.pallas_call(functools.partial(forward_kernel, groups, copies, len(fiel...]
    pallas_call x3, Pallas kernels: 5.71 us -> 3.29 us  [apply_tmat(): pl.pallas_call(functools.partial(tmat_kernel, halves), out_shape=[half_sh...]
    unnamed x14 -> x10, local copies, waits for them, and re-layouts: 2.28 us -> 3.18 us
  transfers between devices with their start and end apart: 37 -> 33, of which waited for: 12 -> 21; matrix products, arithmetic and copies ran while one was open for 0% -> 0% of each run, Pallas kernels for 43% -> 30%
where the time goes in v3:
time: 129 us; the launch traced here: 127 us
  Pallas kernels  42.5 us (33%)
  waiting for transfers between devices  40.6 us (31%)
  starting transfers between devices  39 us (30%)
  local copies, waits for them, and re-layouts  3.18 us (2%)
  between operations  1.59 us (1%)
    ppermute x28, starting transfers between devices, across(): lax.ppermute(value, 'owner', [(source, source ^ bit) for source in range(...  38 us
    ppermute x28, waiting for transfers between devices, across(): lax.ppermute(value, 'owner', [(source, source ^ bit) for source in range(...  37.6 us
    pallas_call x8, Pallas kernels, forward(): pl.pallas_call(functools.partial(forward_kernel, groups, copies, len(fiel...  18.7 us
    pallas_call x6, Pallas kernels, backward(): pl.pallas_call(functools.partial(backward_kernel, first, groups, base), o...  16 us
    pallas_call x1, Pallas kernels, prepare(): pl.pallas_call(functools.partial(prepare_kernel, layers, slots), out_shap...  3.72 us
    pallas_call x3, Pallas kernels, apply_tmat(): pl.pallas_call(functools.partial(tmat_kernel, halves), out_shape=[half_sh...  3.29 us
    unnamed x10, local copies, waits for them, and re-layouts  3.18 us
    ppermute x5, waiting for transfers between devices, from_other(): return lax.ppermute(value, 'pair', [(0, 1), (1, 0)])  3.05 us
  transfers between devices with their start and end apart: 33, of which 21 were waited for; matrix products, arithmetic and copies ran while one was open for 0% of the time, Pallas kernels for 30%

profile of v3, /device:TPU:0, one launch (start us, length us, event | category | flops | bytes accessed | tf_op | source)
XLA Modules:
  0.0 126.9 jit_solution(6380578170371816061)
XLA Ops:
  1.8 3.7 %prepare.1 = (bf16[2,256,2048]{2,1,0:T(8,128)(2,1)}, s32[321]{0:T(512)}) custom-call(s32[1]{0:T(128)} %bitcast.1.owner_ref, s32[1]{0:T(128)} %bitcast.side_ref, s32[336]{0:T(512)} %partners_ref.1, s32[32]{0:T(128)} %rows_of_ref.1, s32[21]{0:T(128)} %holders_ref.1, s32[1]{0:T(128)S(6)} %copy.13.live_ref, f32[2,2,256,512]{3,2,1,0:T(8,128)} %tmat_ref.1), custom_call_target="tpu_custom_call" | custom-call | tf_op jit(solution)/shard_map/prepare/pallas_call | solution.py:105
  5.5 1.6 %copy-done = bf16[2,256,2048]{2,1,0:T(8,128)(2,1)S(1)} copy-done((bf16[2,256,2048]{2,1,0:T(8,128)(2,1)S(1)}, bf16[2,256,2048]{2,1,0:T(8,128)(2,1)}, u32[]{:S(2)}) %copy-start) | copy-done | bytes 2097176
  9.0 2.9 %collective-permute-start.1 = (f32[2,2,32,256]{3,2,1,0:T(8,128)S(1)}, f32[2,2,32,256]{3,2,1,0:T(8,128)S(1)}, u32[]{:S(2)}, u32[]{:S(2)}) collective-permute-start(f32[2,2,32,256]{3,2,1,0:T(8,128)S(1)} %tmat_apply.3.own_ref.refs_3_), channel_id=1, source_target_pairs={{0,2},{2,0},{4,6},{6,4},{8,10},{10,8},{12,14},{14,12},{16,18},{18,... | collective-permute-start | bytes 393224 | tf_op jit(solution)/shard_map/ppermute | solution.py:418
  12.0 1.5 %collective-permute-start.2 = (f32[2,2,32,256]{3,2,1,0:T(8,128)S(1)}, f32[2,2,32,256]{3,2,1,0:T(8,128)S(1)}, u32[]{:S(2)}, u32[]{:S(2)}) collective-permute-start(f32[2,2,32,256]{3,2,1,0:T(8,128)S(1)} %tmat_apply.3.own_ref.refs_3_), channel_id=1, source_target_pairs={{0,4},{2,6},{4,0},{6,2},{8,12},{10,14},{12,8},{14,10},{16,20},{18,... | collective-permute-start | bytes 393224 | tf_op jit(solution)/shard_map/ppermute | solution.py:418
  17.2 2.2 %collective-permute-start.4 = (f32[5,2,32,256]{3,2,1,0:T(8,128)S(1)}, f32[5,2,32,256]{3,2,1,0:T(8,128)S(1)}, u32[]{:S(2)}, u32[]{:S(2)}) collective-permute-start(f32[5,2,32,256]{3,2,1,0:T(8,128)S(1)} %get-tuple-element.41), channel_id=1, source_target_pairs={{0,2},{2,0},{4,6},{6,4},{8,10},{10,8},{12,14},{14,12},{16,18},{18,... | collective-permute-start | bytes 983048 | tf_op jit(solution)/shard_map/ppermute | solution.py:418
  21.1 4.6 %backward_group1.2 = (f32[16,2,32,256]{3,2,1,0:T(8,128)S(1)}, bf16[21,2,2,512,256]{4,3,2,1,0:T(8,128)(2,1)}) custom-call(s32[321]{0:T(512)S(1)} %copy-done.4, f32[2,2,32,256]{3,2,1,0:T(8,128)S(1)} %tmat_apply.3.own_ref.refs_3_, f32[2,2,32,256]{3,2,1,0:T(8,128)S(1)} %collective-permute-done.3.other_ref, ...), custom_call_target="tpu_custom_call", output_to_operand_aliasing={{1}: (4, {})} | custom-call | flops 4194304 | bytes 131072 | tf_op jit(solution)/shard_map/backward_group1/pallas_call | solution.py:275
  28.4 3.7 %collective-permute-start.8 = (f32[8,2,32,256]{3,2,1,0:T(8,128)S(1)}, f32[8,2,32,256]{3,2,1,0:T(8,128)S(1)}, u32[]{:S(2)}, u32[]{:S(2)}) collective-permute-start(f32[8,2,32,256]{3,2,1,0:T(8,128)S(1)} %get-tuple-element.50), channel_id=1, source_target_pairs={{0,2},{2,0},{4,6},{6,4},{8,10},{10,8},{12,14},{14,12},{16,18},{18,... | collective-permute-start | bytes 1572872 | tf_op jit(solution)/shard_map/ppermute | solution.py:418
  32.1 2.8 %collective-permute-start.7 = (f32[4,2,32,256]{3,2,1,0:T(8,128)S(1)}, f32[4,2,32,256]{3,2,1,0:T(8,128)S(1)}, u32[]{:S(2)}, u32[]{:S(2)}) collective-permute-start(f32[4,2,32,256]{3,2,1,0:T(8,128)S(1)} %get-tuple-element.46.own_ref.refs_5_), channel_id=1, source_target_pairs={{0,16},{2,18},{4,20},{6,22},{8,24},{10,26},{12,28},{14,30},{16,0},... | collective-permute-start | bytes 786440 | tf_op jit(solution)/shard_map/ppermute | solution.py:418
  35.0 4.2 %backward_group0.2 = (f32[8,2,32,256]{3,2,1,0:T(8,128)S(1)}, bf16[21,2,2,512,256]{4,3,2,1,0:T(8,128)(2,1)}) custom-call(s32[321]{0:T(512)S(1)} %copy-done.4, f32[4,2,32,256]{3,2,1,0:T(8,128)S(1)} %get-tuple-element.46.own_ref.refs_5_, f32[2,2,32,256]{3,2,1,0:T(8,128)S(1)} %collective-permute-done.3.other_ref, ...), custom_call_target="tpu_custom_call", output_to_operand_aliasing={{1}: (4, {})} | custom-call | flops 4194304 | bytes 262144 | tf_op jit(solution)/shard_map/backward_group0/pallas_call | solution.py:275
  39.2 2.3 %forward_group1.2.refs_5_.refs_0_ = f32[2,2,32,512]{3,2,1,0:T(8,128)S(1)} custom-call(s32[321]{0:T(512)S(1)} %copy-done.4, f32[2,2,32,256]{3,2,1,0:T(8,128)S(1)} %collective-permute-done.1.refs_1_.refs_0_, f32[2,2,32,256]{3,2,1,0:T(8,128)S(1)} %collective-permute-done.2.refs_2_.refs_1_, f32[5,2,32,256]{3,2,1,0:T(8,128)S(1)} %collective-permute-done.4.refs_1_.refs_2_, ...), custom_call_target="tpu_custom_call" | custom-call | flops 4194304 | bytes 262144 | tf_op jit(solution)/shard_map/forward_group1/pallas_call | solution.py:340
  41.5 3.8 %collective-permute-done.7.refs_4_.refs_1_ = f32[4,2,32,256]{3,2,1,0:T(8,128)S(1)} collective-permute-done((f32[4,2,32,256]{3,2,1,0:T(8,128)S(1)}, f32[4,2,32,256]{3,2,1,0:T(8,128)S(1)}, u32[]{:S(2)}, u32[]{:S(2)}) %collective-permute-start.7) | collective-permute-done | bytes 262176 | tf_op jit(solution)/shard_map/ppermute | solution.py:418
  48.7 3.2 %forward_group0.2.refs_2_.refs_1_ = f32[2,2,32,512]{3,2,1,0:T(8,128)S(1)} custom-call(s32[321]{0:T(512)S(1)} %copy-done.4, f32[2,2,32,256]{3,2,1,0:T(8,128)S(1)} %collective-permute-done.6.refs_4_.refs_3_.refs_0_, f32[4,2,32,256]{3,2,1,0:T(8,128)S(1)} %collective-permute-done.7.refs_4_.refs_1_, ...), custom_call_target="tpu_custom_call" | custom-call | flops 4194304 | bytes 262144 | tf_op jit(solution)/shard_map/forward_group0/pallas_call | solution.py:340
  51.9 3.5 %collective-permute-done.10.refs_0_ = f32[6,2,32,256]{3,2,1,0:T(8,128)S(1)} collective-permute-done((f32[6,2,32,256]{3,2,1,0:T(8,128)S(1)}, f32[6,2,32,256]{3,2,1,0:T(8,128)S(1)}, u32[]{:S(2)}, u32[]{:S(2)}) %collective-permute-start.10) | collective-permute-done | bytes 393248 | tf_op jit(solution)/shard_map/ppermute | solution.py:418
  58.6 1.9 %collective-permute-done.12.refs_3_.refs_7_ = f32[4,2,32,256]{3,2,1,0:T(8,128)S(1)} collective-permute-done((f32[4,2,32,256]{3,2,1,0:T(8,128)S(1)}, f32[4,2,32,256]{3,2,1,0:T(8,128)S(1)}, u32[]{:S(2)}, u32[]{:S(2)}) %collective-permute-start.12) | collective-permute-done | bytes 262176 | tf_op jit(solution)/shard_map/ppermute | solution.py:418
  60.6 3.2 %forward_group3.2.refs_3_.refs_2_ = f32[2,2,32,512]{3,2,1,0:T(8,128)S(1)} custom-call(s32[321]{0:T(512)S(1)} %copy-done.4, f32[6,2,32,256]{3,2,1,0:T(8,128)S(1)} %collective-permute-done.10.refs_0_, f32[6,2,32,256]{3,2,1,0:T(8,128)S(1)} %collective-permute-done.11.refs_1_, bf16[21,2,2,512,256]{4,3,2,1,0:T(8,128)(2,1)} %get-tuple-element.48.refs_4_.refs_2_.blocks_ref, ...), custom_call_target="tpu_custom_call" | custom-call | flops 4194304 | bytes 262144 | tf_op jit(solution)/shard_map/forward_group3/pallas_call | solution.py:340
  65.8 1.5 %collective-permute-done.16.theirs_ref = f32[2,2,32,512]{3,2,1,0:T(8,128)S(1)} collective-permute-done((f32[2,2,32,512]{3,2,1,0:T(8,128)S(1)}, f32[2,2,32,512]{3,2,1,0:T(8,128)S(1)}, u32[]{:S(2)}, u32[]{:S(2)}) %collective-permute-start.16) | collective-permute-done | bytes 262176 | tf_op jit(solution)/shard_map/ppermute | solution.py:413
  68.4 4.8 %collective-permute-start.17 = (f32[2,2,32,256]{3,2,1,0:T(8,128)S(1)}, f32[2,2,32,256]{3,2,1,0:T(8,128)S(1)}, u32[]{:S(2)}, u32[]{:S(2)}) collective-permute-start(f32[2,2,32,256]{3,2,1,0:T(8,128)S(1)} %tmat_apply.4.own_ref.refs_3_), channel_id=1, source_target_pairs={{0,2},{2,0},{4,6},{6,4},{8,10},{10,8},{12,14},{14,12},{16,18},{18,... | collective-permute-start | bytes 393224 | tf_op jit(solution)/shard_map/ppermute | solution.py:418
  74.6 2.7 %collective-permute-done.17.refs_1_.refs_0_ = f32[2,2,32,256]{3,2,1,0:T(8,128)S(1)} collective-permute-done((f32[2,2,32,256]{3,2,1,0:T(8,128)S(1)}, f32[2,2,32,256]{3,2,1,0:T(8,128)S(1)}, u32[]{:S(2)}, u32[]{:S(2)}) %collective-permute-start.17) | collective-permute-done | bytes 131104 | tf_op jit(solution)/shard_map/ppermute | solution.py:418
  80.8 3.1 %backward_group1.3.refs_0_ = f32[16,2,32,256]{3,2,1,0:T(8,128)S(1)} custom-call(s32[321]{0:T(512)S(1)} %copy-done.4, f32[2,2,32,256]{3,2,1,0:T(8,128)S(1)} %tmat_apply.4.own_ref.refs_3_, f32[2,2,32,256]{3,2,1,0:T(8,128)S(1)} %collective-permute-done.19.other_ref, bf16[21,2,2,512,256]{4,3,2,1,0:T(8,128)(2,1)} %get-tuple-element.48.refs_4_.refs_2_.blocks_ref), custom_call_target="tpu_custom_call" | custom-call | flops 4194304 | bytes 131072 | tf_op jit(solution)/shard_map/backward_group1/pallas_call | solution.py:275
  84.7 3.0 %collective-permute-done.20.refs_1_.refs_2_ = f32[5,2,32,256]{3,2,1,0:T(8,128)S(1)} collective-permute-done((f32[5,2,32,256]{3,2,1,0:T(8,128)S(1)}, f32[5,2,32,256]{3,2,1,0:T(8,128)S(1)}, u32[]{:S(2)}, u32[]{:S(2)}) %collective-permute-start.20) | collective-permute-done | bytes 327712 | tf_op jit(solution)/shard_map/ppermute | solution.py:418
  88.1 1.5 %collective-permute-start.24 = (f32[8,2,32,256]{3,2,1,0:T(8,128)S(1)}, f32[8,2,32,256]{3,2,1,0:T(8,128)S(1)}, u32[]{:S(2)}, u32[]{:S(2)}) collective-permute-start(f32[8,2,32,256]{3,2,1,0:T(8,128)S(1)} %get-tuple-element.63), channel_id=1, source_target_pairs={{0,2},{2,0},{4,6},{6,4},{8,10},{10,8},{12,14},{14,12},{16,18},{18,... | collective-permute-start | bytes 1572872 | tf_op jit(solution)/shard_map/ppermute | solution.py:418
  90.2 3.2 %collective-permute-start.23 = (f32[4,2,32,256]{3,2,1,0:T(8,128)S(1)}, f32[4,2,32,256]{3,2,1,0:T(8,128)S(1)}, u32[]{:S(2)}, u32[]{:S(2)}) collective-permute-start(f32[4,2,32,256]{3,2,1,0:T(8,128)S(1)} %get-tuple-element.62.refs_5_.own_ref), channel_id=1, source_target_pairs={{0,16},{2,18},{4,20},{6,22},{8,24},{10,26},{12,28},{14,30},{16,0},... | collective-permute-start | bytes 786440 | tf_op jit(solution)/shard_map/ppermute | solution.py:418
  93.4 2.7 %backward_group0.3.refs_0_.refs_4_ = f32[8,2,32,256]{3,2,1,0:T(8,128)S(1)} custom-call(s32[321]{0:T(512)S(1)} %copy-done.4, f32[4,2,32,256]{3,2,1,0:T(8,128)S(1)} %get-tuple-element.62.refs_5_.own_ref, f32[2,2,32,256]{3,2,1,0:T(8,128)S(1)} %collective-permute-done.19.other_ref, bf16[21,2,2,512,256]{4,3,2,1,0:T(8,128)(2,1)} %get-tuple-element.48.refs_4_.refs_2_.blocks_ref), custom_call_target="tpu_custom_call" | custom-call | flops 4194304 | bytes 262144 | tf_op jit(solution)/shard_map/backward_group0/pallas_call | solution.py:275
  96.2 2.3 %forward_group1.3.refs_5_.refs_0_ = f32[2,2,32,512]{3,2,1,0:T(8,128)S(1)} custom-call(s32[321]{0:T(512)S(1)} %copy-done.4, f32[2,2,32,256]{3,2,1,0:T(8,128)S(1)} %collective-permute-done.17.refs_1_.refs_0_, f32[2,2,32,256]{3,2,1,0:T(8,128)S(1)} %collective-permute-done.18.refs_2_.refs_1_, f32[5,2,32,256]{3,2,1,0:T(8,128)S(1)} %collective-permute-done.20.refs_1_.refs_2_, ...), custom_call_target="tpu_custom_call" | custom-call | flops 4194304 | bytes 262144 | tf_op jit(solution)/shard_map/forward_group1/pallas_call | solution.py:340
  98.5 4.5 %collective-permute-done.23.refs_4_.refs_1_ = f32[4,2,32,256]{3,2,1,0:T(8,128)S(1)} collective-permute-done((f32[4,2,32,256]{3,2,1,0:T(8,128)S(1)}, f32[4,2,32,256]{3,2,1,0:T(8,128)S(1)}, u32[]{:S(2)}, u32[]{:S(2)}) %collective-permute-start.23) | collective-permute-done | bytes 262176 | tf_op jit(solution)/shard_map/ppermute | solution.py:418
  106.1 3.2 %forward_group0.3.refs_2_.refs_1_ = f32[2,2,32,512]{3,2,1,0:T(8,128)S(1)} custom-call(s32[321]{0:T(512)S(1)} %copy-done.4, f32[2,2,32,256]{3,2,1,0:T(8,128)S(1)} %collective-permute-done.22.refs_4_.refs_3_.refs_0_, f32[4,2,32,256]{3,2,1,0:T(8,128)S(1)} %collective-permute-done.23.refs_4_.refs_1_, ...), custom_call_target="tpu_custom_call" | custom-call | flops 4194304 | bytes 262144 | tf_op jit(solution)/shard_map/forward_group0/pallas_call | solution.py:340
  109.4 4.4 %collective-permute-done.26.refs_0_ = f32[6,2,32,256]{3,2,1,0:T(8,128)S(1)} collective-permute-done((f32[6,2,32,256]{3,2,1,0:T(8,128)S(1)}, f32[6,2,32,256]{3,2,1,0:T(8,128)S(1)}, u32[]{:S(2)}, u32[]{:S(2)}) %collective-permute-start.26) | collective-permute-done | bytes 393248 | tf_op jit(solution)/shard_map/ppermute | solution.py:418
  116.6 1.5 %collective-permute-done.28.refs_3_.refs_7_ = f32[4,2,32,256]{3,2,1,0:T(8,128)S(1)} collective-permute-done((f32[4,2,32,256]{3,2,1,0:T(8,128)S(1)}, f32[4,2,32,256]{3,2,1,0:T(8,128)S(1)}, u32[]{:S(2)}, u32[]{:S(2)}) %collective-permute-start.28) | collective-permute-done | bytes 262176 | tf_op jit(solution)/shard_map/ppermute | solution.py:418
  118.2 3.2 %forward_group3.3.refs_3_.refs_2_ = f32[2,2,32,512]{3,2,1,0:T(8,128)S(1)} custom-call(s32[321]{0:T(512)S(1)} %copy-done.4, f32[6,2,32,256]{3,2,1,0:T(8,128)S(1)} %collective-permute-done.26.refs_0_, f32[6,2,32,256]{3,2,1,0:T(8,128)S(1)} %collective-permute-done.27.refs_1_, bf16[21,2,2,512,256]{4,3,2,1,0:T(8,128)(2,1)} %get-tuple-element.48.refs_4_.refs_2_.blocks_ref, ...), custom_call_target="tpu_custom_call" | custom-call | flops 4194304 | bytes 262144 | tf_op jit(solution)/shard_map/forward_group3/pallas_call | solution.py:340
  122.1 1.5 %collective-permute-done.31.refs_8_ = f32[2,2,32,256]{3,2,1,0:T(8,128)S(1)} collective-permute-done((f32[2,2,32,256]{3,2,1,0:T(8,128)S(1)}, f32[2,2,32,256]{3,2,1,0:T(8,128)S(1)}, u32[]{:S(2)}, u32[]{:S(2)}) %collective-permute-start.31) | collective-permute-done | bytes 131104 | tf_op jit(solution)/shard_map/ppermute | solution.py:418
  123.8 1.5 %collective-permute-done.32.theirs_ref = f32[2,2,32,512]{3,2,1,0:T(8,128)S(1)} collective-permute-done((f32[2,2,32,512]{3,2,1,0:T(8,128)S(1)}, f32[2,2,32,512]{3,2,1,0:T(8,128)S(1)}, u32[]{:S(2)}, u32[]{:S(2)}) %collective-permute-start.32) | collective-permute-done | bytes 262176 | tf_op jit(solution)/shard_map/ppermute | solution.py:413
  125.4 1.5 %tmat_apply.5 = (f32[2,2,32,256]{3,2,1,0:T(8,128)}, f32[2,2,32,256]{3,2,1,0:T(8,128)}) custom-call(s32[1]{0:T(128)} %bitcast.side_ref, f32[2,2,32,512]{3,2,1,0:T(8,128)S(1)} %total.3.mine_ref, f32[2,2,32,512]{3,2,1,0:T(8,128)S(1)} %collective-permute-done.32.theirs_ref, bf16[2,256,2048]{2,1,0:T(8,128)(2,1)S(1)} %copy-done.1), custom_call_target="tpu_custom_call" | custom-call | tf_op jit(solution)/shard_map/tmat_apply/pallas_call | solution.py:146
  (74 shorter events, 34.1 us)
Async XLA Ops:
  0.6 4.9 %collective-permute-start = (f32[2,2,32,256]{3,2,1,0:T(8,128)}, f32[2,2,32,256]{3,2,1,0:T(8,128)S(1)}, u32[]{:S(2)}, u32[]{:S(2)}) collective-permute-start(f32[2,2,32,256]{3,2,1,0:T(8,128)} %incident_ref.3), channel_id=1, source_target_pairs={{0,1},{1,0},{2,3},{3,2},{4,5},{5,4},{6,7},{7,6},{8,9},{9,8},{10,11... | collective-permute-start | bytes 393224 | tf_op jit(solution)/shard_map/ppermute | solution.py:413
  8.9 4.6 %collective-permute-start.3 = (f32[2,2,32,256]{3,2,1,0:T(8,128)S(1)}, f32[2,2,32,256]{3,2,1,0:T(8,128)S(1)}, u32[]{:S(2)}, u32[]{:S(2)}) collective-permute-start(f32[2,2,32,256]{3,2,1,0:T(8,128)S(1)} %tmat_apply.3.own_ref.refs_3_), channel_id=1, source_target_pairs={{0,1},{1,0},{2,3},{3,2},{4,5},{5,4},{6,7},{7,6},{8,9},{9,8},{10,11... | collective-permute-start | bytes 393224 | tf_op jit(solution)/shard_map/ppermute | solution.py:413
  9.0 6.7 %collective-permute-start.1 = (f32[2,2,32,256]{3,2,1,0:T(8,128)S(1)}, f32[2,2,32,256]{3,2,1,0:T(8,128)S(1)}, u32[]{:S(2)}, u32[]{:S(2)}) collective-permute-start(f32[2,2,32,256]{3,2,1,0:T(8,128)S(1)} %tmat_apply.3.own_ref.refs_3_), channel_id=1, source_target_pairs={{0,2},{2,0},{4,6},{6,4},{8,10},{10,8},{12,14},{14,12},{16,18},{18,... | collective-permute-start | bytes 393224 | tf_op jit(solution)/shard_map/ppermute | solution.py:418
  12.0 5.2 %collective-permute-start.2 = (f32[2,2,32,256]{3,2,1,0:T(8,128)S(1)}, f32[2,2,32,256]{3,2,1,0:T(8,128)S(1)}, u32[]{:S(2)}, u32[]{:S(2)}) collective-permute-start(f32[2,2,32,256]{3,2,1,0:T(8,128)S(1)} %tmat_apply.3.own_ref.refs_3_), channel_id=1, source_target_pairs={{0,4},{2,6},{4,0},{6,2},{8,12},{10,14},{12,8},{14,10},{16,20},{18,... | collective-permute-start | bytes 393224 | tf_op jit(solution)/shard_map/ppermute | solution.py:418
  17.2 9.6 %collective-permute-start.4 = (f32[5,2,32,256]{3,2,1,0:T(8,128)S(1)}, f32[5,2,32,256]{3,2,1,0:T(8,128)S(1)}, u32[]{:S(2)}, u32[]{:S(2)}) collective-permute-start(f32[5,2,32,256]{3,2,1,0:T(8,128)S(1)} %get-tuple-element.41), channel_id=1, source_target_pairs={{0,2},{2,0},{4,6},{6,4},{8,10},{10,8},{12,14},{14,12},{16,18},{18,... | collective-permute-start | bytes 983048 | tf_op jit(solution)/shard_map/ppermute | solution.py:418
  19.5 8.9 %collective-permute-start.5 = (f32[5,2,32,256]{3,2,1,0:T(8,128)S(1)}, f32[5,2,32,256]{3,2,1,0:T(8,128)S(1)}, u32[]{:S(2)}, u32[]{:S(2)}) collective-permute-start(f32[5,2,32,256]{3,2,1,0:T(8,128)S(1)} %get-tuple-element.42), channel_id=1, source_target_pairs={{0,4},{2,6},{4,0},{6,2},{8,12},{10,14},{12,8},{14,10},{16,20},{18,... | collective-permute-start | bytes 983048 | tf_op jit(solution)/shard_map/ppermute | solution.py:418
  19.8 5.9 %collective-permute-start.6 = (f32[2,2,32,256]{3,2,1,0:T(8,128)S(1)}, f32[2,2,32,256]{3,2,1,0:T(8,128)S(1)}, u32[]{:S(2)}, u32[]{:S(2)}) collective-permute-start(f32[2,2,32,256]{3,2,1,0:T(8,128)S(1)} %get-tuple-element.45), channel_id=1, source_target_pairs={{0,8},{2,10},{4,12},{6,14},{8,0},{10,2},{12,4},{14,6},{16,24},{18,... | collective-permute-start | bytes 393224 | tf_op jit(solution)/shard_map/ppermute | solution.py:418
  28.4 16.8 %collective-permute-start.8 = (f32[8,2,32,256]{3,2,1,0:T(8,128)S(1)}, f32[8,2,32,256]{3,2,1,0:T(8,128)S(1)}, u32[]{:S(2)}, u32[]{:S(2)}) collective-permute-start(f32[8,2,32,256]{3,2,1,0:T(8,128)S(1)} %get-tuple-element.50), channel_id=1, source_target_pairs={{0,2},{2,0},{4,6},{6,4},{8,10},{10,8},{12,14},{14,12},{16,18},{18,... | collective-permute-start | bytes 1572872 | tf_op jit(solution)/shard_map/ppermute | solution.py:418
  32.1 13.1 %collective-permute-start.9 = (f32[8,2,32,256]{3,2,1,0:T(8,128)S(1)}, f32[8,2,32,256]{3,2,1,0:T(8,128)S(1)}, u32[]{:S(2)}, u32[]{:S(2)}) collective-permute-start(f32[8,2,32,256]{3,2,1,0:T(8,128)S(1)} %get-tuple-element.51), channel_id=1, source_target_pairs={{0,4},{2,6},{4,0},{6,2},{8,12},{10,14},{12,8},{14,10},{16,20},{18,... | collective-permute-start | bytes 1572872 | tf_op jit(solution)/shard_map/ppermute | solution.py:418
  32.1 13.1 %collective-permute-start.7 = (f32[4,2,32,256]{3,2,1,0:T(8,128)S(1)}, f32[4,2,32,256]{3,2,1,0:T(8,128)S(1)}, u32[]{:S(2)}, u32[]{:S(2)}) collective-permute-start(f32[4,2,32,256]{3,2,1,0:T(8,128)S(1)} %get-tuple-element.46.own_ref.refs_5_), channel_id=1, source_target_pairs={{0,16},{2,18},{4,20},{6,22},{8,24},{10,26},{12,28},{14,30},{16,0},... | collective-permute-start | bytes 786440 | tf_op jit(solution)/shard_map/ppermute | solution.py:418
  45.3 10.0 %collective-permute-start.10 = (f32[6,2,32,256]{3,2,1,0:T(8,128)S(1)}, f32[6,2,32,256]{3,2,1,0:T(8,128)S(1)}, u32[]{:S(2)}, u32[]{:S(2)}) collective-permute-start(f32[6,2,32,256]{3,2,1,0:T(8,128)S(1)} %get-tuple-element.53), channel_id=1, source_target_pairs={{0,2},{2,0},{4,6},{6,4},{8,10},{10,8},{12,14},{14,12},{16,18},{18,... | collective-permute-start | bytes 1179656 | tf_op jit(solution)/shard_map/ppermute | solution.py:418
  46.6 10.1 %collective-permute-start.11 = (f32[6,2,32,256]{3,2,1,0:T(8,128)S(1)}, f32[6,2,32,256]{3,2,1,0:T(8,128)S(1)}, u32[]{:S(2)}, u32[]{:S(2)}) collective-permute-start(f32[6,2,32,256]{3,2,1,0:T(8,128)S(1)} %get-tuple-element.54), channel_id=1, source_target_pairs={{0,4},{2,6},{4,0},{6,2},{8,12},{10,14},{12,8},{14,10},{16,20},{18,... | collective-permute-start | bytes 1179656 | tf_op jit(solution)/shard_map/ppermute | solution.py:418
  47.5 13.0 %collective-permute-start.12 = (f32[4,2,32,256]{3,2,1,0:T(8,128)S(1)}, f32[4,2,32,256]{3,2,1,0:T(8,128)S(1)}, u32[]{:S(2)}, u32[]{:S(2)}) collective-permute-start(f32[4,2,32,256]{3,2,1,0:T(8,128)S(1)} %get-tuple-element.56), channel_id=1, source_target_pairs={{0,16},{2,18},{4,20},{6,22},{8,24},{10,26},{12,28},{14,30},{16,0},... | collective-permute-start | bytes 786440 | tf_op jit(solution)/shard_map/ppermute | solution.py:418
  56.8 7.1 %collective-permute-start.13 = (f32[3,2,32,256]{3,2,1,0:T(8,128)S(1)}, f32[3,2,32,256]{3,2,1,0:T(8,128)S(1)}, u32[]{:S(2)}, u32[]{:S(2)}) collective-permute-start(f32[3,2,32,256]{3,2,1,0:T(8,128)S(1)} %get-tuple-element.57), channel_id=1, source_target_pairs={{0,2},{2,0},{4,6},{6,4},{8,10},{10,8},{12,14},{14,12},{16,18},{18,... | collective-permute-start | bytes 589832 | tf_op jit(solution)/shard_map/ppermute | solution.py:418
  57.2 6.6 %collective-permute-start.14 = (f32[3,2,32,256]{3,2,1,0:T(8,128)S(1)}, f32[3,2,32,256]{3,2,1,0:T(8,128)S(1)}, u32[]{:S(2)}, u32[]{:S(2)}) collective-permute-start(f32[3,2,32,256]{3,2,1,0:T(8,128)S(1)} %get-tuple-element.58), channel_id=1, source_target_pairs={{0,4},{2,6},{4,0},{6,2},{8,12},{10,14},{12,8},{14,10},{16,20},{18,... | collective-permute-start | bytes 589832 | tf_op jit(solution)/shard_map/ppermute | solution.py:418
  60.5 5.0 %collective-permute-start.15 = (f32[2,2,32,256]{3,2,1,0:T(8,128)S(1)}, f32[2,2,32,256]{3,2,1,0:T(8,128)S(1)}, u32[]{:S(2)}, u32[]{:S(2)}) collective-permute-start(f32[2,2,32,256]{3,2,1,0:T(8,128)S(1)} %pack_sums.2.refs_4_), channel_id=1, source_target_pairs={{0,8},{2,10},{4,12},{6,14},{8,0},{10,2},{12,4},{14,6},{16,24},{18,... | collective-permute-start | bytes 393224 | tf_op jit(solution)/shard_map/ppermute | solution.py:418
  65.7 1.6 %collective-permute-start.16 = (f32[2,2,32,512]{3,2,1,0:T(8,128)S(1)}, f32[2,2,32,512]{3,2,1,0:T(8,128)S(1)}, u32[]{:S(2)}, u32[]{:S(2)}) collective-permute-start(f32[2,2,32,512]{3,2,1,0:T(8,128)S(1)} %total.2.mine_ref), channel_id=1, source_target_pairs={{0,1},{1,0},{2,3},{3,2},{4,5},{5,4},{6,7},{7,6},{8,9},{9,8},{10,11... | collective-permute-start | bytes 786440 | tf_op jit(solution)/shard_map/ppermute | solution.py:413
  68.2 5.7 %collective-permute-start.19 = (f32[2,2,32,256]{3,2,1,0:T(8,128)S(1)}, f32[2,2,32,256]{3,2,1,0:T(8,128)S(1)}, u32[]{:S(2)}, u32[]{:S(2)}) collective-permute-start(f32[2,2,32,256]{3,2,1,0:T(8,128)S(1)} %tmat_apply.4.own_ref.refs_3_), channel_id=1, source_target_pairs={{0,1},{1,0},{2,3},{3,2},{4,5},{5,4},{6,7},{7,6},{8,9},{9,8},{10,11... | collective-permute-start | bytes 393224 | tf_op jit(solution)/shard_map/ppermute | solution.py:413
  68.4 8.9 %collective-permute-start.17 = (f32[2,2,32,256]{3,2,1,0:T(8,128)S(1)}, f32[2,2,32,256]{3,2,1,0:T(8,128)S(1)}, u32[]{:S(2)}, u32[]{:S(2)}) collective-permute-start(f32[2,2,32,256]{3,2,1,0:T(8,128)S(1)} %tmat_apply.4.own_ref.refs_3_), channel_id=1, source_target_pairs={{0,2},{2,0},{4,6},{6,4},{8,10},{10,8},{12,14},{14,12},{16,18},{18,... | collective-permute-start | bytes 393224 | tf_op jit(solution)/shard_map/ppermute | solution.py:418
  73.2 5.5 %collective-permute-start.18 = (f32[2,2,32,256]{3,2,1,0:T(8,128)S(1)}, f32[2,2,32,256]{3,2,1,0:T(8,128)S(1)}, u32[]{:S(2)}, u32[]{:S(2)}) collective-permute-start(f32[2,2,32,256]{3,2,1,0:T(8,128)S(1)} %tmat_apply.4.own_ref.refs_3_), channel_id=1, source_target_pairs={{0,4},{2,6},{4,0},{6,2},{8,12},{10,14},{12,8},{14,10},{16,20},{18,... | collective-permute-start | bytes 393224 | tf_op jit(solution)/shard_map/ppermute | solution.py:418
  78.7 8.9 %collective-permute-start.20 = (f32[5,2,32,256]{3,2,1,0:T(8,128)S(1)}, f32[5,2,32,256]{3,2,1,0:T(8,128)S(1)}, u32[]{:S(2)}, u32[]{:S(2)}) collective-permute-start(f32[5,2,32,256]{3,2,1,0:T(8,128)S(1)} %get-tuple-element.59), channel_id=1, source_target_pairs={{0,2},{2,0},{4,6},{6,4},{8,10},{10,8},{12,14},{14,12},{16,18},{18,... | collective-permute-start | bytes 983048 | tf_op jit(solution)/shard_map/ppermute | solution.py:418
  79.1 8.9 %collective-permute-start.21 = (f32[5,2,32,256]{3,2,1,0:T(8,128)S(1)}, f32[5,2,32,256]{3,2,1,0:T(8,128)S(1)}, u32[]{:S(2)}, u32[]{:S(2)}) collective-permute-start(f32[5,2,32,256]{3,2,1,0:T(8,128)S(1)} %get-tuple-element.60), channel_id=1, source_target_pairs={{0,4},{2,6},{4,0},{6,2},{8,12},{10,14},{12,8},{14,10},{16,20},{18,... | collective-permute-start | bytes 983048 | tf_op jit(solution)/shard_map/ppermute | solution.py:418
  79.7 5.0 %collective-permute-start.22 = (f32[2,2,32,256]{3,2,1,0:T(8,128)S(1)}, f32[2,2,32,256]{3,2,1,0:T(8,128)S(1)}, u32[]{:S(2)}, u32[]{:S(2)}) collective-permute-start(f32[2,2,32,256]{3,2,1,0:T(8,128)S(1)} %get-tuple-element.61), channel_id=1, source_target_pairs={{0,8},{2,10},{4,12},{6,14},{8,0},{10,2},{12,4},{14,6},{16,24},{18,... | collective-permute-start | bytes 393224 | tf_op jit(solution)/shard_map/ppermute | solution.py:418
  88.1 14.8 %collective-permute-start.24 = (f32[8,2,32,256]{3,2,1,0:T(8,128)S(1)}, f32[8,2,32,256]{3,2,1,0:T(8,128)S(1)}, u32[]{:S(2)}, u32[]{:S(2)}) collective-permute-start(f32[8,2,32,256]{3,2,1,0:T(8,128)S(1)} %get-tuple-element.63), channel_id=1, source_target_pairs={{0,2},{2,0},{4,6},{6,4},{8,10},{10,8},{12,14},{14,12},{16,18},{18,... | collective-permute-start | bytes 1572872 | tf_op jit(solution)/shard_map/ppermute | solution.py:418
  89.6 13.4 %collective-permute-start.25 = (f32[8,2,32,256]{3,2,1,0:T(8,128)S(1)}, f32[8,2,32,256]{3,2,1,0:T(8,128)S(1)}, u32[]{:S(2)}, u32[]{:S(2)}) collective-permute-start(f32[8,2,32,256]{3,2,1,0:T(8,128)S(1)} %get-tuple-element.64), channel_id=1, source_target_pairs={{0,4},{2,6},{4,0},{6,2},{8,12},{10,14},{12,8},{14,10},{16,20},{18,... | collective-permute-start | bytes 1572872 | tf_op jit(solution)/shard_map/ppermute | solution.py:418
  90.2 12.7 %collective-permute-start.23 = (f32[4,2,32,256]{3,2,1,0:T(8,128)S(1)}, f32[4,2,32,256]{3,2,1,0:T(8,128)S(1)}, u32[]{:S(2)}, u32[]{:S(2)}) collective-permute-start(f32[4,2,32,256]{3,2,1,0:T(8,128)S(1)} %get-tuple-element.62.refs_5_.own_ref), channel_id=1, source_target_pairs={{0,16},{2,18},{4,20},{6,22},{8,24},{10,26},{12,28},{14,30},{16,0},... | collective-permute-start | bytes 786440 | tf_op jit(solution)/shard_map/ppermute | solution.py:418
  103.0 10.7 %collective-permute-start.26 = (f32[6,2,32,256]{3,2,1,0:T(8,128)S(1)}, f32[6,2,32,256]{3,2,1,0:T(8,128)S(1)}, u32[]{:S(2)}, u32[]{:S(2)}) collective-permute-start(f32[6,2,32,256]{3,2,1,0:T(8,128)S(1)} %get-tuple-element.66), channel_id=1, source_target_pairs={{0,2},{2,0},{4,6},{6,4},{8,10},{10,8},{12,14},{14,12},{16,18},{18,... | collective-permute-start | bytes 1179656 | tf_op jit(solution)/shard_map/ppermute | solution.py:418
  104.0 10.7 %collective-permute-start.27 = (f32[6,2,32,256]{3,2,1,0:T(8,128)S(1)}, f32[6,2,32,256]{3,2,1,0:T(8,128)S(1)}, u32[]{:S(2)}, u32[]{:S(2)}) collective-permute-start(f32[6,2,32,256]{3,2,1,0:T(8,128)S(1)} %get-tuple-element.67), channel_id=1, source_target_pairs={{0,4},{2,6},{4,0},{6,2},{8,12},{10,14},{12,8},{14,10},{16,20},{18,... | collective-permute-start | bytes 1179656 | tf_op jit(solution)/shard_map/ppermute | solution.py:418
  104.7 13.4 %collective-permute-start.28 = (f32[4,2,32,256]{3,2,1,0:T(8,128)S(1)}, f32[4,2,32,256]{3,2,1,0:T(8,128)S(1)}, u32[]{:S(2)}, u32[]{:S(2)}) collective-permute-start(f32[4,2,32,256]{3,2,1,0:T(8,128)S(1)} %get-tuple-element.69), channel_id=1, source_target_pairs={{0,16},{2,18},{4,20},{6,22},{8,24},{10,26},{12,28},{14,30},{16,0},... | collective-permute-start | bytes 786440 | tf_op jit(solution)/shard_map/ppermute | solution.py:418
  114.7 6.7 %collective-permute-start.29 = (f32[3,2,32,256]{3,2,1,0:T(8,128)S(1)}, f32[3,2,32,256]{3,2,1,0:T(8,128)S(1)}, u32[]{:S(2)}, u32[]{:S(2)}) collective-permute-start(f32[3,2,32,256]{3,2,1,0:T(8,128)S(1)} %get-tuple-element.70), channel_id=1, source_target_pairs={{0,2},{2,0},{4,6},{6,4},{8,10},{10,8},{12,14},{14,12},{16,18},{18,... | collective-permute-start | bytes 589832 | tf_op jit(solution)/shard_map/ppermute | solution.py:418
  115.6 5.9 %collective-permute-start.30 = (f32[3,2,32,256]{3,2,1,0:T(8,128)S(1)}, f32[3,2,32,256]{3,2,1,0:T(8,128)S(1)}, u32[]{:S(2)}, u32[]{:S(2)}) collective-permute-start(f32[3,2,32,256]{3,2,1,0:T(8,128)S(1)} %get-tuple-element.71), channel_id=1, source_target_pairs={{0,4},{2,6},{4,0},{6,2},{8,12},{10,14},{12,8},{14,10},{16,20},{18,... | collective-permute-start | bytes 589832 | tf_op jit(solution)/shard_map/ppermute | solution.py:418
  118.2 5.5 %collective-permute-start.31 = (f32[2,2,32,256]{3,2,1,0:T(8,128)S(1)}, f32[2,2,32,256]{3,2,1,0:T(8,128)S(1)}, u32[]{:S(2)}, u32[]{:S(2)}) collective-permute-start(f32[2,2,32,256]{3,2,1,0:T(8,128)S(1)} %pack_sums.3.refs_4_), channel_id=1, source_target_pairs={{0,8},{2,10},{4,12},{6,14},{8,0},{10,2},{12,4},{14,6},{16,24},{18,... | collective-permute-start | bytes 393224 | tf_op jit(solution)/shard_map/ppermute | solution.py:418
  (6 other events, 16.6 us)

commit v4 on v3

--- a/solution.py
+++ b/solution.py
@@ -14,7 +14,7 @@
 BF16 = jnp.bfloat16
 MIB = 1 << 20
 STREAM_LIMIT = 48 * MIB
-ALONE_LIMIT = 61 * MIB
+ALONE_LIMIT = 119 * MIB // 2
 GROUPS = 5
 VMEM = pl.BlockSpec(memory_space=pltpu.VMEM)
 SMEM = pl.BlockSpec(memory_space=pltpu.SMEM)
@@ -56,18 +56,12 @@
     return (column * particles + particle) * layers + layer
 
 
-def prepare_kernel(
-    layers, slots, owner_ref, side_ref, partners_ref, rows_of_ref, holders_ref, live_ref, tmat_ref, *refs
+def index_kernel(
+    layers, particles, owner_ref, side_ref, partners_ref, rows_of_ref, holders_ref, live_ref, *refs
 ):
-    parts_ref, index_ref, buf_ref, sems = refs
-    particles, _, half, width = tmat_ref.shape
+    index_ref = refs[-1]
+    slots = holders_ref.shape[0]
     stride, counts = GROUPS * slots, 3 * GROUPS * slots
-
-    def fetch(row):
-        return pltpu.make_async_copy(tmat_ref.at[row], buf_ref.at[row], sems.at[row])
-
-    for row in range(particles):
-        fetch(row).start()
     me = owner_ref[0]
     my_column, my_layer = lax.rem(me, COLUMNS), lax.div(me, COLUMNS)
     for group in range(GROUPS):
@@ -91,34 +85,58 @@
         return carry
 
     lax.fori_loop(0, live_ref[0], step, 0)
+
+
+def slot_index(my_owner, side, partners, owner_of, block_rows, live, layers, particles, after):
+    slots = block_rows.shape[0]
+    return pl.pallas_call(
+        functools.partial(index_kernel, layers, particles),
+        out_shape=jax.ShapeDtypeStruct((3 * GROUPS * slots + GROUPS + 1,), jnp.int32),
+        in_specs=[SMEM] * 6 + [ANY],
+        out_specs=SMEM,
+        name="slot_index",
+    )(my_owner, side, partners, owner_of, block_rows, live, after)
+
+
+def prepare_kernel(tmat_ref, incident_ref, parts_ref, copy_ref, buf_ref, sems):
+    particles, _, half, width = tmat_ref.shape
+
+    def fetch(row):
+        return pltpu.make_async_copy(tmat_ref.at[row], buf_ref.at[row], sems.at[row])
+
+    for row in range(particles):
+        fetch(row).start()
+    own = pltpu.make_async_copy(incident_ref, copy_ref, sems.at[particles])
+    own.start()
     for row in range(particles):
         fetch(row).wait()
         for part in range(2):
             high, low = split_value(buf_ref[row, part])
             parts_ref[row, :, part * width : (part + 1) * width] = high
             parts_ref[row, :, (2 + part) * width : (3 + part) * width] = low
-
-
-def prepare(my_owner, side, partners, owner_of, block_rows, live, tmat, layers):
+    own.wait()
+
+
+def prepare(tmat, incident):
     particles, _, half, width = tmat.shape
-    slots = block_rows.shape[0]
     return pl.pallas_call(
-        functools.partial(prepare_kernel, layers, slots),
+        prepare_kernel,
         out_shape=(
             jax.ShapeDtypeStruct((particles, half, 4 * width), BF16),
-            jax.ShapeDtypeStruct((3 * GROUPS * slots + GROUPS + 1,), jnp.int32),
+            jax.ShapeDtypeStruct(incident.shape, F32),
         ),
-        in_specs=[SMEM] * 6 + [HBM],
-        out_specs=(VMEM, SMEM),
-        scratch_shapes=[pltpu.VMEM(tmat.shape, F32), pltpu.SemaphoreType.DMA((particles,))],
+        in_specs=[HBM, HBM],
+        out_specs=(VMEM, VMEM),
+        scratch_shapes=[pltpu.VMEM(tmat.shape, F32), pltpu.SemaphoreType.DMA((particles + 1,))],
         compiler_params=pltpu.CompilerParams(vmem_limit_bytes=ALONE_LIMIT),
         name="prepare",
-    )(my_owner, side, partners, owner_of, block_rows, live, tmat)
+    )(tmat, incident)
 
 
 def tmat_kernel(halves, side_ref, mine_ref, theirs_ref, parts_ref, *refs):
-    exciting_ref = refs[0] if len(refs) == 3 else None
-    scattered_ref, full_ref = refs[-2:]
+    last = len(refs) == 4
+    exciting_ref = refs[0] if last else None
+    scattered_ref, full_ref = refs[1:3] if last else refs
     particles, _, directions, width = full_ref.shape
     half = width // 2
     start = pl.multiple_of(side_ref[0] * half, half)
@@ -127,6 +145,10 @@
         full_ref[:, :, :, pl.ds(pl.multiple_of(half - start, half), half)] = theirs_ref[...]
     else:
         full_ref[...] = mine_ref[...] + theirs_ref[...]
+    if last:
+        window = full_ref.at[:, :, :, pl.ds(start, half)]
+        leave = pltpu.make_async_copy(window, exciting_ref, refs[3])
+        leave.start()
     for row in range(particles):
         with_real, with_imag = stacked_parts(full_ref[row, 0], full_ref[row, 1])
         right = jnp.concatenate((with_real, with_imag, with_real, with_imag), axis=1)
@@ -134,21 +156,23 @@
         out = (total[:, : 2 * directions] + total[:, 2 * directions :]).T
         scattered_ref[row, 0] = out[:directions]
         scattered_ref[row, 1] = out[directions:]
-    if exciting_ref is not None:
-        exciting_ref[...] = full_ref[:, :, :, pl.ds(start, half)]
+    if last:
+        leave.wait()
 
 
 def apply_tmat(halves, last, side, mine, theirs, parts):
     particles, _, directions, _ = mine.shape
     half = parts.shape[1]
     half_shape = jax.ShapeDtypeStruct((particles, 2, directions, half), F32)
-    count = 2 if last else 1
+    scratch = [pltpu.VMEM((particles, 2, directions, 2 * half), F32)]
+    if last:
+        scratch.append(pltpu.SemaphoreType.DMA)
     return pl.pallas_call(
         functools.partial(tmat_kernel, halves),
-        out_shape=[half_shape] * count,
+        out_shape=[half_shape] * (2 if last else 1),
         in_specs=[SMEM, VMEM, VMEM, VMEM],
-        out_specs=[VMEM] * count,
-        scratch_shapes=[pltpu.VMEM((particles, 2, directions, 2 * half), F32)],
+        out_specs=[HBM, VMEM] if last else [VMEM],
+        scratch_shapes=scratch,
         compiler_params=params(3 * size_of(mine, theirs), size_of(parts)),
         name="tmat_apply",
     )(side, mine, theirs, parts)
@@ -316,9 +340,11 @@
         _, place, holder = at_turn(turn)
         with_real, with_imag = stacked_parts(every_ref[place, 0], every_ref[place, 1])
         fetch(turn, here).wait()
-        total = dot_nt(with_real, buf_ref[here, 0, 0]) + dot_nt(with_imag, buf_ref[here, 0, 1])
-        rest = dot_nt(with_real[: 2 * directions], buf_ref[here, 1, 0])
-        rest += dot_nt(with_imag[: 2 * directions], buf_ref[here, 1, 1])
+        left = jnp.concatenate((with_real, with_imag), axis=1)
+        high = jnp.concatenate((buf_ref[here, 0, 0], buf_ref[here, 0, 1]), axis=1)
+        low = jnp.concatenate((buf_ref[here, 1, 0], buf_ref[here, 1, 1]), axis=1)
+        total = dot_nt(left, high)
+        rest = dot_nt(left[: 2 * directions], low)
         acc_ref[holder] += total[: 2 * directions] + total[2 * directions :] + rest
 
         @pl.when(turn + BUFFERS < wanted)
@@ -436,6 +462,8 @@
     other = from_other(scattered)
     x1 = across(scattered, 1)
     y1 = across(scattered, 2)
+    reached = [across(scattered, COLUMNS)]
+    where = {1: (0, 0), 2: (1, 0), 3: (2, 0)}
     fetched = (scattered, other, blocks)
     products_d, *made = backward(
         first, (2, 4), first_d, total_rows - first_d, index, *fetched, parts
@@ -450,30 +478,22 @@
     x_plan += [[(2, particle)] for particle in by_y]
     y_plan += [[(1, particle)] for particle in by_x]
     x2, y2, copied = pack(
-        "pack_second", inputs, [x_plan, y_plan, [[(3, particle)] for particle in every]]
+        "pack_second",
+        inputs,
+        [x_plan, y_plan, [[(3, particle)] for particle in every]],
+        reached,
     )
     x2, y2 = across(x2, 1), across(y2, 2)
-    reached = [across(copied, COLUMNS)]
+    reached.append(across(copied, 2 * COLUMNS))
     products_n, *made = backward(first, (1, 3), first_n, first_d - first_n, index, *fetched, parts)
     if first:
         parts = made[0]
 
     def z_row(particle, layer):
-        step = layer.bit_length() - 1
-        return step, (layer - (1 << step)) * particles + particle
-
-    def z_rows(offset, own, count):
-        rows = []
-        for layer in range(count):
-            for particle in every:
-                if layer == 0:
-                    rows.append([(own, particle)])
-                else:
-                    step, row = z_row(particle, layer)
-                    rows.append([(offset + step, row)])
-        return rows
-
-    inputs = [products_n, x2, y2, scattered] + reached
+        number, start = where[layer]
+        return number, start + particle
+
+    inputs = [products_n, x2, y2, scattered, reached[0]]
     x_plan, y_plan = [], []
     for particle in every:
         for layer in range(layers):
@@ -485,13 +505,19 @@
                 x_terms.append((2, row_of(particle - len(by_x), layer)))
             x_plan.append(x_terms)
             y_plan.append(y_terms)
-    x3, y3, known = pack("pack_third", inputs, [x_plan, y_plan, z_rows(4, 3, 2)])
+    z_plans = [[[(number, particle)] for particle in every] for number in (3, 4)]
+    x3, y3, copied, known = pack("pack_third", inputs, [x_plan, y_plan] + z_plans, reached[1:])
     x3, y3 = across(x3, 1), across(y3, 2)
-    for bit in powers[1:]:
-        if bit > 2:
-            (known,) = pack("pack_layers", [scattered] + reached, [z_rows(1, 0, bit)])
+    reached.append(across(known, 2 * COLUMNS))
+    for bit in powers[2:]:
+        plan = [[(0, particle)] for particle in every]
+        for layer in range(1, bit):
+            plan += [[(1 + where[layer][0], where[layer][1] + particle)] for particle in every]
+        (known,) = pack("pack_layers", [scattered] + reached, [plan])
+        for layer in range(bit):
+            where[bit + layer] = (len(reached), layer * particles)
         reached.append(across(known, bit * COLUMNS))
-    products_o, *made = backward(first, (0,), 0, first_n, index, known, other, blocks, parts)
+    products_o, *made = backward(first, (0,), 0, first_n, index, copied, other, blocks, parts)
     if first:
         parts = made[0]
     copies = []
@@ -503,7 +529,14 @@
         else:
             copies.append((2, x_head + particle - len(by_x), at(3, particle, 0)))
     near_level = forward(
-        (1, 2), index, [x1, y1, x2, y2], tuple(copies), parts, particles, total_rows, [known]
+        (1, 2),
+        index,
+        [x1, y1, x2, y2],
+        tuple(copies),
+        parts,
+        particles,
+        total_rows,
+        [products_o],
     )
 
     def summed(layer, particle, arrived):
@@ -582,10 +615,11 @@
     my_owner = lax.axis_index("owner").astype(jnp.int32)[None]
     side = lax.axis_index("pair").astype(jnp.int32)[None]
     theirs = from_other(incident)
-    tmat_parts, index = prepare(
-        my_owner, side, partners, owner_of, block_rows, live, tmat, layers
-    )
+    tmat_parts, incident = prepare(tmat, incident)
     (scattered,) = apply_tmat(True, False, side, incident, theirs, tmat_parts)
+    index = slot_index(
+        my_owner, side, partners, owner_of, block_rows, live, layers, incident.shape[0], scattered
+    )
     parts = None
     for turn in range(ITERS):
         mine, parts = scatter_step(incident, scattered, blocks, parts, index, side, layers)

time: 129 us -> 130 us (level); the launches traced: 127 us -> 130 us
  waiting for transfers between devices: 40.6 us -> 14.3 us
  Pallas kernels: 42.5 us -> 66 us
  starting transfers between devices: 39 us -> 43.7 us
    ppermute x28 -> x30, waiting for transfers between devices: 37.6 us -> 11.3 us  [across(): lax.ppermute(value, 'owner', [(source, source ^ bit) for source in range(...]
    pallas_call x6, Pallas kernels: 16 us -> 27.8 us  [backward(): pl.pallas_call(functools.partial(backward_kernel, first, groups, base), o...]
    pallas_call x8, Pallas kernels: 18.7 us -> 29.3 us  [forward(): pl.pallas_call(functools.partial(forward_kernel, groups, copies, len(fiel...]
    ppermute x28 -> x30, starting transfers between devices: 38 us -> 42.7 us  [across(): lax.ppermute(value, 'owner', [(source, source ^ bit) for source in range(...]
    pallas_call x1 -> x2, Pallas kernels: 3.72 us -> 4.78 us  [the longest x1 3.05 us: prepare(): pl.pallas_call(prepare_kernel, out_shape=(jax.ShapeDtypeStruct((particles...]
    unnamed x10 -> x16, local copies, waits for them, and re-layouts: 3.18 us -> 4.09 us
  transfers between devices with their start and end apart: 33 -> 35, of which waited for: 21 -> 13; matrix products, arithmetic and copies ran while one was open for 0% -> 0% of each run, Pallas kernels for 30% -> 48%
where the time goes in v4:
time: 130 us
  Pallas kernels  66 us (51%)
  starting transfers between devices  43.7 us (34%)
  waiting for transfers between devices  14.3 us (11%)
  local copies, waits for them, and re-layouts  4.09 us (3%)
  between operations  1.76 us (1%)
    ppermute x30, starting transfers between devices, across(): lax.ppermute(value, 'owner', [(source, source ^ bit) for source in range(...  42.7 us
    pallas_call x8, Pallas kernels, forward(): pl.pallas_call(functools.partial(forward_kernel, groups, copies, len(fiel...  29.3 us
    pallas_call x6, Pallas kernels, backward(): pl.pallas_call(functools.partial(backward_kernel, first, groups, base), o...  27.8 us
    ppermute x30, waiting for transfers between devices, across(): lax.ppermute(value, 'owner', [(source, source ^ bit) for source in range(...  11.3 us
    unnamed x16, local copies, waits for them, and re-layouts  4.09 us
    pallas_call x3, Pallas kernels, apply_tmat(): pl.pallas_call(functools.partial(tmat_kernel, halves), out_shape=[half_sh...  3.3 us
    ppermute x5, waiting for transfers between devices, from_other(): return lax.ppermute(value, 'pair', [(0, 1), (1, 0)])  3.05 us
    pallas_call x1, Pallas kernels, prepare(): pl.pallas_call(prepare_kernel, out_shape=(jax.ShapeDtypeStruct((particles...  3.05 us
  transfers between devices with their start and end apart: 35, of which 13 were waited for; matrix products, arithmetic and copies ran while one was open for 0% of the time, Pallas kernels for 48%

profile of v4, /device:TPU:0, one launch (start us, length us, event | category | flops | bytes accessed | tf_op | source)
XLA Modules:
  0.0 129.9 jit_solution(16357382248231659804)
XLA Ops:
  1.1 3.0 %prepare.1 = (bf16[2,256,2048]{2,1,0:T(8,128)(2,1)}, f32[2,2,32,256]{3,2,1,0:T(8,128)}) custom-call(f32[2,2,256,512]{3,2,1,0:T(8,128)} %tmat_ref.1, f32[2,2,32,256]{3,2,1,0:T(8,128)} %incident_ref.1), custom_call_target="tpu_custom_call" | custom-call | tf_op jit(solution)/shard_map/prepare/pallas_call | solution.py:122
  4.2 1.6 %copy-done = bf16[2,256,2048]{2,1,0:T(8,128)(2,1)S(1)} copy-done((bf16[2,256,2048]{2,1,0:T(8,128)(2,1)S(1)}, bf16[2,256,2048]{2,1,0:T(8,128)(2,1)}, u32[]{:S(2)}) %copy-start) | copy-done | bytes 2097176
  7.7 3.0 %collective-permute-start.4 = (f32[2,2,32,256]{3,2,1,0:T(8,128)S(1)}, f32[2,2,32,256]{3,2,1,0:T(8,128)S(1)}, u32[]{:S(2)}, u32[]{:S(2)}) collective-permute-start(f32[2,2,32,256]{3,2,1,0:T(8,128)S(1)} %tmat_apply.3.refs_0_.own_ref.refs_3_), channel_id=1, source_target_pairs={{0,8},{2,10},{4,12},{6,14},{8,0},{10,2},{12,4},{14,6},{16,24},{18,... | collective-permute-start | bytes 393224 | tf_op jit(solution)/shard_map/ppermute | solution.py:444
  14.4 1.7 %slot_index.1.index_ref = s32[321]{0:T(512)} custom-call(s32[1]{0:T(128)} %bitcast.1.owner_ref, s32[1]{0:T(128)} %bitcast.side_ref, s32[336]{0:T(512)} %partners_ref.1, s32[32]{0:T(128)} %rows_of_ref.1, s32[21]{0:T(128)} %holders_ref.1, s32[1]{0:T(128)S(6)} %copy.13.live_ref, f32[2,2,32,256]{3,2,1,0:T(8,128)} %copy-done.2), custom_call_target="tpu_custom_call" | custom-call | tf_op jit(solution)/shard_map/slot_index/pallas_call | solution.py:92
  17.8 4.2 %backward_group2.2 = (f32[8,2,32,256]{3,2,1,0:T(8,128)S(1)}, bf16[21,2,2,512,256]{4,3,2,1,0:T(8,128)(2,1)}) custom-call(s32[321]{0:T(512)S(1)} %copy-done.6, f32[2,2,32,256]{3,2,1,0:T(8,128)S(1)} %copy-done.3, f32[2,2,32,256]{3,2,1,0:T(8,128)S(1)} %collective-permute-done.3.other_ref, f32[21,2,512,256]{3,2,1,0:T(8,128)} %blocks_ref.5), custom_call_target="tpu_custom_call" | custom-call | flops 4194304 | bytes 131072 | tf_op jit(solution)/shard_map/backward_group2/pallas_call | solution.py:299
  22.2 4.0 %collective-permute-start.7 = (f32[2,2,32,256]{3,2,1,0:T(8,128)S(1)}, f32[2,2,32,256]{3,2,1,0:T(8,128)S(1)}, u32[]{:S(2)}, u32[]{:S(2)}) collective-permute-start(f32[2,2,32,256]{3,2,1,0:T(8,128)S(1)} %get-tuple-element.47), channel_id=1, source_target_pairs={{0,16},{2,18},{4,20},{6,22},{8,24},{10,26},{12,28},{14,30},{16,0},... | collective-permute-start | bytes 393224 | tf_op jit(solution)/shard_map/ppermute | solution.py:444
  26.3 8.0 %backward_group1.2 = (f32[16,2,32,256]{3,2,1,0:T(8,128)S(1)}, bf16[21,2,2,512,256]{4,3,2,1,0:T(8,128)(2,1)}) custom-call(s32[321]{0:T(512)S(1)} %copy-done.6, f32[2,2,32,256]{3,2,1,0:T(8,128)S(1)} %copy-done.3, f32[2,2,32,256]{3,2,1,0:T(8,128)S(1)} %collective-permute-done.3.other_ref, ...), custom_call_target="tpu_custom_call", output_to_operand_aliasing={{1}: (4, {})} | custom-call | flops 4194304 | bytes 131072 | tf_op jit(solution)/shard_map/backward_group1/pallas_call | solution.py:299
  34.7 6.4 %collective-permute-start.8 = (f32[2,2,32,256]{3,2,1,0:T(8,128)S(1)}, f32[2,2,32,256]{3,2,1,0:T(8,128)S(1)}, u32[]{:S(2)}, u32[]{:S(2)}) collective-permute-start(f32[2,2,32,256]{3,2,1,0:T(8,128)S(1)} %get-tuple-element.52), channel_id=1, source_target_pairs={{0,16},{2,18},{4,20},{6,22},{8,24},{10,26},{12,28},{14,30},{16,0},... | collective-permute-start | bytes 393224 | tf_op jit(solution)/shard_map/ppermute | solution.py:444
  41.0 4.5 %backward_group0.2 = (f32[8,2,32,256]{3,2,1,0:T(8,128)S(1)}, bf16[21,2,2,512,256]{4,3,2,1,0:T(8,128)(2,1)}) custom-call(s32[321]{0:T(512)S(1)} %copy-done.6, f32[2,2,32,256]{3,2,1,0:T(8,128)S(1)} %get-tuple-element.48.own_ref, f32[2,2,32,256]{3,2,1,0:T(8,128)S(1)} %collective-permute-done.3.other_ref, ...), custom_call_target="tpu_custom_call", output_to_operand_aliasing={{1}: (4, {})} | custom-call | flops 4194304 | bytes 131072 | tf_op jit(solution)/shard_map/backward_group0/pallas_call | solution.py:299
  45.6 2.8 %forward_group1.2.refs_6_.refs_0_ = f32[2,2,32,512]{3,2,1,0:T(8,128)S(1)} custom-call(s32[321]{0:T(512)S(1)} %copy-done.6, f32[2,2,32,256]{3,2,1,0:T(8,128)S(1)} %collective-permute-done.1.refs_1_.refs_0_, f32[2,2,32,256]{3,2,1,0:T(8,128)S(1)} %collective-permute-done.2.refs_2_.refs_1_, f32[5,2,32,256]{3,2,1,0:T(8,128)S(1)} %collective-permute-done.5.refs_1_.refs_2_, ...), custom_call_target="tpu_custom_call" | custom-call | flops 4194304 | bytes 262144 | tf_op jit(solution)/shard_map/forward_group1/pallas_call | solution.py:366
  49.5 4.3 %collective-permute-start.13 = (f32[4,2,32,256]{3,2,1,0:T(8,128)S(1)}, f32[4,2,32,256]{3,2,1,0:T(8,128)S(1)}, u32[]{:S(2)}, u32[]{:S(2)}) collective-permute-start(f32[4,2,32,256]{3,2,1,0:T(8,128)S(1)} %get-tuple-element.59), channel_id=1, source_target_pairs={{0,16},{2,18},{4,20},{6,22},{8,24},{10,26},{12,28},{14,30},{16,0},... | collective-permute-start | bytes 786440 | tf_op jit(solution)/shard_map/ppermute | solution.py:444
  53.8 3.7 %forward_group0.2.refs_2_.refs_1_ = f32[2,2,32,512]{3,2,1,0:T(8,128)S(1)} custom-call(s32[321]{0:T(512)S(1)} %copy-done.6, f32[2,2,32,256]{3,2,1,0:T(8,128)S(1)} %collective-permute-done.4.refs_4_.refs_3_.refs_0_, f32[2,2,32,256]{3,2,1,0:T(8,128)S(1)} %collective-permute-done.7.refs_5_.refs_4_.refs_1_, ...), custom_call_target="tpu_custom_call" | custom-call | flops 4194304 | bytes 262144 | tf_op jit(solution)/shard_map/forward_group0/pallas_call | solution.py:366
  57.7 1.7 %collective-permute-start.14 = (f32[3,2,32,256]{3,2,1,0:T(8,128)S(1)}, f32[3,2,32,256]{3,2,1,0:T(8,128)S(1)}, u32[]{:S(2)}, u32[]{:S(2)}) collective-permute-start(f32[3,2,32,256]{3,2,1,0:T(8,128)S(1)} %get-tuple-element.60), channel_id=1, source_target_pairs={{0,2},{2,0},{4,6},{6,4},{8,10},{10,8},{12,14},{14,12},{16,18},{18,... | collective-permute-start | bytes 589832 | tf_op jit(solution)/shard_map/ppermute | solution.py:444
  59.5 1.8 %collective-permute-done.13.refs_3_.refs_7_ = f32[4,2,32,256]{3,2,1,0:T(8,128)S(1)} collective-permute-done((f32[4,2,32,256]{3,2,1,0:T(8,128)S(1)}, f32[4,2,32,256]{3,2,1,0:T(8,128)S(1)}, u32[]{:S(2)}, u32[]{:S(2)}) %collective-permute-start.13) | collective-permute-done | bytes 262176 | tf_op jit(solution)/shard_map/ppermute | solution.py:444
  61.5 5.5 %forward_group3.2.refs_3_.refs_2_ = f32[2,2,32,512]{3,2,1,0:T(8,128)S(1)} custom-call(s32[321]{0:T(512)S(1)} %copy-done.6, f32[6,2,32,256]{3,2,1,0:T(8,128)S(1)} %collective-permute-done.11.refs_0_, f32[6,2,32,256]{3,2,1,0:T(8,128)S(1)} %collective-permute-done.12.refs_1_, bf16[21,2,2,512,256]{4,3,2,1,0:T(8,128)(2,1)} %get-tuple-element.50.refs_4_.refs_3_.refs_2_.blocks_ref, ...), custom_call_target="tpu_custom_call" | custom-call | flops 4194304 | bytes 262144 | tf_op jit(solution)/shard_map/forward_group3/pallas_call | solution.py:366
  67.0 2.7 %forward_group4.2.refs_3_ = f32[2,2,32,512]{3,2,1,0:T(8,128)S(1)} custom-call(s32[321]{0:T(512)S(1)} %copy-done.7, f32[3,2,32,256]{3,2,1,0:T(8,128)S(1)} %collective-permute-done.14.refs_0_, f32[3,2,32,256]{3,2,1,0:T(8,128)S(1)} %collective-permute-done.15.refs_1_, bf16[21,2,2,512,256]{4,3,2,1,0:T(8,128)(2,1)} %get-tuple-element.50.refs_4_.refs_3_.refs_2_.blocks_ref, ...), custom_call_target="tpu_custom_call" | custom-call | flops 4194304 | bytes 262144 | tf_op jit(solution)/shard_map/forward_group4/pallas_call | solution.py:366
  72.9 3.7 %collective-permute-start.18 = (f32[2,2,32,256]{3,2,1,0:T(8,128)S(1)}, f32[2,2,32,256]{3,2,1,0:T(8,128)S(1)}, u32[]{:S(2)}, u32[]{:S(2)}) collective-permute-start(f32[2,2,32,256]{3,2,1,0:T(8,128)S(1)} %tmat_apply.4.own_ref.refs_3_), channel_id=1, source_target_pairs={{0,2},{2,0},{4,6},{6,4},{8,10},{10,8},{12,14},{14,12},{16,18},{18,... | collective-permute-start | bytes 393224 | tf_op jit(solution)/shard_map/ppermute | solution.py:444
  76.5 2.8 %backward_group2.3.refs_0_ = f32[8,2,32,256]{3,2,1,0:T(8,128)S(1)} custom-call(s32[321]{0:T(512)S(1)} %copy-done.7, f32[2,2,32,256]{3,2,1,0:T(8,128)S(1)} %tmat_apply.4.own_ref.refs_3_, f32[2,2,32,256]{3,2,1,0:T(8,128)S(1)} %collective-permute-done.20.other_ref, bf16[21,2,2,512,256]{4,3,2,1,0:T(8,128)(2,1)} %get-tuple-element.50.refs_4_.refs_3_.refs_2_.blocks_ref), custom_call_target="tpu_custom_call" | custom-call | flops 4194304 | bytes 131072 | tf_op jit(solution)/shard_map/backward_group2/pallas_call | solution.py:299
  80.0 1.8 %collective-permute-start.22 = (f32[5,2,32,256]{3,2,1,0:T(8,128)S(1)}, f32[5,2,32,256]{3,2,1,0:T(8,128)S(1)}, u32[]{:S(2)}, u32[]{:S(2)}) collective-permute-start(f32[5,2,32,256]{3,2,1,0:T(8,128)S(1)} %get-tuple-element.62), channel_id=1, source_target_pairs={{0,2},{2,0},{4,6},{6,4},{8,10},{10,8},{12,14},{14,12},{16,18},{18,... | collective-permute-start | bytes 983048 | tf_op jit(solution)/shard_map/ppermute | solution.py:444
  82.1 2.0 %collective-permute-start.24 = (f32[2,2,32,256]{3,2,1,0:T(8,128)S(1)}, f32[2,2,32,256]{3,2,1,0:T(8,128)S(1)}, u32[]{:S(2)}, u32[]{:S(2)}) collective-permute-start(f32[2,2,32,256]{3,2,1,0:T(8,128)S(1)} %get-tuple-element.64), channel_id=1, source_target_pairs={{0,16},{2,18},{4,20},{6,22},{8,24},{10,26},{12,28},{14,30},{16,0},... | collective-permute-start | bytes 393224 | tf_op jit(solution)/shard_map/ppermute | solution.py:444
  84.2 5.2 %backward_group1.3.refs_0_ = f32[16,2,32,256]{3,2,1,0:T(8,128)S(1)} custom-call(s32[321]{0:T(512)S(1)} %copy-done.7, f32[2,2,32,256]{3,2,1,0:T(8,128)S(1)} %tmat_apply.4.own_ref.refs_3_, f32[2,2,32,256]{3,2,1,0:T(8,128)S(1)} %collective-permute-done.20.other_ref, bf16[21,2,2,512,256]{4,3,2,1,0:T(8,128)(2,1)} %get-tuple-element.50.refs_4_.refs_3_.refs_2_.blocks_ref), custom_call_target="tpu_custom_call" | custom-call | flops 4194304 | bytes 131072 | tf_op jit(solution)/shard_map/backward_group1/pallas_call | solution.py:299
  92.1 2.5 %collective-permute-start.25 = (f32[2,2,32,256]{3,2,1,0:T(8,128)S(1)}, f32[2,2,32,256]{3,2,1,0:T(8,128)S(1)}, u32[]{:S(2)}, u32[]{:S(2)}) collective-permute-start(f32[2,2,32,256]{3,2,1,0:T(8,128)S(1)} %get-tuple-element.66), channel_id=1, source_target_pairs={{0,16},{2,18},{4,20},{6,22},{8,24},{10,26},{12,28},{14,30},{16,0},... | collective-permute-start | bytes 393224 | tf_op jit(solution)/shard_map/ppermute | solution.py:444
  94.7 3.1 %backward_group0.3.refs_5_.refs_0_.refs_4_ = f32[8,2,32,256]{3,2,1,0:T(8,128)S(1)} custom-call(s32[321]{0:T(512)S(1)} %copy-done.7, f32[2,2,32,256]{3,2,1,0:T(8,128)S(1)} %get-tuple-element.65.own_ref, f32[2,2,32,256]{3,2,1,0:T(8,128)S(1)} %collective-permute-done.20.other_ref, bf16[21,2,2,512,256]{4,3,2,1,0:T(8,128)(2,1)} %get-tuple-element.50.refs_4_.refs_3_.refs_2_.blocks_ref), custom_call_target="tpu_custom_call" | custom-call | flops 4194304 | bytes 131072 | tf_op jit(solution)/shard_map/backward_group0/pallas_call | solution.py:299
  97.7 2.8 %forward_group1.3.refs_6_.refs_0_ = f32[2,2,32,512]{3,2,1,0:T(8,128)S(1)} custom-call(s32[321]{0:T(512)S(1)} %copy-done.7, f32[2,2,32,256]{3,2,1,0:T(8,128)S(1)} %collective-permute-done.18.refs_1_.refs_0_, f32[2,2,32,256]{3,2,1,0:T(8,128)S(1)} %collective-permute-done.19.refs_2_.refs_1_, f32[5,2,32,256]{3,2,1,0:T(8,128)S(1)} %collective-permute-done.22.refs_1_.refs_2_, ...), custom_call_target="tpu_custom_call" | custom-call | flops 4194304 | bytes 262144 | tf_op jit(solution)/shard_map/forward_group1/pallas_call | solution.py:366
  100.5 2.6 %collective-permute-done.26.refs_1_.refs_5_ = f32[8,2,32,256]{3,2,1,0:T(8,128)S(1)} collective-permute-done((f32[8,2,32,256]{3,2,1,0:T(8,128)S(1)}, f32[8,2,32,256]{3,2,1,0:T(8,128)S(1)}, u32[]{:S(2)}, u32[]{:S(2)}) %collective-permute-start.26) | collective-permute-done | bytes 524320 | tf_op jit(solution)/shard_map/ppermute | solution.py:444
  103.3 1.7 %collective-permute-start.28 = (f32[6,2,32,256]{3,2,1,0:T(8,128)S(1)}, f32[6,2,32,256]{3,2,1,0:T(8,128)S(1)}, u32[]{:S(2)}, u32[]{:S(2)}) collective-permute-start(f32[6,2,32,256]{3,2,1,0:T(8,128)S(1)} %get-tuple-element.70), channel_id=1, source_target_pairs={{0,2},{2,0},{4,6},{6,4},{8,10},{10,8},{12,14},{14,12},{16,18},{18,... | collective-permute-start | bytes 1179656 | tf_op jit(solution)/shard_map/ppermute | solution.py:444
  107.3 3.6 %forward_group0.3.refs_2_.refs_1_ = f32[2,2,32,512]{3,2,1,0:T(8,128)S(1)} custom-call(s32[321]{0:T(512)S(1)} %copy-done.7, f32[2,2,32,256]{3,2,1,0:T(8,128)S(1)} %collective-permute-done.21.refs_4_.refs_3_.refs_0_, f32[2,2,32,256]{3,2,1,0:T(8,128)S(1)} %collective-permute-done.24.refs_5_.refs_4_.refs_1_, ...), custom_call_target="tpu_custom_call" | custom-call | flops 4194304 | bytes 262144 | tf_op jit(solution)/shard_map/forward_group0/pallas_call | solution.py:366
  114.2 1.6 %collective-permute-start.32 = (f32[3,2,32,256]{3,2,1,0:T(8,128)S(1)}, f32[3,2,32,256]{3,2,1,0:T(8,128)S(1)}, u32[]{:S(2)}, u32[]{:S(2)}) collective-permute-start(f32[3,2,32,256]{3,2,1,0:T(8,128)S(1)} %get-tuple-element.75), channel_id=1, source_target_pairs={{0,4},{2,6},{4,0},{6,2},{8,12},{10,14},{12,8},{14,10},{16,20},{18,... | collective-permute-start | bytes 589832 | tf_op jit(solution)/shard_map/ppermute | solution.py:444
  115.8 2.5 %collective-permute-done.30.refs_3_.refs_7_ = f32[4,2,32,256]{3,2,1,0:T(8,128)S(1)} collective-permute-done((f32[4,2,32,256]{3,2,1,0:T(8,128)S(1)}, f32[4,2,32,256]{3,2,1,0:T(8,128)S(1)}, u32[]{:S(2)}, u32[]{:S(2)}) %collective-permute-start.30) | collective-permute-done | bytes 262176 | tf_op jit(solution)/shard_map/ppermute | solution.py:444
  118.4 5.5 %forward_group3.3.refs_3_.refs_2_ = f32[2,2,32,512]{3,2,1,0:T(8,128)S(1)} custom-call(s32[321]{0:T(512)S(1)} %copy-done.7, f32[6,2,32,256]{3,2,1,0:T(8,128)S(1)} %collective-permute-done.28.refs_0_, f32[6,2,32,256]{3,2,1,0:T(8,128)S(1)} %collective-permute-done.29.refs_1_, bf16[21,2,2,512,256]{4,3,2,1,0:T(8,128)(2,1)} %get-tuple-element.50.refs_4_.refs_3_.refs_2_.blocks_ref, ...), custom_call_target="tpu_custom_call" | custom-call | flops 4194304 | bytes 262144 | tf_op jit(solution)/shard_map/forward_group3/pallas_call | solution.py:366
  123.9 2.8 %forward_group4.3.refs_3_ = f32[2,2,32,512]{3,2,1,0:T(8,128)S(1)} custom-call(s32[321]{0:T(512)S(1)} %copy-done.7, f32[3,2,32,256]{3,2,1,0:T(8,128)S(1)} %collective-permute-done.31.refs_0_, f32[3,2,32,256]{3,2,1,0:T(8,128)S(1)} %collective-permute-done.32.refs_1_, bf16[21,2,2,512,256]{4,3,2,1,0:T(8,128)(2,1)} %get-tuple-element.50.refs_4_.refs_3_.refs_2_.blocks_ref, ...), custom_call_target="tpu_custom_call" | custom-call | flops 4194304 | bytes 262144 | tf_op jit(solution)/shard_map/forward_group4/pallas_call | solution.py:366
  128.4 1.5 %tmat_apply.5 = (f32[2,2,32,256]{3,2,1,0:T(8,128)}, f32[2,2,32,256]{3,2,1,0:T(8,128)}) custom-call(s32[1]{0:T(128)} %bitcast.side_ref, f32[2,2,32,512]{3,2,1,0:T(8,128)S(1)} %total.3.mine_ref, f32[2,2,32,512]{3,2,1,0:T(8,128)S(1)} %collective-permute-done.34.theirs_ref, bf16[2,256,2048]{2,1,0:T(8,128)(2,1)S(1)} %copy-done.1), custom_call_target="tpu_custom_call" | custom-call | tf_op jit(solution)/shard_map/tmat_apply/pallas_call | solution.py:170
  (85 shorter events, 23.4 us)
Async XLA Ops:
  7.6 8.6 %collective-permute-start.3 = (f32[2,2,32,256]{3,2,1,0:T(8,128)S(1)}, f32[2,2,32,256]{3,2,1,0:T(8,128)S(1)}, u32[]{:S(2)}, u32[]{:S(2)}) collective-permute-start(f32[2,2,32,256]{3,2,1,0:T(8,128)S(1)} %tmat_apply.3.refs_0_.own_ref.refs_3_), channel_id=1, source_target_pairs={{0,1},{1,0},{2,3},{3,2},{4,5},{5,4},{6,7},{7,6},{8,9},{9,8},{10,11... | collective-permute-start | bytes 393224 | tf_op jit(solution)/shard_map/ppermute | solution.py:439
  7.7 14.3 %collective-permute-start.4 = (f32[2,2,32,256]{3,2,1,0:T(8,128)S(1)}, f32[2,2,32,256]{3,2,1,0:T(8,128)S(1)}, u32[]{:S(2)}, u32[]{:S(2)}) collective-permute-start(f32[2,2,32,256]{3,2,1,0:T(8,128)S(1)} %tmat_apply.3.refs_0_.own_ref.refs_3_), channel_id=1, source_target_pairs={{0,8},{2,10},{4,12},{6,14},{8,0},{10,2},{12,4},{14,6},{16,24},{18,... | collective-permute-start | bytes 393224 | tf_op jit(solution)/shard_map/ppermute | solution.py:444
  10.8 11.2 %collective-permute-start.2 = (f32[2,2,32,256]{3,2,1,0:T(8,128)S(1)}, f32[2,2,32,256]{3,2,1,0:T(8,128)S(1)}, u32[]{:S(2)}, u32[]{:S(2)}) collective-permute-start(f32[2,2,32,256]{3,2,1,0:T(8,128)S(1)} %tmat_apply.3.refs_0_.own_ref.refs_3_), channel_id=1, source_target_pairs={{0,4},{2,6},{4,0},{6,2},{8,12},{10,14},{12,8},{14,10},{16,20},{18,... | collective-permute-start | bytes 393224 | tf_op jit(solution)/shard_map/ppermute | solution.py:444
  12.3 9.7 %collective-permute-start.1 = (f32[2,2,32,256]{3,2,1,0:T(8,128)S(1)}, f32[2,2,32,256]{3,2,1,0:T(8,128)S(1)}, u32[]{:S(2)}, u32[]{:S(2)}) collective-permute-start(f32[2,2,32,256]{3,2,1,0:T(8,128)S(1)} %tmat_apply.3.refs_0_.own_ref.refs_3_), channel_id=1, source_target_pairs={{0,2},{2,0},{4,6},{6,4},{8,10},{10,8},{12,14},{14,12},{16,18},{18,... | collective-permute-start | bytes 393224 | tf_op jit(solution)/shard_map/ppermute | solution.py:444
  22.1 12.2 %collective-permute-start.5 = (f32[5,2,32,256]{3,2,1,0:T(8,128)S(1)}, f32[5,2,32,256]{3,2,1,0:T(8,128)S(1)}, u32[]{:S(2)}, u32[]{:S(2)}) collective-permute-start(f32[5,2,32,256]{3,2,1,0:T(8,128)S(1)} %get-tuple-element.43), channel_id=1, source_target_pairs={{0,2},{2,0},{4,6},{6,4},{8,10},{10,8},{12,14},{14,12},{16,18},{18,... | collective-permute-start | bytes 983048 | tf_op jit(solution)/shard_map/ppermute | solution.py:444
  22.2 12.1 %collective-permute-start.6 = (f32[5,2,32,256]{3,2,1,0:T(8,128)S(1)}, f32[5,2,32,256]{3,2,1,0:T(8,128)S(1)}, u32[]{:S(2)}, u32[]{:S(2)}) collective-permute-start(f32[5,2,32,256]{3,2,1,0:T(8,128)S(1)} %get-tuple-element.44), channel_id=1, source_target_pairs={{0,4},{2,6},{4,0},{6,2},{8,12},{10,14},{12,8},{14,10},{16,20},{18,... | collective-permute-start | bytes 983048 | tf_op jit(solution)/shard_map/ppermute | solution.py:444
  22.2 12.0 %collective-permute-start.7 = (f32[2,2,32,256]{3,2,1,0:T(8,128)S(1)}, f32[2,2,32,256]{3,2,1,0:T(8,128)S(1)}, u32[]{:S(2)}, u32[]{:S(2)}) collective-permute-start(f32[2,2,32,256]{3,2,1,0:T(8,128)S(1)} %get-tuple-element.47), channel_id=1, source_target_pairs={{0,16},{2,18},{4,20},{6,22},{8,24},{10,26},{12,28},{14,30},{16,0},... | collective-permute-start | bytes 393224 | tf_op jit(solution)/shard_map/ppermute | solution.py:444
  34.4 13.9 %collective-permute-start.9 = (f32[8,2,32,256]{3,2,1,0:T(8,128)S(1)}, f32[8,2,32,256]{3,2,1,0:T(8,128)S(1)}, u32[]{:S(2)}, u32[]{:S(2)}) collective-permute-start(f32[8,2,32,256]{3,2,1,0:T(8,128)S(1)} %get-tuple-element.53), channel_id=1, source_target_pairs={{0,2},{2,0},{4,6},{6,4},{8,10},{10,8},{12,14},{14,12},{16,18},{18,... | collective-permute-start | bytes 1572872 | tf_op jit(solution)/shard_map/ppermute | solution.py:444
  34.5 13.8 %collective-permute-start.10 = (f32[8,2,32,256]{3,2,1,0:T(8,128)S(1)}, f32[8,2,32,256]{3,2,1,0:T(8,128)S(1)}, u32[]{:S(2)}, u32[]{:S(2)}) collective-permute-start(f32[8,2,32,256]{3,2,1,0:T(8,128)S(1)} %get-tuple-element.54), channel_id=1, source_target_pairs={{0,4},{2,6},{4,0},{6,2},{8,12},{10,14},{12,8},{14,10},{16,20},{18,... | collective-permute-start | bytes 1572872 | tf_op jit(solution)/shard_map/ppermute | solution.py:444
  34.7 13.7 %collective-permute-start.8 = (f32[2,2,32,256]{3,2,1,0:T(8,128)S(1)}, f32[2,2,32,256]{3,2,1,0:T(8,128)S(1)}, u32[]{:S(2)}, u32[]{:S(2)}) collective-permute-start(f32[2,2,32,256]{3,2,1,0:T(8,128)S(1)} %get-tuple-element.52), channel_id=1, source_target_pairs={{0,16},{2,18},{4,20},{6,22},{8,24},{10,26},{12,28},{14,30},{16,0},... | collective-permute-start | bytes 393224 | tf_op jit(solution)/shard_map/ppermute | solution.py:444
  48.5 9.2 %collective-permute-start.11 = (f32[6,2,32,256]{3,2,1,0:T(8,128)S(1)}, f32[6,2,32,256]{3,2,1,0:T(8,128)S(1)}, u32[]{:S(2)}, u32[]{:S(2)}) collective-permute-start(f32[6,2,32,256]{3,2,1,0:T(8,128)S(1)} %get-tuple-element.56), channel_id=1, source_target_pairs={{0,2},{2,0},{4,6},{6,4},{8,10},{10,8},{12,14},{14,12},{16,18},{18,... | collective-permute-start | bytes 1179656 | tf_op jit(solution)/shard_map/ppermute | solution.py:444
  49.2 8.5 %collective-permute-start.12 = (f32[6,2,32,256]{3,2,1,0:T(8,128)S(1)}, f32[6,2,32,256]{3,2,1,0:T(8,128)S(1)}, u32[]{:S(2)}, u32[]{:S(2)}) collective-permute-start(f32[6,2,32,256]{3,2,1,0:T(8,128)S(1)} %get-tuple-element.57), channel_id=1, source_target_pairs={{0,4},{2,6},{4,0},{6,2},{8,12},{10,14},{12,8},{14,10},{16,20},{18,... | collective-permute-start | bytes 1179656 | tf_op jit(solution)/shard_map/ppermute | solution.py:444
  49.5 11.9 %collective-permute-start.13 = (f32[4,2,32,256]{3,2,1,0:T(8,128)S(1)}, f32[4,2,32,256]{3,2,1,0:T(8,128)S(1)}, u32[]{:S(2)}, u32[]{:S(2)}) collective-permute-start(f32[4,2,32,256]{3,2,1,0:T(8,128)S(1)} %get-tuple-element.59), channel_id=1, source_target_pairs={{0,16},{2,18},{4,20},{6,22},{8,24},{10,26},{12,28},{14,30},{16,0},... | collective-permute-start | bytes 786440 | tf_op jit(solution)/shard_map/ppermute | solution.py:444
  57.7 9.3 %collective-permute-start.14 = (f32[3,2,32,256]{3,2,1,0:T(8,128)S(1)}, f32[3,2,32,256]{3,2,1,0:T(8,128)S(1)}, u32[]{:S(2)}, u32[]{:S(2)}) collective-permute-start(f32[3,2,32,256]{3,2,1,0:T(8,128)S(1)} %get-tuple-element.60), channel_id=1, source_target_pairs={{0,2},{2,0},{4,6},{6,4},{8,10},{10,8},{12,14},{14,12},{16,18},{18,... | collective-permute-start | bytes 589832 | tf_op jit(solution)/shard_map/ppermute | solution.py:444
  59.5 7.5 %collective-permute-start.15 = (f32[3,2,32,256]{3,2,1,0:T(8,128)S(1)}, f32[3,2,32,256]{3,2,1,0:T(8,128)S(1)}, u32[]{:S(2)}, u32[]{:S(2)}) collective-permute-start(f32[3,2,32,256]{3,2,1,0:T(8,128)S(1)} %get-tuple-element.61), channel_id=1, source_target_pairs={{0,4},{2,6},{4,0},{6,2},{8,12},{10,14},{12,8},{14,10},{16,20},{18,... | collective-permute-start | bytes 589832 | tf_op jit(solution)/shard_map/ppermute | solution.py:444
  61.4 8.4 %collective-permute-start.16 = (f32[2,2,32,256]{3,2,1,0:T(8,128)S(1)}, f32[2,2,32,256]{3,2,1,0:T(8,128)S(1)}, u32[]{:S(2)}, u32[]{:S(2)}) collective-permute-start(f32[2,2,32,256]{3,2,1,0:T(8,128)S(1)} %pack_sums.2.refs_4_), channel_id=1, source_target_pairs={{0,8},{2,10},{4,12},{6,14},{8,0},{10,2},{12,4},{14,6},{16,24},{18,... | collective-permute-start | bytes 393224 | tf_op jit(solution)/shard_map/ppermute | solution.py:444
  72.4 4.1 %collective-permute-start.20 = (f32[2,2,32,256]{3,2,1,0:T(8,128)S(1)}, f32[2,2,32,256]{3,2,1,0:T(8,128)S(1)}, u32[]{:S(2)}, u32[]{:S(2)}) collective-permute-start(f32[2,2,32,256]{3,2,1,0:T(8,128)S(1)} %tmat_apply.4.own_ref.refs_3_), channel_id=1, source_target_pairs={{0,1},{1,0},{2,3},{3,2},{4,5},{5,4},{6,7},{7,6},{8,9},{9,8},{10,11... | collective-permute-start | bytes 393224 | tf_op jit(solution)/shard_map/ppermute | solution.py:439
  72.6 6.7 %collective-permute-start.21 = (f32[2,2,32,256]{3,2,1,0:T(8,128)S(1)}, f32[2,2,32,256]{3,2,1,0:T(8,128)S(1)}, u32[]{:S(2)}, u32[]{:S(2)}) collective-permute-start(f32[2,2,32,256]{3,2,1,0:T(8,128)S(1)} %tmat_apply.4.own_ref.refs_3_), channel_id=1, source_target_pairs={{0,8},{2,10},{4,12},{6,14},{8,0},{10,2},{12,4},{14,6},{16,24},{18,... | collective-permute-start | bytes 393224 | tf_op jit(solution)/shard_map/ppermute | solution.py:444
  72.6 6.7 %collective-permute-start.19 = (f32[2,2,32,256]{3,2,1,0:T(8,128)S(1)}, f32[2,2,32,256]{3,2,1,0:T(8,128)S(1)}, u32[]{:S(2)}, u32[]{:S(2)}) collective-permute-start(f32[2,2,32,256]{3,2,1,0:T(8,128)S(1)} %tmat_apply.4.own_ref.refs_3_), channel_id=1, source_target_pairs={{0,4},{2,6},{4,0},{6,2},{8,12},{10,14},{12,8},{14,10},{16,20},{18,... | collective-permute-start | bytes 393224 | tf_op jit(solution)/shard_map/ppermute | solution.py:444
  72.9 7.1 %collective-permute-start.18 = (f32[2,2,32,256]{3,2,1,0:T(8,128)S(1)}, f32[2,2,32,256]{3,2,1,0:T(8,128)S(1)}, u32[]{:S(2)}, u32[]{:S(2)}) collective-permute-start(f32[2,2,32,256]{3,2,1,0:T(8,128)S(1)} %tmat_apply.4.own_ref.refs_3_), channel_id=1, source_target_pairs={{0,2},{2,0},{4,6},{6,4},{8,10},{10,8},{12,14},{14,12},{16,18},{18,... | collective-permute-start | bytes 393224 | tf_op jit(solution)/shard_map/ppermute | solution.py:444
  80.0 9.9 %collective-permute-start.22 = (f32[5,2,32,256]{3,2,1,0:T(8,128)S(1)}, f32[5,2,32,256]{3,2,1,0:T(8,128)S(1)}, u32[]{:S(2)}, u32[]{:S(2)}) collective-permute-start(f32[5,2,32,256]{3,2,1,0:T(8,128)S(1)} %get-tuple-element.62), channel_id=1, source_target_pairs={{0,2},{2,0},{4,6},{6,4},{8,10},{10,8},{12,14},{14,12},{16,18},{18,... | collective-permute-start | bytes 983048 | tf_op jit(solution)/shard_map/ppermute | solution.py:444
  81.9 8.3 %collective-permute-start.23 = (f32[5,2,32,256]{3,2,1,0:T(8,128)S(1)}, f32[5,2,32,256]{3,2,1,0:T(8,128)S(1)}, u32[]{:S(2)}, u32[]{:S(2)}) collective-permute-start(f32[5,2,32,256]{3,2,1,0:T(8,128)S(1)} %get-tuple-element.63), channel_id=1, source_target_pairs={{0,4},{2,6},{4,0},{6,2},{8,12},{10,14},{12,8},{14,10},{16,20},{18,... | collective-permute-start | bytes 983048 | tf_op jit(solution)/shard_map/ppermute | solution.py:444
  82.1 7.8 %collective-permute-start.24 = (f32[2,2,32,256]{3,2,1,0:T(8,128)S(1)}, f32[2,2,32,256]{3,2,1,0:T(8,128)S(1)}, u32[]{:S(2)}, u32[]{:S(2)}) collective-permute-start(f32[2,2,32,256]{3,2,1,0:T(8,128)S(1)} %get-tuple-element.64), channel_id=1, source_target_pairs={{0,16},{2,18},{4,20},{6,22},{8,24},{10,26},{12,28},{14,30},{16,0},... | collective-permute-start | bytes 393224 | tf_op jit(solution)/shard_map/ppermute | solution.py:444
  90.2 12.9 %collective-permute-start.26 = (f32[8,2,32,256]{3,2,1,0:T(8,128)S(1)}, f32[8,2,32,256]{3,2,1,0:T(8,128)S(1)}, u32[]{:S(2)}, u32[]{:S(2)}) collective-permute-start(f32[8,2,32,256]{3,2,1,0:T(8,128)S(1)} %get-tuple-element.67), channel_id=1, source_target_pairs={{0,2},{2,0},{4,6},{6,4},{8,10},{10,8},{12,14},{14,12},{16,18},{18,... | collective-permute-start | bytes 1572872 | tf_op jit(solution)/shard_map/ppermute | solution.py:444
  91.2 11.9 %collective-permute-start.27 = (f32[8,2,32,256]{3,2,1,0:T(8,128)S(1)}, f32[8,2,32,256]{3,2,1,0:T(8,128)S(1)}, u32[]{:S(2)}, u32[]{:S(2)}) collective-permute-start(f32[8,2,32,256]{3,2,1,0:T(8,128)S(1)} %get-tuple-element.68), channel_id=1, source_target_pairs={{0,4},{2,6},{4,0},{6,2},{8,12},{10,14},{12,8},{14,10},{16,20},{18,... | collective-permute-start | bytes 1572872 | tf_op jit(solution)/shard_map/ppermute | solution.py:444
  92.1 8.4 %collective-permute-start.25 = (f32[2,2,32,256]{3,2,1,0:T(8,128)S(1)}, f32[2,2,32,256]{3,2,1,0:T(8,128)S(1)}, u32[]{:S(2)}, u32[]{:S(2)}) collective-permute-start(f32[2,2,32,256]{3,2,1,0:T(8,128)S(1)} %get-tuple-element.66), channel_id=1, source_target_pairs={{0,16},{2,18},{4,20},{6,22},{8,24},{10,26},{12,28},{14,30},{16,0},... | collective-permute-start | bytes 393224 | tf_op jit(solution)/shard_map/ppermute | solution.py:444
  103.3 9.1 %collective-permute-start.28 = (f32[6,2,32,256]{3,2,1,0:T(8,128)S(1)}, f32[6,2,32,256]{3,2,1,0:T(8,128)S(1)}, u32[]{:S(2)}, u32[]{:S(2)}) collective-permute-start(f32[6,2,32,256]{3,2,1,0:T(8,128)S(1)} %get-tuple-element.70), channel_id=1, source_target_pairs={{0,2},{2,0},{4,6},{6,4},{8,10},{10,8},{12,14},{14,12},{16,18},{18,... | collective-permute-start | bytes 1179656 | tf_op jit(solution)/shard_map/ppermute | solution.py:444
  105.0 8.7 %collective-permute-start.29 = (f32[6,2,32,256]{3,2,1,0:T(8,128)S(1)}, f32[6,2,32,256]{3,2,1,0:T(8,128)S(1)}, u32[]{:S(2)}, u32[]{:S(2)}) collective-permute-start(f32[6,2,32,256]{3,2,1,0:T(8,128)S(1)} %get-tuple-element.71), channel_id=1, source_target_pairs={{0,4},{2,6},{4,0},{6,2},{8,12},{10,14},{12,8},{14,10},{16,20},{18,... | collective-permute-start | bytes 1179656 | tf_op jit(solution)/shard_map/ppermute | solution.py:444
  106.3 12.0 %collective-permute-start.30 = (f32[4,2,32,256]{3,2,1,0:T(8,128)S(1)}, f32[4,2,32,256]{3,2,1,0:T(8,128)S(1)}, u32[]{:S(2)}, u32[]{:S(2)}) collective-permute-start(f32[4,2,32,256]{3,2,1,0:T(8,128)S(1)} %get-tuple-element.73), channel_id=1, source_target_pairs={{0,16},{2,18},{4,20},{6,22},{8,24},{10,26},{12,28},{14,30},{16,0},... | collective-permute-start | bytes 786440 | tf_op jit(solution)/shard_map/ppermute | solution.py:444
  113.7 10.1 %collective-permute-start.31 = (f32[3,2,32,256]{3,2,1,0:T(8,128)S(1)}, f32[3,2,32,256]{3,2,1,0:T(8,128)S(1)}, u32[]{:S(2)}, u32[]{:S(2)}) collective-permute-start(f32[3,2,32,256]{3,2,1,0:T(8,128)S(1)} %get-tuple-element.74), channel_id=1, source_target_pairs={{0,2},{2,0},{4,6},{6,4},{8,10},{10,8},{12,14},{14,12},{16,18},{18,... | collective-permute-start | bytes 589832 | tf_op jit(solution)/shard_map/ppermute | solution.py:444
  114.2 9.7 %collective-permute-start.32 = (f32[3,2,32,256]{3,2,1,0:T(8,128)S(1)}, f32[3,2,32,256]{3,2,1,0:T(8,128)S(1)}, u32[]{:S(2)}, u32[]{:S(2)}) collective-permute-start(f32[3,2,32,256]{3,2,1,0:T(8,128)S(1)} %get-tuple-element.75), channel_id=1, source_target_pairs={{0,4},{2,6},{4,0},{6,2},{8,12},{10,14},{12,8},{14,10},{16,20},{18,... | collective-permute-start | bytes 589832 | tf_op jit(solution)/shard_map/ppermute | solution.py:444
  118.3 8.3 %collective-permute-start.33 = (f32[2,2,32,256]{3,2,1,0:T(8,128)S(1)}, f32[2,2,32,256]{3,2,1,0:T(8,128)S(1)}, u32[]{:S(2)}, u32[]{:S(2)}) collective-permute-start(f32[2,2,32,256]{3,2,1,0:T(8,128)S(1)} %pack_sums.3.refs_4_), channel_id=1, source_target_pairs={{0,8},{2,10},{4,12},{6,14},{8,0},{10,2},{12,4},{14,6},{16,24},{18,... | collective-permute-start | bytes 393224 | tf_op jit(solution)/shard_map/ppermute | solution.py:444
  (11 other events, 49.5 us)
